TPU v7x, 512 devices: a whole 4x8x8 slice. The times are simulated.
512 devices in a mesh: dom: 128 (over y, z, core), type: 4 (over x).
Axes of the slice: x: 4, y: 8, z: 8, core: 2. Of those that a mesh axis runs over, the one named last changes fastest.
Arguments:
- vertex_table: bfloat16 [262144, 128], P(('dom', 'type')), may hold values from -3 to 3
- context_table: bfloat16 [262144, 128], P(('dom', 'type')), may hold values from -3 to 3
- vertex_state: float32 [262144], P(('dom', 'type')), may hold values from 0.05 to 2
- context_state: float32 [262144], P(('dom', 'type')), may hold values from 0.05 to 2
- pair_blocks: int32 [2, 4096, 2], P(None, ('dom', 'type')), may hold values from 0 to 3
- pair_offsets: int32 [2, 4096, 16, 2], P(None, ('dom', 'type')), may hold values from 0 to 127
- negative_owner: int32 [2, 4096, 16, 5], P(None, ('dom', 'type')), may hold values from 0 to 511, all different within a row; in each aligned block of 128 rows (0 to 127, 128 to 255, ..., all dimensions but the last counted through in order) at most 3 rows name the same one
- negative_row: int32 [2, 4096, 16, 5], P(None, ('dom', 'type')), may hold values from 0 to 511
Outputs:
- new_vertex: bfloat16 [262144, 128], P(('dom', 'type'))
- new_context: bfloat16 [262144, 128], P(('dom', 'type'))
- new_vertex_state: float32 [262144], P(('dom', 'type'))
- new_context_state: float32 [262144], P(('dom', 'type'))
Inputs may be any that keep to these rules, and one draw needn't show every extreme that they name: `negative_owner`: in each episode, among the 5 negatives of all 128 pairs of one device, no owner is named more than 3 times, a bound that some block reaches; the 5 owners of one pair differ.
All inputs are finite; a program needn't handle non-finite values.
Results may differ from a plain program's by a relative error of at most 0.009.
Values may be sent and summed in bfloat16 or wider, within the bound.
No kernel may reach another device: no remote copies, remote signals or barrier semaphores. Data moves between devices by JAX's collectives and lax.ppermute only.
A program may use at most 64 MiB of HBM per device.

v0:
```python
import jax
import jax.numpy as jnp
from jax import lax
from jax.experimental import pallas as pl
from jax.experimental.pallas import tpu as pltpu
from jax.sharding import PartitionSpec as P

AXES = ("dom", "type")
TILE = 128
CAP = 3
LANES = 128
F32 = jnp.float32
BF16 = jnp.bfloat16


def iota(shape, dim):
    return lax.broadcasted_iota(jnp.int32, shape, dim).astype(F32)


def dot(a, b):
    return jnp.dot(a, b, preferred_element_type=F32)


def eye():
    return iota((LANES, LANES), 0) == iota((LANES, LANES), 1)


def to_row(col):
    return jnp.sum(jnp.where(eye(), col, 0.0), axis=0, keepdims=True)


def to_col(row):
    return jnp.sum(jnp.where(eye(), row, 0.0), axis=1, keepdims=True)


def one_hot_of_col(col, rows):
    return jnp.where(col == iota((col.shape[0], rows), 1), 1.0, 0.0).astype(BF16)


def one_hot_of_row(row, rows, first):
    return jnp.where(row == iota((rows, row.shape[1]), 0) + first, 1.0, 0.0).astype(BF16)


def lane_of(episode, slot, part):
    return 16 * episode + 4 * slot + part


def slot_col(table, lane):
    return table[:, lane : lane + 1] * 256.0 + table[:, lane + 1 : lane + 2] - 1.0


def slot_row(turned, lane):
    return turned[lane : lane + 1, :] * 256.0 + turned[lane + 1 : lane + 2, :] - 1.0


def row_dot(a, b):
    return jnp.sum(a * b, axis=1, keepdims=True)


def blocks(n, step):
    lax.fori_loop(0, n // TILE, lambda b, c: (step(pl.multiple_of(b * TILE, TILE), b), c)[1], 0)


def turn(slots_ref, turned_ref):
    def step(at, b):
        turned_ref[b] = jnp.transpose(slots_ref[CAP, pl.ds(at, TILE), :].astype(F32))

    blocks(slots_ref.shape[1], step)


def gather_slots(table_ref, slots_ref, out_ref, first_out, episode, part):
    def step(at, b):
        slots = slots_ref[CAP, pl.ds(at, TILE), :].astype(F32)
        for s in range(CAP):
            col = slot_col(slots, lane_of(episode, s, part))
            rows = dot(one_hot_of_col(col, table_ref.shape[0]), table_ref[...])
            out_ref[first_out + s, pl.ds(at, TILE), :] = rows.astype(BF16)

    blocks(slots_ref.shape[1], step)


def weigh_slots(here_ref, first_here, there_ref, first_there, out_ref):
    def step(at, b):
        for s in range(CAP):
            here = here_ref[first_here + s, pl.ds(at, TILE), :].astype(F32)
            there = there_ref[first_there + s, pl.ds(at, TILE), :].astype(F32)
            out_ref[s, pl.ds(at, TILE), :] = (jax.nn.sigmoid(row_dot(here, there)) * there).astype(BF16)

    blocks(out_ref.shape[1], step)


def adagrad(
    table_ref, state_ref, new_ref, new_state_ref, turned_ref, terms_ref, lane0, pair_row, pair_terms
):
    owners = terms_ref.shape[1]
    width = table_ref.shape[1]

    def step(at, b):
        first = at.astype(F32)
        grad = dot(one_hot_of_row(pair_row, TILE, first), pair_terms)
        for s in range(CAP):
            for o in range(owners // TILE):
                row = slot_row(turned_ref[o], lane0 + 4 * s)
                grad += dot(one_hot_of_row(row, TILE, first), terms_ref[s, o * TILE : (o + 1) * TILE, :])
        state = jnp.transpose(jnp.broadcast_to(state_ref[pl.ds(b, 1), :], (TILE, TILE)))
        state = state + row_dot(grad, grad) * (1.0 / width)
        rows = table_ref[pl.ds(at, TILE), :].astype(F32) - 0.5 * grad / jnp.sqrt(state)
        new_ref[pl.ds(at, TILE), :] = rows.astype(BF16)
        new_state_ref[pl.ds(b, 1), :] = jnp.transpose(state)[0:1, :]

    blocks(table_ref.shape[0], step)


def pairs_out(pairs_ref, episode, table_ref, out_ref):
    pairs = pairs_ref[episode].astype(F32)
    n = pairs.shape[0]
    rows = dot(one_hot_of_col(pairs[:, 0:1], table_ref.shape[0]), table_ref[...])
    out_ref[0:n, :] = rows.astype(BF16)
    high = jnp.floor(pairs[:, 1:2] * (1.0 / 256.0))
    low = pairs[:, 1:2] - high * 256.0
    which = iota((16, LANES), 0)
    tail = jnp.where(which == 0, to_row(high), jnp.where(which == 1, to_row(low), 0.0))
    out_ref[n : n + 16, :] = tail.astype(BF16)


def pair_terms_of(here, there):
    return ((jax.nn.sigmoid(row_dot(here, there)) - 1.0) * there).astype(BF16)


def first_kernel(owner_ref, row_ref, pairs_ref, table_ref, send_ref, pair_ref):
    episodes, pairs, negatives = owner_ref.shape
    owners = send_ref.shape[1]
    lane = lax.broadcasted_iota(jnp.int32, (pairs, LANES), 1)
    slot_of_lane = ((lane // 4) % 4).astype(F32)
    earlier = iota((pairs, pairs), 1) < iota((pairs, pairs), 0)
    owner_rows, values = [], []
    for e in range(episodes):
        vertex = pairs_ref[e].astype(F32)[:, 0:1] + 1.0
        vertex_high = jnp.floor(vertex * (1.0 / 256.0))
        cols = [owner_ref[e].astype(F32)[:, k : k + 1] for k in range(negatives)]
        rows = [to_row(c) for c in cols]
        for k in range(negatives):
            same = jnp.where((cols[k] == rows[k]) & earlier, 1.0, 0.0)
            for j in range(k):
                same += jnp.where(cols[k] == rows[j], 1.0, 0.0)
            rank = jnp.sum(same, axis=1, keepdims=True)
            target = row_ref[e].astype(F32)[:, k : k + 1] + 1.0
            target_high = jnp.floor(target * (1.0 / 256.0))
            part = lane % 4
            value = jnp.where(part == 0, target_high, target - 256.0 * target_high)
            value = jnp.where(part == 2, vertex_high, value)
            value = jnp.where(part == 3, vertex - 256.0 * vertex_high, value)
            mine = (slot_of_lane == rank) & (lane // 16 == e)
            values.append(jnp.where(mine, value, 0.0).astype(BF16))
            owner_rows.append(rows[k])

    for b in range(owners // TILE):
        total = jnp.zeros((TILE, LANES), F32)
        for row, value in zip(owner_rows, values):
            total += dot(one_hot_of_row(row, TILE, float(b * TILE)), value)
        send_ref[CAP, b * TILE : (b + 1) * TILE, :] = total.astype(BF16)
    gather_slots(table_ref, send_ref, send_ref, 0, 0, 2)
    pairs_out(pairs_ref, 0, table_ref, pair_ref)


def context_side(pair_ref, table_ref):
    n = pair_ref.shape[0] - 16
    tail = pair_ref[n : n + 16, :].astype(F32)
    row = tail[0:1, :] * 256.0 + tail[1:2, :]
    mine = dot(one_hot_of_col(to_col(row), table_ref.shape[0]), table_ref[...])
    return row, pair_terms_of(mine, pair_ref[0:n, :].astype(F32))


def vertex_side(pairs_ref, episode, table_ref, partner_ref):
    pairs = pairs_ref[episode].astype(F32)
    mine = dot(one_hot_of_col(pairs[:, 0:1], table_ref.shape[0]), table_ref[...])
    theirs = dot(one_hot_of_col(pairs[:, 1:2], partner_ref.shape[0]), partner_ref[...])
    return to_row(pairs[:, 0:1]), pair_terms_of(mine, theirs)


def context_first(got_ref, pair_ref, table_ref, state_ref, send_ref, new_ref, new_state_ref, turned_ref, terms_ref):
    turn(got_ref, turned_ref)
    gather_slots(table_ref, got_ref, send_ref, 0, 0, 0)
    weigh_slots(send_ref, 0, got_ref, 0, terms_ref)
    row, pair_terms = context_side(pair_ref, table_ref)
    adagrad(
        table_ref, state_ref, new_ref, new_state_ref, turned_ref, terms_ref, lane_of(0, 0, 0), row, pair_terms
    )
    gather_slots(new_ref, got_ref, send_ref, CAP, 1, 0)


def vertex_first(
    got_ref, sent_ref, pairs_ref, partner_ref, table_ref, state_ref,
    send_ref, pair_ref, new_ref, new_state_ref, turned_ref, terms_ref,
):
    turn(sent_ref, turned_ref)
    weigh_slots(sent_ref, 0, got_ref, 0, terms_ref)
    row, pair_terms = vertex_side(pairs_ref, 0, table_ref, partner_ref)
    adagrad(
        table_ref, state_ref, new_ref, new_state_ref, turned_ref, terms_ref, lane_of(0, 0, 2), row, pair_terms
    )
    gather_slots(new_ref, sent_ref, send_ref, 0, 1, 2)
    pairs_out(pairs_ref, 1, new_ref, pair_ref)


def vertex_last(
    got_ref, sent_ref, slots_ref, pairs_ref, partner_ref, table_ref, state_ref,
    new_ref, new_state_ref, turned_ref, terms_ref,
):
    turn(slots_ref, turned_ref)
    weigh_slots(sent_ref, 0, got_ref, CAP, terms_ref)
    row, pair_terms = vertex_side(pairs_ref, 1, table_ref, partner_ref)
    adagrad(
        table_ref, state_ref, new_ref, new_state_ref, turned_ref, terms_ref, lane_of(1, 0, 2), row, pair_terms
    )


def context_last(
    got_ref, sent_ref, slots_ref, pair_ref, table_ref, state_ref, new_ref, new_state_ref, turned_ref, terms_ref
):
    turn(slots_ref, turned_ref)
    weigh_slots(sent_ref, CAP, got_ref, 0, terms_ref)
    row, pair_terms = context_side(pair_ref, table_ref)
    adagrad(
        table_ref, state_ref, new_ref, new_state_ref, turned_ref, terms_ref, lane_of(1, 0, 0), row, pair_terms
    )


def call(kernel, name, outs, scratch, *args):
    return pl.pallas_call(
        kernel,
        name=name,
        out_shape=[jax.ShapeDtypeStruct(s, d) for s, d in outs],
        scratch_shapes=scratch,
        compiler_params=pltpu.CompilerParams(vmem_limit_bytes=16 * 1024 * 1024),
        cost_estimate=pl.CostEstimate(flops=600_000_000, bytes_accessed=4_000_000, transcendentals=2000),
    )(*args)


def exchange(rows):
    return lax.all_to_all(rows, AXES, split_axis=1, concat_axis=1, tiled=True)


def exchange_packed(rows):
    s, n, w = rows.shape
    packed = rows.reshape(2, s // 2, n, w).transpose(2, 0, 1, 3).reshape(n, 2, s // 2 * w)
    packed = lax.all_to_all(packed, AXES, split_axis=0, concat_axis=0, tiled=True)
    return packed.reshape(n, 2, s // 2, w).transpose(1, 2, 0, 3).reshape(s, n, w)


def passed_along(block, distance, n_devices):
    return lax.ppermute(block, AXES, [((i - distance) % n_devices, i) for i in range(n_devices)])


def body(
    vertex_table, context_table, vertex_state, context_state, pair_blocks, pair_offsets, negative_owner, negative_row
):
    n_type = lax.axis_size("type")
    n = lax.axis_size("dom") * n_type
    rows, width = vertex_table.shape
    episodes, block_pairs, per_block, negatives = negative_owner.shape
    n_pairs = block_pairs * per_block
    shifts = [1 + n_type * (e + 1) for e in range(episodes)]
    pairs = (pair_blocks[:, :, None, :] * TILE + pair_offsets).reshape(episodes, n_pairs, 2)
    owner = negative_owner.reshape(episodes, n_pairs, negatives)
    target = negative_row.reshape(episodes, n_pairs, negatives)
    v_state = vertex_state.reshape(rows // TILE, TILE)
    c_state = context_state.reshape(rows // TILE, TILE)

    table = ((rows, width), BF16)
    state = ((rows // TILE, TILE), F32)
    pair_rows = ((n_pairs + 16, width), BF16)
    scratch = [pltpu.VMEM((n // TILE, LANES, TILE), F32), pltpu.VMEM((CAP, n, width), BF16)]

    sent_a, pair_a = call(
        first_kernel, "slots", [((CAP + 1, n, width), BF16), pair_rows], [], owner, target, pairs, vertex_table
    )
    partner_0 = passed_along(context_table, shifts[0], n)
    got_pair_a = passed_along(pair_a, n - shifts[0], n)
    got_a = exchange(sent_a)
    sent_b, context_1, c_state_1 = call(
        context_first, "context_first", [((2 * CAP, n, width), BF16), table, state], scratch,
        got_a, got_pair_a, context_table, c_state,
    )
    partner_1 = passed_along(context_1, shifts[1], n)
    got_b = exchange_packed(sent_b)
    sent_c, pair_c, vertex_1, v_state_1 = call(
        vertex_first, "vertex_first", [((CAP, n, width), BF16), pair_rows, table, state], scratch,
        got_b, sent_a, pairs, partner_0, vertex_table, v_state,
    )
    got_pair_c = passed_along(pair_c, n - shifts[1], n)
    got_c = exchange(sent_c)
    vertex_2, v_state_2 = call(
        vertex_last, "vertex_last", [table, state], scratch,
        got_b, sent_c, sent_a, pairs, partner_1, vertex_1, v_state_1,
    )
    context_2, c_state_2 = call(
        context_last, "context_last", [table, state], scratch,
        got_c, sent_b, got_a, got_pair_c, context_1, c_state_1,
    )
    return vertex_2, context_2, v_state_2.reshape(rows), c_state_2.reshape(rows)


def solution(mesh):
    in_specs = (
        P(AXES, None),
        P(AXES, None),
        P(AXES),
        P(AXES),
        P(None, AXES, None),
        P(None, AXES, None, None),
        P(None, AXES, None, None),
        P(None, AXES, None, None),
    )
    out_specs = (P(AXES, None), P(AXES, None), P(AXES), P(AXES))
    return jax.shard_map(body, mesh=mesh, in_specs=in_specs, out_specs=out_specs, check_vma=False)
```

profile of v0, /device:TPU:1, one launch (start us, length us, event | category | flops | bytes accessed | tf_op | source)
XLA Modules:
  0.0 151.5 jit_solution(8888212812259784343)
XLA Ops:
  0.6 1.0 copy.22
  1.6 0.2 copy.23
  1.8 0.5 copy-done.10
  2.3 0.1 copy.24
  2.5 0.2 copy.25
  2.6 0.6 copy-done.1
  3.2 3.5 %slots.1 = (bf16[4,512,128]{2,1,0:T(8,128)(2,1)S(1)}, bf16[144,128]{1,0:T(8,128)(2,1)S(1)}) custom-call(s32[2,128,5]{2,1,0:T(8,128)S(1)} %bitcast.21, s32[2,128,5]{2,1,0:T(8,128)S(1)} %bitcast.22, s32[2,128,2]{2,1,0:T(8,128)S(1)} %bitcast.18, bf16[512,128]{1,0:T(8,128)(2,1)S(1)} %copy-done.1), custom_call_target="tpu_custom_call" | custom-call | flops 600000000 | bytes 4000000 | tf_op jit(solution)/shard_map/slots/pallas_call | solution.py:230
  6.7 1.2 copy.26
  7.9 22.2 %all-to-all-start = ((bf16[4,512,128]{2,0,1:T(4,128)(2,1)}), bf16[4,512,128]{2,0,1:T(4,128)(2,1)S(1)}, u32[]{:S(2)}, u32[]{:S(2)}) async-start(bf16[4,512,128]{2,0,1:T(4,128)(2,1)} %copy.26), calls=%async_computation | async-start | bytes 1048576 | tf_op jit(solution)/shard_map/all_to_all | solution.py:241
  30.1 13.0 %collective-permute-start = (bf16[144,128]{1,0:T(8,128)(2,1)S(1)}, bf16[144,128]{1,0:T(8,128)(2,1)S(1)}, u32[]{:S(2)}, u32[]{:S(2)}) collective-permute-start(bf16[144,128]{1,0:T(8,128)(2,1)S(1)} %get-tuple-element.18), channel_id=1, source_target_pairs={{5,0},{6,1},{7,2},{8,3},{9,4},{10,5},{11,6},{12,7},{13,8},{14,9},{... | collective-permute-start | bytes 110600 | tf_op jit(solution)/shard_map/ppermute | solution.py:252
  43.1 8.9 %all-to-all-done = bf16[4,512,128]{2,0,1:T(4,128)(2,1)S(1)} async-done(((bf16[4,512,128]{2,0,1:T(4,128)(2,1)}), bf16[4,512,128]{2,0,1:T(4,128)(2,1)S(1)}, u32[]{:S(2)}, u32[]{:S(2)}) %all-to-all-start) | async-done | bytes 524320 | tf_op jit(solution)/shard_map/all_to_all | solution.py:241
  52.1 6.1 %context_first.1 = (bf16[6,512,128]{2,1,0:T(8,128)(2,1)S(1)}, bf16[512,128]{1,0:T(8,128)(2,1)S(1)}, f32[4,128]{1,0:T(4,128)S(1)}) custom-call(bf16[4,512,128]{2,1,0:T(8,128)(2,1)S(1)} %copy.27.got_ref.slots_ref, bf16[144,128]{1,0:T(8,128)(2,1)S(1)} %collective-permute-done.pair_ref, bf16[512,128]{1,0:T(8,128)(2,1)S(1)} %copy-done, f32[4,128]{1,0:T(4,128)S(1)} %bitcast.23), custom_call_target="tpu_custom_call" | custom-call | flops 600000000 | bytes 4000000 | tf_op jit(solution)/shard_map/context_first/pallas_call | solution.py:230
  58.2 0.3 copy.28
  58.5 1.9 %copy.29 = bf16[512,2,384]{2,1,0:T(2,128)(2,1)} copy(bf16[512,2,384]{0,2,1:T(8,128)(2,1)S(1)} %bitcast.26) | data formatting | bytes 1572864 | tf_op jit(solution)/shard_map/reshape | solution.py:246
  60.4 9.1 %all-to-all-start.1 = ((bf16[512,2,384]{2,1,0:T(2,128)(2,1)}), bf16[512,2,384]{2,1,0:T(2,128)(2,1)S(1)}, u32[]{:S(2)}, u32[]{:S(2)}) async-start(bf16[512,2,384]{2,1,0:T(2,128)(2,1)} %copy.29), calls=%async_computation.1 | async-start | bytes 1572864 | tf_op jit(solution)/shard_map/all_to_all | solution.py:247
  69.5 5.0 %collective-permute-start.1 = (bf16[512,128]{1,0:T(8,128)(2,1)S(1)}, bf16[512,128]{1,0:T(8,128)(2,1)S(1)}, u32[]{:S(2)}, u32[]{:S(2)}) collective-permute-start(bf16[512,128]{1,0:T(8,128)(2,1)S(1)} %copy-done), channel_id=1, source_target_pairs={{507,0},{508,1},{509,2},{510,3},{511,4},{0,5},{1,6},{2,7},{3,8},{4... | collective-permute-start | bytes 393224 | tf_op jit(solution)/shard_map/ppermute | solution.py:252
  74.5 22.6 %all-to-all-done.1 = bf16[512,2,384]{2,1,0:T(2,128)(2,1)S(1)} async-done(((bf16[512,2,384]{2,1,0:T(2,128)(2,1)}), bf16[512,2,384]{2,1,0:T(2,128)(2,1)S(1)}, u32[]{:S(2)}, u32[]{:S(2)}) %all-to-all-start.1) | async-done | bytes 786464 | tf_op jit(solution)/shard_map/all_to_all | solution.py:247
  97.1 2.1 %copy.30 = bf16[512,2,384]{0,2,1:T(8,128)(2,1)} copy(bf16[512,2,384]{2,1,0:T(2,128)(2,1)S(1)} %all-to-all-done.1) | data formatting | bytes 1572864 | tf_op jit(solution)/shard_map/all_to_all | solution.py:247
  99.2 1.5 copy.31
  100.7 0.7 copy-done.5
  101.4 4.8 %vertex_first.1 = (bf16[3,512,128]{2,1,0:T(8,128)(2,1)S(1)}, bf16[144,128]{1,0:T(8,128)(2,1)S(1)}, bf16[512,128]{1,0:T(8,128)(2,1)S(1)}, f32[4,128]{1,0:T(4,128)S(1)}) custom-call(bf16[6,512,128]{2,1,0:T(8,128)(2,1)S(1)} %bitcast.16, bf16[4,512,128]{2,1,0:T(8,128)(2,1)S(1)} %get-tuple-element.17.sent_ref.slots_ref, s32[2,128,2]{2,1,0:T(8,128)S(1)} %bitcast.19, ...), custom_call_target="tpu_custom_call" | custom-call | flops 600000000 | bytes 4000000 | tf_op jit(solution)/shard_map/vertex_first/pallas_call | solution.py:230
  106.2 0.6 copy-done.2
  106.8 0.7 copy-done.6
  107.4 1.1 copy.32
  108.6 11.6 %all-to-all-start.2 = ((bf16[3,512,128]{2,0,1:T(4,128)(2,1)}), bf16[3,512,128]{2,0,1:T(4,128)(2,1)}, u32[]{:S(2)}, u32[]{:S(2)}) async-start(bf16[3,512,128]{2,0,1:T(4,128)(2,1)} %copy.32), calls=%async_computation.2 | async-start | bytes 1048576 | tf_op jit(solution)/shard_map/all_to_all | solution.py:241
  120.2 4.7 %collective-permute-start.2 = (bf16[512,128]{1,0:T(8,128)(2,1)S(1)}, bf16[512,128]{1,0:T(8,128)(2,1)S(1)}, u32[]{:S(2)}, u32[]{:S(2)}) collective-permute-start(bf16[512,128]{1,0:T(8,128)(2,1)S(1)} %get-tuple-element.21.table_ref), channel_id=1, source_target_pairs={{503,0},{504,1},{505,2},{506,3},{507,4},{508,5},{509,6},{510,7},{5... | collective-permute-start | bytes 393224 | tf_op jit(solution)/shard_map/ppermute | solution.py:252
  125.0 10.4 %collective-permute-start.3 = (bf16[144,128]{1,0:T(8,128)(2,1)S(1)}, bf16[144,128]{1,0:T(8,128)(2,1)S(1)}, u32[]{:S(2)}, u32[]{:S(2)}) collective-permute-start(bf16[144,128]{1,0:T(8,128)(2,1)S(1)} %copy-done.3), channel_id=1, source_target_pairs={{9,0},{10,1},{11,2},{12,3},{13,4},{14,5},{15,6},{16,7},{17,8},{18,... | collective-permute-start | bytes 110600 | tf_op jit(solution)/shard_map/ppermute | solution.py:252
  135.4 6.7 %collective-permute-done.2.partner_ref = bf16[512,128]{1,0:T(8,128)(2,1)S(1)} collective-permute-done((bf16[512,128]{1,0:T(8,128)(2,1)S(1)}, bf16[512,128]{1,0:T(8,128)(2,1)S(1)}, u32[]{:S(2)}, u32[]{:S(2)}) %collective-permute-start.2) | collective-permute-done | bytes 131104 | tf_op jit(solution)/shard_map/ppermute | solution.py:252
  142.2 0.9 copy-done.7
  143.1 3.7 %vertex_last.1 = (bf16[512,128]{1,0:T(8,128)(2,1)}, f32[4,128]{1,0:T(4,128)}) custom-call(bf16[6,512,128]{2,1,0:T(8,128)(2,1)S(1)} %bitcast.17, bf16[3,512,128]{2,1,0:T(8,128)(2,1)S(1)} %get-tuple-element.20.sent_ref, bf16[4,512,128]{2,1,0:T(8,128)(2,1)S(1)} %get-tuple-element.17.sent_ref.slots_ref, s32[2,128,2]{2,1,0:T(8,128)S(1)} %bitcast.20, ...), custom_call_target="tpu_custom_call" | custom-call | flops 600000000 | bytes 4000000 | tf_op jit(solution)/shard_map/vertex_last/pallas_call | solution.py:230
  146.7 1.1 copy.33.got_ref
  147.9 3.7 %context_last.1 = (bf16[512,128]{1,0:T(8,128)(2,1)}, f32[4,128]{1,0:T(4,128)}) custom-call(bf16[3,512,128]{2,1,0:T(8,128)(2,1)S(1)} %copy.33.got_ref, bf16[6,512,128]{2,1,0:T(8,128)(2,1)S(1)} %get-tuple-element.19.sent_ref, bf16[4,512,128]{2,1,0:T(8,128)(2,1)S(1)} %copy.27.got_ref.slots_ref, bf16[144,128]{1,0:T(8,128)(2,1)S(1)} %collective-permute-done.3.pair_ref, ...), custom_call_target="tpu_custom_call" | custom-call | flops 600000000 | bytes 4000000 | tf_op jit(solution)/shard_map/context_last/pallas_call | solution.py:230
  (23 shorter events, 0.2 us)
Async XLA Ops:
  0.6 1.0 copy-start.8
  1.6 0.7 copy-start.10
  1.6 0.8 copy-start.9
  2.3 0.9 copy-start.1
  7.9 44.1 %all-to-all-start = ((bf16[4,512,128]{2,0,1:T(4,128)(2,1)}), bf16[4,512,128]{2,0,1:T(4,128)(2,1)S(1)}, u32[]{:S(2)}, u32[]{:S(2)}) async-start(bf16[4,512,128]{2,0,1:T(4,128)(2,1)} %copy.26), calls=%async_computation | async-start | bytes 1048576 | tf_op jit(solution)/shard_map/all_to_all | solution.py:241
  30.1 22.0 %copy-start = (bf16[512,128]{1,0:T(8,128)(2,1)S(1)}, bf16[512,128]{1,0:T(8,128)(2,1)}, u32[]{:S(2)}) copy-start(bf16[512,128]{1,0:T(8,128)(2,1)} %table_ref.4) | copy-start | bytes 393220
  30.1 22.0 %copy-start.4 = (f32[512]{0:T(512)S(1)}, f32[512]{0:T(512)}, u32[]{:S(2)}) copy-start(f32[512]{0:T(512)} %param.11) | copy-start | bytes 6148
  30.1 22.0 %collective-permute-start = (bf16[144,128]{1,0:T(8,128)(2,1)S(1)}, bf16[144,128]{1,0:T(8,128)(2,1)S(1)}, u32[]{:S(2)}, u32[]{:S(2)}) collective-permute-start(bf16[144,128]{1,0:T(8,128)(2,1)S(1)} %get-tuple-element.18), channel_id=1, source_target_pairs={{5,0},{6,1},{7,2},{8,3},{9,4},{10,5},{11,6},{12,7},{13,8},{14,9},{... | collective-permute-start | bytes 110600 | tf_op jit(solution)/shard_map/ppermute | solution.py:252
  60.4 36.7 %all-to-all-start.1 = ((bf16[512,2,384]{2,1,0:T(2,128)(2,1)}), bf16[512,2,384]{2,1,0:T(2,128)(2,1)S(1)}, u32[]{:S(2)}, u32[]{:S(2)}) async-start(bf16[512,2,384]{2,1,0:T(2,128)(2,1)} %copy.29), calls=%async_computation.1 | async-start | bytes 1572864 | tf_op jit(solution)/shard_map/all_to_all | solution.py:247
  69.5 31.2 %collective-permute-start.1 = (bf16[512,128]{1,0:T(8,128)(2,1)S(1)}, bf16[512,128]{1,0:T(8,128)(2,1)S(1)}, u32[]{:S(2)}, u32[]{:S(2)}) collective-permute-start(bf16[512,128]{1,0:T(8,128)(2,1)S(1)} %copy-done), channel_id=1, source_target_pairs={{507,0},{508,1},{509,2},{510,3},{511,4},{0,5},{1,6},{2,7},{3,8},{4... | collective-permute-start | bytes 393224 | tf_op jit(solution)/shard_map/ppermute | solution.py:252
  100.7 0.7 copy-start.5
  106.2 0.6 copy-start.2
  106.8 0.7 copy-start.6
  108.6 16.4 %copy-start.3 = (bf16[144,128]{1,0:T(8,128)(2,1)S(1)}, bf16[144,128]{1,0:T(8,128)(2,1)}, u32[]{:S(2)}) copy-start(bf16[144,128]{1,0:T(8,128)(2,1)} %copy-done.2) | copy-start | bytes 110596
  108.6 38.2 %all-to-all-start.2 = ((bf16[3,512,128]{2,0,1:T(4,128)(2,1)}), bf16[3,512,128]{2,0,1:T(4,128)(2,1)}, u32[]{:S(2)}, u32[]{:S(2)}) async-start(bf16[3,512,128]{2,0,1:T(4,128)(2,1)} %copy.32), calls=%async_computation.2 | async-start | bytes 1048576 | tf_op jit(solution)/shard_map/all_to_all | solution.py:241
  120.2 21.9 %collective-permute-start.2 = (bf16[512,128]{1,0:T(8,128)(2,1)S(1)}, bf16[512,128]{1,0:T(8,128)(2,1)S(1)}, u32[]{:S(2)}, u32[]{:S(2)}) collective-permute-start(bf16[512,128]{1,0:T(8,128)(2,1)S(1)} %get-tuple-element.21.table_ref), channel_id=1, source_target_pairs={{503,0},{504,1},{505,2},{506,3},{507,4},{508,5},{509,6},{510,7},{5... | collective-permute-start | bytes 393224 | tf_op jit(solution)/shard_map/ppermute | solution.py:252
  125.0 22.9 %collective-permute-start.3 = (bf16[144,128]{1,0:T(8,128)(2,1)S(1)}, bf16[144,128]{1,0:T(8,128)(2,1)S(1)}, u32[]{:S(2)}, u32[]{:S(2)}) collective-permute-start(bf16[144,128]{1,0:T(8,128)(2,1)S(1)} %copy-done.3), channel_id=1, source_target_pairs={{9,0},{10,1},{11,2},{12,3},{13,4},{14,5},{15,6},{16,7},{17,8},{18,... | collective-permute-start | bytes 110600 | tf_op jit(solution)/shard_map/ppermute | solution.py:252
  142.1 0.9 copy-start.7
where the time goes:
time: 152 us
  starting transfers between devices  76 us (50%)
  waiting for transfers between devices  38.2 us (25%)
  Pallas kernels  21.7 us (14%)
  local copies, waits for them, and re-layouts  14.6 us (10%)
    all_to_all x2, starting transfers between devices, exchange(): return lax.all_to_all(rows, AXES, split_axis=1, concat_axis=1, tiled=True)  33.8 us
    ppermute x4, starting transfers between devices, passed_along(): lax.ppermute(block, AXES, [((i - distance) % n_devices, i) for i in range...  33.2 us
    all_to_all x1, waiting for transfers between devices, exchange_packed(): lax.all_to_all(packed, AXES, split_axis=0, concat_axis=0, tiled=True)  22.6 us
    pallas_call x5, Pallas kernels, call(): pl.pallas_call(kernel, name=name, out_shape=[jax.ShapeDtypeStruct(s, d) f...  21.7 us
    all_to_all x1, starting transfers between devices, exchange_packed(): lax.all_to_all(packed, AXES, split_axis=0, concat_axis=0, tiled=True)  9.09 us
    all_to_all x2, waiting for transfers between devices, exchange(): return lax.all_to_all(rows, AXES, split_axis=1, concat_axis=1, tiled=True)  8.9 us
    ppermute x4, waiting for transfers between devices, passed_along(): lax.ppermute(block, AXES, [((i - distance) % n_devices, i) for i in range...  6.74 us
    unnamed x24, local copies, waits for them, and re-layouts  5.03 us
  transfers between devices with their start and end apart: 7, of which 3 were waited for; matrix products, arithmetic and copies ran while one was open for 3% of the time, Pallas kernels for 2%

commit v1 on v0

v1 whole, which is shorter than its diff:
```python
import jax
import jax.numpy as jnp
from jax import lax
from jax.experimental import pallas as pl
from jax.experimental.pallas import tpu as pltpu
from jax.sharding import PartitionSpec as P

AXES = ("dom", "type")
TILE = 128
CAP = 3
PART = 64
BLOCK = 128
LANES = 128
F32 = jnp.float32
BF16 = jnp.bfloat16


def iota(shape, dim):
    return lax.broadcasted_iota(jnp.int32, shape, dim)


def fiota(shape, dim):
    return iota(shape, dim).astype(F32)


def ones_where(mask):
    return jnp.where(mask, 1.0, 0.0).astype(BF16)


def dot(a, b):
    return jnp.dot(a, b, preferred_element_type=F32)


def eye():
    return iota((LANES, LANES), 0) == iota((LANES, LANES), 1)


def to_row(col):
    return jnp.sum(jnp.where(eye(), col, 0.0), axis=0, keepdims=True)


def to_col(row):
    return jnp.sum(jnp.where(eye(), row, 0.0), axis=1, keepdims=True)


def one_hot_of_col(col, rows):
    return ones_where(col == fiota((col.shape[0], rows), 1))


def one_hot_of_row(row, rows, first):
    return ones_where(row == fiota((rows, row.shape[1]), 0) + first)


def lane_of(episode, slot, part):
    return 16 * episode + 4 * slot + part


def slot_col(table, lane):
    return table[:, lane : lane + 1] * 256.0 + table[:, lane + 1 : lane + 2] - 1.0


def slot_row(turned_ref, lane):
    return turned_ref[lane : lane + 1, :] * 256.0 + turned_ref[lane + 1 : lane + 2, :] - 1.0


def row_dot(a, b):
    return jnp.sum(a * b, axis=1, keepdims=True)


def blocks(n, size, step):
    if n == size:
        step(0, 0)
    else:
        lax.fori_loop(0, n // size, lambda b, c: (step(pl.multiple_of(b * size, size), b), c)[1], 0)


def by_owner(slots_ref, flat_ref, slots, group):
    j = iota((group * PART, slots * PART), 1)
    move = ones_where(iota((group * PART, slots * PART), 0) == (j % PART) * group + j // PART)

    def step(at, b):
        rows = jnp.concatenate([slots_ref[s, pl.ds(at, PART), :] for s in range(slots)], axis=0)
        flat_ref[pl.ds(pl.multiple_of(at * group, PART), group * PART), :] = dot(move, rows).astype(BF16)

    blocks(slots_ref.shape[1], PART, step)


def by_slot(flat_ref, slots_ref, slots, group):
    i = iota((slots * PART, group * PART), 0)
    move = ones_where(iota((slots * PART, group * PART), 1) == (i % PART) * group + i // PART)

    def step(at, b):
        rows = dot(move, flat_ref[pl.ds(pl.multiple_of(at * group, PART), group * PART), :]).astype(BF16)
        for s in range(slots):
            slots_ref[s, pl.ds(at, PART), :] = rows[s * PART : (s + 1) * PART, :]

    blocks(slots_ref.shape[1], PART, step)


def turn(table_ref, turned_ref):
    for o in range(0, table_ref.shape[0], TILE):
        turned_ref[:, o : o + TILE] = jnp.transpose(table_ref[o : o + TILE, :].astype(F32))


def gather_slots(table_ref, slots_ref, out_ref, first_out, episode, part, after=None):
    def step(at, b):
        slots = slots_ref[pl.ds(at, BLOCK), :].astype(F32)
        for s in range(CAP):
            col = slot_col(slots, lane_of(episode, s, part))
            rows = dot(one_hot_of_col(col, table_ref.shape[0]), table_ref[...])
            out_ref[first_out + s, pl.ds(at, BLOCK), :] = rows.astype(BF16)
            if after:
                after(s, at, rows)

    blocks(slots_ref.shape[0], BLOCK, step)


def weigh_slots(here_ref, first_here, there_ref, first_there, out_ref):
    def step(at, b):
        for s in range(CAP):
            here = here_ref[first_here + s, pl.ds(at, BLOCK), :].astype(F32)
            there = there_ref[first_there + s, pl.ds(at, BLOCK), :].astype(F32)
            out_ref[s, pl.ds(at, BLOCK), :] = (jax.nn.sigmoid(row_dot(here, there)) * there).astype(BF16)

    blocks(out_ref.shape[1], BLOCK, step)


def adagrad(
    table_ref, state_ref, new_ref, new_state_ref, turned_ref, terms_ref, lane0, pair_row, pair_terms
):
    width = table_ref.shape[1]
    index = [slot_row(turned_ref, lane0 + 4 * s) for s in range(CAP)]

    def step(at, b):
        first = jnp.asarray(at).astype(F32)
        grad = dot(one_hot_of_row(pair_row, TILE, first), pair_terms)
        for s in range(CAP):
            grad += dot(one_hot_of_row(index[s], TILE, first), terms_ref[s])
        state = jnp.transpose(jnp.broadcast_to(state_ref[pl.ds(b, 1), :], (TILE, TILE)))
        state = state + row_dot(grad, grad) * (1.0 / width)
        rows = table_ref[pl.ds(at, TILE), :].astype(F32) - 0.5 * grad / jnp.sqrt(state)
        new_ref[pl.ds(at, TILE), :] = rows.astype(BF16)
        new_state_ref[pl.ds(b, 1), :] = jnp.transpose(state)[0:1, :]

    blocks(table_ref.shape[0], TILE, step)


def pairs_out(pairs_ref, episode, table_ref, out_ref):
    pairs = pairs_ref[episode].astype(F32)
    n = pairs.shape[0]
    rows = dot(one_hot_of_col(pairs[:, 0:1], table_ref.shape[0]), table_ref[...])
    out_ref[0:n, :] = rows.astype(BF16)
    high = jnp.floor(pairs[:, 1:2] * (1.0 / 256.0))
    low = pairs[:, 1:2] - high * 256.0
    which = iota((16, LANES), 0)
    tail = jnp.where(which == 0, to_row(high), jnp.where(which == 1, to_row(low), 0.0))
    out_ref[n : n + 16, :] = tail.astype(BF16)


def pair_terms_of(here, there):
    return ((jax.nn.sigmoid(row_dot(here, there)) - 1.0) * there).astype(BF16)


def first_kernel(owner_ref, row_ref, pairs_ref, table_ref, flat_ref, rows_ref, pair_ref):
    episodes, pairs, negatives = owner_ref.shape
    owners = rows_ref.shape[1]
    lane = iota((pairs, LANES), 1)
    part = lane % 4
    slot_of_lane = ((lane // 4) % 4).astype(F32)
    earlier = iota((pairs, pairs), 1) < iota((pairs, pairs), 0)
    owner_rows, values = [], []
    for e in range(episodes):
        vertex = pairs_ref[e].astype(F32)[:, 0:1] + 1.0
        vertex_high = jnp.floor(vertex * (1.0 / 256.0))
        cols = [owner_ref[e].astype(F32)[:, k : k + 1] for k in range(negatives)]
        rows = [to_row(c) for c in cols]
        for k in range(negatives):
            same = jnp.where((cols[k] == rows[k]) & earlier, 1.0, 0.0)
            for j in range(k):
                same += jnp.where(cols[k] == rows[j], 1.0, 0.0)
            rank = jnp.sum(same, axis=1, keepdims=True)
            target = row_ref[e].astype(F32)[:, k : k + 1] + 1.0
            target_high = jnp.floor(target * (1.0 / 256.0))
            value = jnp.where(part == 0, target_high, target - 256.0 * target_high)
            value = jnp.where(part == 2, vertex_high, value)
            value = jnp.where(part == 3, vertex - 256.0 * vertex_high, value)
            mine = (slot_of_lane == rank) & (lane // 16 == e)
            values.append(jnp.where(mine, value, 0.0).astype(BF16))
            owner_rows.append(rows[k])

    for o in range(0, owners, TILE):
        total = jnp.zeros((TILE, LANES), F32)
        for row, value in zip(owner_rows, values):
            total += dot(one_hot_of_row(row, TILE, float(o)), value)
        rows_ref[CAP, o : o + TILE, :] = total.astype(BF16)
    gather_slots(table_ref, rows_ref.at[CAP], rows_ref, 0, 0, 2)
    by_owner(rows_ref, flat_ref, CAP + 1, CAP + 1)
    pairs_out(pairs_ref, 0, table_ref, pair_ref)


def context_side(pair_ref, table_ref):
    n = pair_ref.shape[0] - 16
    tail = pair_ref[n : n + 16, :].astype(F32)
    row = tail[0:1, :] * 256.0 + tail[1:2, :]
    mine = dot(one_hot_of_col(to_col(row), table_ref.shape[0]), table_ref[...])
    return row, pair_terms_of(mine, pair_ref[0:n, :].astype(F32))


def vertex_side(pairs_ref, episode, table_ref, partner_ref):
    pairs = pairs_ref[episode].astype(F32)
    mine = dot(one_hot_of_col(pairs[:, 0:1], table_ref.shape[0]), table_ref[...])
    theirs = dot(one_hot_of_col(pairs[:, 1:2], partner_ref.shape[0]), partner_ref[...])
    return to_row(pairs[:, 0:1]), pair_terms_of(mine, theirs)


def context_first(
    flat_ref, pair_ref, table_ref, state_ref,
    send_ref, slots_ref, new_ref, new_state_ref, rows_ref, got_ref, turned_ref, terms_ref,
):
    by_slot(flat_ref, got_ref, CAP + 1, CAP + 1)
    slots_ref[...] = got_ref[CAP]
    turn(slots_ref, turned_ref)

    def weigh(s, at, mine):
        there = got_ref[s, pl.ds(at, BLOCK), :].astype(F32)
        terms_ref[s, pl.ds(at, BLOCK), :] = (jax.nn.sigmoid(row_dot(mine, there)) * there).astype(BF16)

    gather_slots(table_ref, slots_ref, rows_ref, 0, 0, 0, weigh)
    row, pair_terms = context_side(pair_ref, table_ref)
    adagrad(
        table_ref, state_ref, new_ref, new_state_ref, turned_ref, terms_ref, lane_of(0, 0, 0), row, pair_terms
    )
    gather_slots(new_ref, slots_ref, rows_ref, CAP, 1, 0)
    by_owner(rows_ref, send_ref, 2 * CAP, 2 * CAP)


def vertex_first(
    flat_ref, sent_ref, pairs_ref, partner_ref, table_ref, state_ref,
    send_ref, rows_ref, got_ref, pair_ref, new_ref, new_state_ref, turned_ref, terms_ref,
):
    by_slot(flat_ref, got_ref, 2 * CAP, 2 * CAP)
    turn(sent_ref.at[CAP], turned_ref)
    weigh_slots(sent_ref, 0, got_ref, 0, terms_ref)
    row, pair_terms = vertex_side(pairs_ref, 0, table_ref, partner_ref)
    adagrad(
        table_ref, state_ref, new_ref, new_state_ref, turned_ref, terms_ref, lane_of(0, 0, 2), row, pair_terms
    )
    gather_slots(new_ref, sent_ref.at[CAP], rows_ref, 0, 1, 2)
    by_owner(rows_ref, send_ref, CAP, CAP + 1)
    pairs_out(pairs_ref, 1, new_ref, pair_ref)


def vertex_last(
    got_ref, rows_ref, sent_ref, pairs_ref, partner_ref, table_ref, state_ref, slots_ref, context_ref,
    new_ref, new_state_ref, context_rows_ref, context_turned_ref, turned_ref, terms_ref,
):
    gather_slots(context_ref, slots_ref, context_rows_ref, 0, 1, 0)
    turn(slots_ref, context_turned_ref)
    turn(sent_ref.at[CAP], turned_ref)
    weigh_slots(rows_ref, 0, got_ref, CAP, terms_ref)
    row, pair_terms = vertex_side(pairs_ref, 1, table_ref, partner_ref)
    adagrad(
        table_ref, state_ref, new_ref, new_state_ref, turned_ref, terms_ref, lane_of(1, 0, 2), row, pair_terms
    )


def context_last(
    flat_ref, rows_ref, turned_ref, pair_ref, table_ref, state_ref, new_ref, new_state_ref, got_ref, terms_ref
):
    by_slot(flat_ref, got_ref, CAP, CAP + 1)
    weigh_slots(rows_ref, 0, got_ref, 0, terms_ref)
    row, pair_terms = context_side(pair_ref, table_ref)
    adagrad(
        table_ref, state_ref, new_ref, new_state_ref, turned_ref, terms_ref, lane_of(1, 0, 0), row, pair_terms
    )


def call(kernel, name, outs, scratch, *args):
    return pl.pallas_call(
        kernel,
        name=name,
        out_shape=[jax.ShapeDtypeStruct(s, d) for s, d in outs],
        scratch_shapes=scratch,
        compiler_params=pltpu.CompilerParams(vmem_limit_bytes=24 * 1024 * 1024),
        cost_estimate=pl.CostEstimate(flops=600_000_000, bytes_accessed=4_000_000, transcendentals=2000),
    )(*args)


def exchange(flat, n):
    shape = flat.shape
    per = shape[0] // n
    sub = 2 if per % 4 else 4
    split = flat.reshape(n, per // sub, sub, shape[1]) if per > sub else flat.reshape(n, per, shape[1])
    return lax.all_to_all(split, AXES, split_axis=0, concat_axis=0, tiled=True).reshape(shape)


def passed_along(block, distance, n_devices):
    return lax.ppermute(block, AXES, [((i - distance) % n_devices, i) for i in range(n_devices)])


def body(
    vertex_table, context_table, vertex_state, context_state, pair_blocks, pair_offsets, negative_owner, negative_row
):
    n_type = lax.axis_size("type")
    n = lax.axis_size("dom") * n_type
    rows, width = vertex_table.shape
    episodes, block_pairs, per_block, negatives = negative_owner.shape
    n_pairs = block_pairs * per_block
    shifts = [1 + n_type * (e + 1) for e in range(episodes)]
    pairs = (pair_blocks[:, :, None, :] * TILE + pair_offsets).reshape(episodes, n_pairs, 2)
    owner = negative_owner.reshape(episodes, n_pairs, negatives)
    target = negative_row.reshape(episodes, n_pairs, negatives)
    v_state = vertex_state.reshape(rows // TILE, TILE)
    c_state = context_state.reshape(rows // TILE, TILE)

    table = ((rows, width), BF16)
    state = ((rows // TILE, TILE), F32)
    pair_rows = ((n_pairs + 16, width), BF16)

    def flat(slots):
        return ((n * slots, width), BF16)

    def slots(number):
        return ((number, n, width), BF16)

    turned = pltpu.VMEM((LANES, n), F32)
    terms = pltpu.VMEM((CAP, n, width), BF16)

    flat_a, rows_a, pair_a = call(
        first_kernel, "slots", [flat(CAP + 1), slots(CAP + 1), pair_rows], [], owner, target, pairs, vertex_table
    )
    context_table, pair_a, flat_a = lax.optimization_barrier((context_table, pair_a, flat_a))
    partner_0 = passed_along(context_table, shifts[0], n)
    got_pair_a = passed_along(pair_a, n - shifts[0], n)
    got_a = exchange(flat_a, n)
    got_a, got_pair_a, partner_0 = lax.optimization_barrier((got_a, got_pair_a, partner_0))
    flat_b, slots_b, context_1, c_state_1 = call(
        context_first, "context_first", [flat(2 * CAP), ((n, LANES), BF16), table, state],
        [pltpu.VMEM((2 * CAP, n, width), BF16), pltpu.VMEM((CAP + 1, n, width), BF16), turned, terms],
        got_a, got_pair_a, context_table, c_state,
    )
    partner_1 = passed_along(context_1, shifts[1], n)
    got_b = exchange(flat_b, n)
    got_b, partner_1 = lax.optimization_barrier((got_b, partner_1))
    flat_c, rows_c, rows_got_b, pair_c, vertex_1, v_state_1 = call(
        vertex_first, "vertex_first", [flat(CAP + 1), slots(CAP), slots(2 * CAP), pair_rows, table, state],
        [turned, terms],
        got_b, rows_a, pairs, partner_0, vertex_table, v_state,
    )
    got_pair_c = passed_along(pair_c, n - shifts[1], n)
    got_c = exchange(flat_c, n)
    vertex_2, v_state_2, rows_b, turned_b = call(
        vertex_last, "vertex_last", [table, state, slots(CAP), ((LANES, n), F32)], [turned, terms],
        rows_got_b, rows_c, rows_a, pairs, partner_1, vertex_1, v_state_1, slots_b, context_1,
    )
    context_2, c_state_2 = call(
        context_last, "context_last", [table, state], [pltpu.VMEM((CAP, n, width), BF16), terms],
        got_c, rows_b, turned_b, got_pair_c, context_1, c_state_1,
    )
    return vertex_2, context_2, v_state_2.reshape(rows), c_state_2.reshape(rows)


def solution(mesh):
    in_specs = (
        P(AXES, None),
        P(AXES, None),
        P(AXES),
        P(AXES),
        P(None, AXES, None),
        P(None, AXES, None, None),
        P(None, AXES, None, None),
        P(None, AXES, None, None),
    )
    out_specs = (P(AXES, None), P(AXES, None), P(AXES), P(AXES))
    return jax.shard_map(body, mesh=mesh, in_specs=in_specs, out_specs=out_specs, check_vma=False)
```

time: 152 us -> 149 us (0.980)
  Pallas kernels: 21.7 us -> 33.6 us
  local copies, waits for them, and re-layouts: 14.6 us -> 4.62 us
  starting transfers between devices: 76 us -> 72.8 us
  waiting for transfers between devices: 38.2 us -> 35.2 us
    all_to_all x3, waiting for transfers between devices: 31.5 us -> 3.3 us  [exchange(): lax.all_to_all(split, AXES, split_axis=0, concat_axis=0, tiled=True)]
    ppermute x4, waiting for transfers between devices: 6.74 us -> 31.9 us  [passed_along(): lax.ppermute(block, AXES, [((i - distance) % n_devices, i) for i in range...]
    pallas_call x5, Pallas kernels: 21.7 us -> 33.6 us  [call(): pl.pallas_call(kernel, name=name, out_shape=[jax.ShapeDtypeStruct(s, d) f...]
    all_to_all x3 -> x0, local copies, waits for them, and re-layouts: 3.29 us -> none  [the longest x1 2.12 us: exchange_packed(): lax.all_to_all(packed, AXES, split_axis=0, concat_axis=0, tiled=True)]
    all_to_all x3, starting transfers between devices: 42.9 us -> 40.2 us  [exchange(): lax.all_to_all(split, AXES, split_axis=0, concat_axis=0, tiled=True)]
    pallas_call x2 -> x0, local copies, waits for them, and re-layouts: 2.35 us -> none  [call(): pl.pallas_call(kernel, name=name, out_shape=[jax.ShapeDtypeStruct(s, d) f...]
    reshape x2 -> x0, local copies, waits for them, and re-layouts: 2.14 us -> none  [exchange_packed(): rows.reshape(2, s // 2, n, w).transpose(2, 0, 1, 3)]
    unnamed x24 -> x18, local copies, waits for them, and re-layouts: 5.03 us -> 4.36 us
  transfers between devices with their start and end apart: 7 -> 7, of which waited for: 3 -> 4; matrix products, arithmetic and copies ran while one was open for 3% -> 0% of each run, Pallas kernels for 2% -> 3%
where the time goes in v1:
time: 149 us; the launch traced here: 148 us
  starting transfers between devices  72.8 us (49%)
  waiting for transfers between devices  35.2 us (24%)
  Pallas kernels  33.6 us (23%)
  local copies, waits for them, and re-layouts  4.62 us (3%)
    all_to_all x3, starting transfers between devices, exchange(): lax.all_to_all(split, AXES, split_axis=0, concat_axis=0, tiled=True)  40.2 us
    pallas_call x5, Pallas kernels, call(): pl.pallas_call(kernel, name=name, out_shape=[jax.ShapeDtypeStruct(s, d) f...  33.6 us
    ppermute x4, starting transfers between devices, passed_along(): lax.ppermute(block, AXES, [((i - distance) % n_devices, i) for i in range...  32.6 us
    ppermute x4, waiting for transfers between devices, passed_along(): lax.ppermute(block, AXES, [((i - distance) % n_devices, i) for i in range...  31.9 us
    unnamed x18, local copies, waits for them, and re-layouts  4.36 us
    all_to_all x3, waiting for transfers between devices, exchange(): lax.all_to_all(split, AXES, split_axis=0, concat_axis=0, tiled=True)  3.3 us
  transfers between devices with their start and end apart: 7, of which 4 were waited for; matrix products, arithmetic and copies ran while one was open for 0% of the time, Pallas kernels for 3%

profile of v1, /device:TPU:1, one launch (start us, length us, event | category | flops | bytes accessed | tf_op | source)
XLA Modules:
  0.0 148.4 jit_solution(10833594821962110298)
XLA Ops:
  0.6 0.7 broadcast_multiply_fusion
  1.3 0.1 copy.14
  1.4 0.8 broadcast_add_fusion
  2.2 0.0 copy-start.6
  2.2 0.2 copy.15
  2.4 0.6 copy-done.6
  3.0 0.2 copy.12
  3.2 0.6 copy-done.7
  3.8 0.2 copy.13
  3.9 0.7 copy-done.1
  4.7 5.6 %slots.1 = (bf16[2048,128]{1,0:T(8,128)(2,1)}, bf16[4,512,128]{2,1,0:T(8,128)(2,1)S(1)}, bf16[144,128]{1,0:T(8,128)(2,1)S(1)}) custom-call(s32[2,128,5]{2,1,0:T(8,128)S(1)} %bitcast.19, s32[2,128,5]{2,1,0:T(8,128)S(1)} %bitcast.20, s32[2,128,2]{2,1,0:T(8,128)S(1)} %bitcast.16, bf16[512,128]{1,0:T(8,128)(2,1)S(1)} %copy-done.1), custom_call_target="tpu_custom_call" | custom-call | flops 600000000 | bytes 4000000 | tf_op jit(solution)/shard_map/slots/pallas_call | solution.py:279
  10.3 22.2 %all-to-all-start = ((bf16[512,4,128]{2,1,0:T(4,128)(2,1)}), bf16[512,4,128]{2,1,0:T(4,128)(2,1)S(1)}, u32[]{:S(2)}, u32[]{:S(2)}) async-start(bf16[512,4,128]{2,1,0:T(4,128)(2,1)} %bitcast.3), calls=%async_computation | async-start | bytes 1048576 | tf_op jit(solution)/shard_map/all_to_all | solution.py:294
  32.4 0.0 copy-start.4
  32.4 4.8 %collective-permute-start.1 = (bf16[512,128]{1,0:T(8,128)(2,1)S(1)}, bf16[512,128]{1,0:T(8,128)(2,1)S(1)}, u32[]{:S(2)}, u32[]{:S(2)}) collective-permute-start(bf16[512,128]{1,0:T(8,128)(2,1)S(1)} %copy-done), channel_id=1, source_target_pairs={{507,0},{508,1},{509,2},{510,3},{511,4},{0,5},{1,6},{2,7},{3,8},{4... | collective-permute-start | bytes 393224 | tf_op jit(solution)/shard_map/ppermute | solution.py:298
  37.3 9.9 %collective-permute-start = (bf16[144,128]{1,0:T(8,128)(2,1)S(1)}, bf16[144,128]{1,0:T(8,128)(2,1)S(1)}, u32[]{:S(2)}, u32[]{:S(2)}) collective-permute-start(bf16[144,128]{1,0:T(8,128)(2,1)S(1)} %get-tuple-element.34), channel_id=1, source_target_pairs={{5,0},{6,1},{7,2},{8,3},{9,4},{10,5},{11,6},{12,7},{13,8},{14,9},{... | collective-permute-start | bytes 110600 | tf_op jit(solution)/shard_map/ppermute | solution.py:298
  47.3 1.0 collective-permute-done.pair_ref
  48.3 6.5 %collective-permute-done.1.partner_ref = bf16[512,128]{1,0:T(8,128)(2,1)S(1)} collective-permute-done((bf16[512,128]{1,0:T(8,128)(2,1)S(1)}, bf16[512,128]{1,0:T(8,128)(2,1)S(1)}, u32[]{:S(2)}, u32[]{:S(2)}) %collective-permute-start.1) | collective-permute-done | bytes 131104 | tf_op jit(solution)/shard_map/ppermute | solution.py:298
  54.8 0.0 all-to-all-done
  54.8 9.9 %context_first.1 = (bf16[3072,128]{1,0:T(8,128)(2,1)}, bf16[512,128]{1,0:T(8,128)(2,1)S(1)}, bf16[512,128]{1,0:T(8,128)(2,1)S(1)}, f32[4,128]{1,0:T(4,128)S(1)}) custom-call(bf16[2048,128]{1,0:T(8,128)(2,1)S(1)} %bitcast.15, bf16[144,128]{1,0:T(8,128)(2,1)S(1)} %collective-permute-done.pair_ref, bf16[512,128]{1,0:T(8,128)(2,1)S(1)} %copy-done, ...), custom_call_target="tpu_custom_call" | custom-call | flops 600000000 | bytes 4000000 | tf_op jit(solution)/shard_map/context_first/pallas_call | solution.py:279
  64.7 9.0 %all-to-all-start.1 = ((bf16[512,3,2,128]{3,2,1,0:T(2,128)(2,1)}), bf16[512,3,2,128]{3,2,1,0:T(2,128)(2,1)S(1)}, u32[]{:S(2)}, u32[]{:S(2)}) async-start(bf16[512,3,2,128]{3,2,1,0:T(2,128)(2,1)} %bitcast.6), calls=%async_computation.1 | async-start | bytes 1572864 | tf_op jit(solution)/shard_map/all_to_all | solution.py:294
  73.7 4.7 %collective-permute-start.2 = (bf16[512,128]{1,0:T(8,128)(2,1)S(1)}, bf16[512,128]{1,0:T(8,128)(2,1)S(1)}, u32[]{:S(2)}, u32[]{:S(2)}) collective-permute-start(bf16[512,128]{1,0:T(8,128)(2,1)S(1)} %get-tuple-element.39.context_ref.table_ref), channel_id=1, source_target_pairs={{503,0},{504,1},{505,2},{506,3},{507,4},{508,5},{509,6},{510,7},{5... | collective-permute-start | bytes 393224 | tf_op jit(solution)/shard_map/ppermute | solution.py:298
  78.5 24.3 %collective-permute-done.2.partner_ref = bf16[512,128]{1,0:T(8,128)(2,1)S(1)} collective-permute-done((bf16[512,128]{1,0:T(8,128)(2,1)S(1)}, bf16[512,128]{1,0:T(8,128)(2,1)S(1)}, u32[]{:S(2)}, u32[]{:S(2)}) %collective-permute-start.2) | collective-permute-done | bytes 131104 | tf_op jit(solution)/shard_map/ppermute | solution.py:298
  102.8 0.0 all-to-all-done.1
  102.8 0.7 copy-done.5
  103.5 8.6 %vertex_first.1 = (bf16[2048,128]{1,0:T(8,128)(2,1)}, bf16[3,512,128]{2,1,0:T(8,128)(2,1)S(1)}, bf16[6,512,128]{2,1,0:T(8,128)(2,1)S(1)}, bf16[144,128]{1,0:T(8,...) custom-call(bf16[3072,128]{1,0:T(8,128)(2,1)S(1)} %bitcast.13, ...), custom_call_target="tpu_custom_call" | custom-call | flops 600000000 | bytes 4000000 | tf_op jit(solution)/shard_map/vertex_first/pallas_call | solution.py:279
  112.1 9.0 %all-to-all-start.2 = ((bf16[512,4,128]{2,1,0:T(4,128)(2,1)}), bf16[512,4,128]{2,1,0:T(4,128)(2,1)S(1)}, u32[]{:S(2)}, u32[]{:S(2)}) async-start(bf16[512,4,128]{2,1,0:T(4,128)(2,1)} %bitcast.9), calls=%async_computation.2 | async-start | bytes 1048576 | tf_op jit(solution)/shard_map/all_to_all | solution.py:294
  121.1 13.1 %collective-permute-start.3 = (bf16[144,128]{1,0:T(8,128)(2,1)}, bf16[144,128]{1,0:T(8,128)(2,1)S(1)}, u32[]{:S(2)}, u32[]{:S(2)}) collective-permute-start(bf16[144,128]{1,0:T(8,128)(2,1)} %get-tuple-element.53), channel_id=1, source_target_pairs={{9,0},{10,1},{11,2},{12,3},{13,4},{14,5},{15,6},{16,7},{17,8},{18,... | collective-permute-start | bytes 110600 | tf_op jit(solution)/shard_map/ppermute | solution.py:298
  134.3 4.9 %vertex_last.1 = (bf16[512,128]{1,0:T(8,128)(2,1)}, f32[4,128]{1,0:T(4,128)}, bf16[3,512,128]{2,1,0:T(8,128)(2,1)S(1)}, f32[128,512]{1,0:T(8,128)S(1)}) custom-call(bf16[6,512,128]{2,1,0:T(8,128)(2,1)S(1)} %get-tuple-element.43.got_ref, bf16[3,512,128]{2,1,0:T(8,128)(2,1)S(1)} %get-tuple-element.44.rows_ref, ...), custom_call_target="tpu_custom_call" | custom-call | flops 600000000 | bytes 4000000 | tf_op jit(solution)/shard_map/vertex_last/pallas_call | solution.py:279
  139.1 0.6 copy-done.2
  139.8 3.3 %all-to-all-done.2 = bf16[512,4,128]{2,1,0:T(4,128)(2,1)S(1)} async-done(((bf16[512,4,128]{2,1,0:T(4,128)(2,1)}), bf16[512,4,128]{2,1,0:T(4,128)(2,1)S(1)}, u32[]{:S(2)}, u32[]{:S(2)}) %all-to-all-start.2) | async-done | bytes 524320 | tf_op jit(solution)/shard_map/all_to_all | solution.py:294
  143.1 0.8 copy-done.3
  143.8 4.6 %context_last.1 = (bf16[512,128]{1,0:T(8,128)(2,1)}, f32[4,128]{1,0:T(4,128)}) custom-call(bf16[2048,128]{1,0:T(8,128)(2,1)S(1)} %bitcast.14, bf16[3,512,128]{2,1,0:T(8,128)(2,1)S(1)} %get-tuple-element.51.rows_ref, f32[128,512]{1,0:T(8,128)S(1)} %get-tuple-element.52.turned_ref, bf16[144,128]{1,0:T(8,128)(2,1)S(1)} %copy-done.3, ...), custom_call_target="tpu_custom_call" | custom-call | flops 600000000 | bytes 4000000 | tf_op jit(solution)/shard_map/context_last/pallas_call | solution.py:279
  (9 shorter events, 0.0 us)
Async XLA Ops:
  2.2 0.8 copy-start.6
  3.0 0.8 copy-start.7
  3.8 0.9 copy-start.1
  10.3 22.2 %copy-start = (bf16[512,128]{1,0:T(8,128)(2,1)S(1)}, bf16[512,128]{1,0:T(8,128)(2,1)}, u32[]{:S(2)}) copy-start(bf16[512,128]{1,0:T(8,128)(2,1)} %table_ref.3) | copy-start | bytes 393220
  10.3 44.6 %all-to-all-start = ((bf16[512,4,128]{2,1,0:T(4,128)(2,1)}), bf16[512,4,128]{2,1,0:T(4,128)(2,1)S(1)}, u32[]{:S(2)}, u32[]{:S(2)}) async-start(bf16[512,4,128]{2,1,0:T(4,128)(2,1)} %bitcast.3), calls=%async_computation | async-start | bytes 1048576 | tf_op jit(solution)/shard_map/all_to_all | solution.py:294
  32.4 22.4 %copy-start.4 = (f32[512]{0:T(512)S(1)}, f32[512]{0:T(512)}, u32[]{:S(2)}) copy-start(f32[512]{0:T(512)} %param.11) | copy-start | bytes 6148
  32.4 22.4 %collective-permute-start.1 = (bf16[512,128]{1,0:T(8,128)(2,1)S(1)}, bf16[512,128]{1,0:T(8,128)(2,1)S(1)}, u32[]{:S(2)}, u32[]{:S(2)}) collective-permute-start(bf16[512,128]{1,0:T(8,128)(2,1)S(1)} %copy-done), channel_id=1, source_target_pairs={{507,0},{508,1},{509,2},{510,3},{511,4},{0,5},{1,6},{2,7},{3,8},{4... | collective-permute-start | bytes 393224 | tf_op jit(solution)/shard_map/ppermute | solution.py:298
  37.3 11.0 %collective-permute-start = (bf16[144,128]{1,0:T(8,128)(2,1)S(1)}, bf16[144,128]{1,0:T(8,128)(2,1)S(1)}, u32[]{:S(2)}, u32[]{:S(2)}) collective-permute-start(bf16[144,128]{1,0:T(8,128)(2,1)S(1)} %get-tuple-element.34), channel_id=1, source_target_pairs={{5,0},{6,1},{7,2},{8,3},{9,4},{10,5},{11,6},{12,7},{13,8},{14,9},{... | collective-permute-start | bytes 110600 | tf_op jit(solution)/shard_map/ppermute | solution.py:298
  64.7 38.1 %all-to-all-start.1 = ((bf16[512,3,2,128]{3,2,1,0:T(2,128)(2,1)}), bf16[512,3,2,128]{3,2,1,0:T(2,128)(2,1)S(1)}, u32[]{:S(2)}, u32[]{:S(2)}) async-start(bf16[512,3,2,128]{3,2,1,0:T(2,128)(2,1)} %bitcast.6), calls=%async_computation.1 | async-start | bytes 1572864 | tf_op jit(solution)/shard_map/all_to_all | solution.py:294
  73.7 29.1 %collective-permute-start.2 = (bf16[512,128]{1,0:T(8,128)(2,1)S(1)}, bf16[512,128]{1,0:T(8,128)(2,1)S(1)}, u32[]{:S(2)}, u32[]{:S(2)}) collective-permute-start(bf16[512,128]{1,0:T(8,128)(2,1)S(1)} %get-tuple-element.39.context_ref.table_ref), channel_id=1, source_target_pairs={{503,0},{504,1},{505,2},{506,3},{507,4},{508,5},{509,6},{510,7},{5... | collective-permute-start | bytes 393224 | tf_op jit(solution)/shard_map/ppermute | solution.py:298
  102.8 0.7 copy-start.5
  112.1 31.0 %all-to-all-start.2 = ((bf16[512,4,128]{2,1,0:T(4,128)(2,1)}), bf16[512,4,128]{2,1,0:T(4,128)(2,1)S(1)}, u32[]{:S(2)}, u32[]{:S(2)}) async-start(bf16[512,4,128]{2,1,0:T(4,128)(2,1)} %bitcast.9), calls=%async_computation.2 | async-start | bytes 1048576 | tf_op jit(solution)/shard_map/all_to_all | solution.py:294
  121.1 18.0 %collective-permute-start.3 = (bf16[144,128]{1,0:T(8,128)(2,1)}, bf16[144,128]{1,0:T(8,128)(2,1)S(1)}, u32[]{:S(2)}, u32[]{:S(2)}) collective-permute-start(bf16[144,128]{1,0:T(8,128)(2,1)} %get-tuple-element.53), channel_id=1, source_target_pairs={{9,0},{10,1},{11,2},{12,3},{13,4},{14,5},{15,6},{16,7},{17,8},{18,... | collective-permute-start | bytes 110600 | tf_op jit(solution)/shard_map/ppermute | solution.py:298
  139.1 0.6 copy-start.2
  143.1 0.8 copy-start.3

commit v2 on v1

--- a/solution.py
+++ b/solution.py
@@ -68,10 +68,8 @@
 
 
 def blocks(n, size, step):
-    if n == size:
-        step(0, 0)
-    else:
-        lax.fori_loop(0, n // size, lambda b, c: (step(pl.multiple_of(b * size, size), b), c)[1], 0)
+    for b in range(n // size):
+        step(b * size, b)
 
 
 def by_owner(slots_ref, flat_ref, slots, group):
@@ -80,7 +78,7 @@
 
     def step(at, b):
         rows = jnp.concatenate([slots_ref[s, pl.ds(at, PART), :] for s in range(slots)], axis=0)
-        flat_ref[pl.ds(pl.multiple_of(at * group, PART), group * PART), :] = dot(move, rows).astype(BF16)
+        flat_ref[pl.ds(at * group, group * PART), :] = dot(move, rows).astype(BF16)
 
     blocks(slots_ref.shape[1], PART, step)
 
@@ -90,7 +88,7 @@
     move = ones_where(iota((slots * PART, group * PART), 1) == (i % PART) * group + i // PART)
 
     def step(at, b):
-        rows = dot(move, flat_ref[pl.ds(pl.multiple_of(at * group, PART), group * PART), :]).astype(BF16)
+        rows = dot(move, flat_ref[pl.ds(at * group, group * PART), :]).astype(BF16)
         for s in range(slots):
             slots_ref[s, pl.ds(at, PART), :] = rows[s * PART : (s + 1) * PART, :]
 
@@ -146,8 +144,8 @@
 
 
 def pairs_out(pairs_ref, episode, table_ref, out_ref):
-    pairs = pairs_ref[episode].astype(F32)
-    n = pairs.shape[0]
+    n = pairs_ref.shape[0]
+    pairs = pairs_ref[:, 2 * episode : 2 * episode + 2]
     rows = dot(one_hot_of_col(pairs[:, 0:1], table_ref.shape[0]), table_ref[...])
     out_ref[0:n, :] = rows.astype(BF16)
     high = jnp.floor(pairs[:, 1:2] * (1.0 / 256.0))
@@ -161,25 +159,54 @@
     return ((jax.nn.sigmoid(row_dot(here, there)) - 1.0) * there).astype(BF16)
 
 
-def first_kernel(owner_ref, row_ref, pairs_ref, table_ref, flat_ref, rows_ref, pair_ref):
-    episodes, pairs, negatives = owner_ref.shape
+def columns_of(grids):
+    high_part, groups = LANES // 8, []
+    spread = ones_where(iota((LANES, 8), 0) // high_part == iota((LANES, 8), 1))
+    keep = iota((LANES, LANES), 1) % high_part == iota((LANES, LANES), 0) % high_part
+    collect = ones_where(iota((LANES, LANES), 0) // high_part == iota((LANES, LANES), 1))
+    for g in range(0, len(grids), 8):
+        wide = jnp.concatenate(grids[g : g + 8], axis=1)
+        high = jnp.floor(wide * (1.0 / 256.0))
+        total = 0.0
+        for digit, scale in ((high, 256.0), (wide - 256.0 * high, 1.0)):
+            kept = jnp.where(keep, dot(spread, digit.astype(BF16)), 0.0).astype(BF16)
+            total = total + scale * dot(kept, collect)
+        groups.append(total)
+    return [groups[i // 8][:, i % 8 : i % 8 + 1] for i in range(len(grids))]
+
+
+def first_kernel(owner_ref, row_ref, block_ref, offset_ref, table_ref, flat_ref, rows_ref, pair_ref, pairs_ref):
+    episodes, negatives = owner_ref.shape[:2]
+    pairs = pairs_ref.shape[0]
     owners = rows_ref.shape[1]
     lane = iota((pairs, LANES), 1)
     part = lane % 4
     slot_of_lane = ((lane // 4) % 4).astype(F32)
     earlier = iota((pairs, pairs), 1) < iota((pairs, pairs), 0)
+    grids = [r[e, k].astype(F32) for r in (owner_ref, row_ref) for e in range(episodes) for k in range(negatives)]
+    grids += [offset_ref[e, :, w, :].astype(F32) for e in range(episodes) for w in range(2)]
+    columns = columns_of(grids)
+    wide = jnp.zeros((pairs, LANES), F32)
+    for e in range(episodes):
+        for w in range(2):
+            which = block_ref[e, w : w + 1, :].astype(F32)
+            here = iota((pairs, 8), 1) == iota((pairs, 8), 0) // (pairs // 8)
+            block = jnp.sum(jnp.where(here, which, 0.0), axis=1, keepdims=True)
+            column = block * float(TILE) + columns[2 * episodes * negatives + 2 * e + w]
+            wide = jnp.where(lane == 2 * e + w, column, wide)
+    pairs_ref[...] = wide
     owner_rows, values = [], []
     for e in range(episodes):
-        vertex = pairs_ref[e].astype(F32)[:, 0:1] + 1.0
+        vertex = wide[:, 2 * e : 2 * e + 1] + 1.0
         vertex_high = jnp.floor(vertex * (1.0 / 256.0))
-        cols = [owner_ref[e].astype(F32)[:, k : k + 1] for k in range(negatives)]
+        cols = columns[e * negatives : (e + 1) * negatives]
         rows = [to_row(c) for c in cols]
         for k in range(negatives):
             same = jnp.where((cols[k] == rows[k]) & earlier, 1.0, 0.0)
             for j in range(k):
                 same += jnp.where(cols[k] == rows[j], 1.0, 0.0)
             rank = jnp.sum(same, axis=1, keepdims=True)
-            target = row_ref[e].astype(F32)[:, k : k + 1] + 1.0
+            target = columns[(episodes + e) * negatives + k] + 1.0
             target_high = jnp.floor(target * (1.0 / 256.0))
             value = jnp.where(part == 0, target_high, target - 256.0 * target_high)
             value = jnp.where(part == 2, vertex_high, value)
@@ -207,7 +234,7 @@
 
 
 def vertex_side(pairs_ref, episode, table_ref, partner_ref):
-    pairs = pairs_ref[episode].astype(F32)
+    pairs = pairs_ref[:, 2 * episode : 2 * episode + 2]
     mine = dot(one_hot_of_col(pairs[:, 0:1], table_ref.shape[0]), table_ref[...])
     theirs = dot(one_hot_of_col(pairs[:, 1:2], partner_ref.shape[0]), partner_ref[...])
     return to_row(pairs[:, 0:1]), pair_terms_of(mine, theirs)
@@ -275,13 +302,13 @@
     )
 
 
-def call(kernel, name, outs, scratch, *args):
+def call(kernel, name, outs, scratch, *args, mib=24):
     return pl.pallas_call(
         kernel,
         name=name,
         out_shape=[jax.ShapeDtypeStruct(s, d) for s, d in outs],
         scratch_shapes=scratch,
-        compiler_params=pltpu.CompilerParams(vmem_limit_bytes=24 * 1024 * 1024),
+        compiler_params=pltpu.CompilerParams(vmem_limit_bytes=mib * 1024 * 1024),
         cost_estimate=pl.CostEstimate(flops=600_000_000, bytes_accessed=4_000_000, transcendentals=2000),
     )(*args)
 
@@ -307,9 +334,10 @@
     episodes, block_pairs, per_block, negatives = negative_owner.shape
     n_pairs = block_pairs * per_block
     shifts = [1 + n_type * (e + 1) for e in range(episodes)]
-    pairs = (pair_blocks[:, :, None, :] * TILE + pair_offsets).reshape(episodes, n_pairs, 2)
-    owner = negative_owner.reshape(episodes, n_pairs, negatives)
-    target = negative_row.reshape(episodes, n_pairs, negatives)
+    owner = negative_owner.transpose(0, 3, 1, 2)
+    target = negative_row.transpose(0, 3, 1, 2)
+    block = pair_blocks.transpose(0, 2, 1)
+    offset = pair_offsets.transpose(0, 1, 3, 2)
     v_state = vertex_state.reshape(rows // TILE, TILE)
     c_state = context_state.reshape(rows // TILE, TILE)
 
@@ -326,8 +354,9 @@
     turned = pltpu.VMEM((LANES, n), F32)
     terms = pltpu.VMEM((CAP, n, width), BF16)
 
-    flat_a, rows_a, pair_a = call(
-        first_kernel, "slots", [flat(CAP + 1), slots(CAP + 1), pair_rows], [], owner, target, pairs, vertex_table
+    flat_a, rows_a, pair_a, pairs = call(
+        first_kernel, "slots", [flat(CAP + 1), slots(CAP + 1), pair_rows, ((n_pairs, LANES), F32)], [],
+        owner, target, block, offset, vertex_table, mib=60,
     )
     context_table, pair_a, flat_a = lax.optimization_barrier((context_table, pair_a, flat_a))
     partner_0 = passed_along(context_table, shifts[0], n)

time: 149 us -> 131 us (0.88)
  Pallas kernels: 33.6 us -> 16.4 us
  local copies, waits for them, and re-layouts: 4.62 us -> 0.68 us
  waiting for transfers between devices: 35.2 us -> 38 us
  starting transfers between devices: 72.8 us -> 74.4 us
    pallas_call x5, Pallas kernels: 33.6 us -> 16.4 us  [call(): pl.pallas_call(kernel, name=name, out_shape=[jax.ShapeDtypeStruct(s, d) f...]
    unnamed x18 -> x14, local copies, waits for them, and re-layouts: 4.36 us -> 0.68 us
    all_to_all x3, waiting for transfers between devices: 3.3 us -> 6.37 us  [exchange(): lax.all_to_all(split, AXES, split_axis=0, concat_axis=0, tiled=True)]
    all_to_all x3, starting transfers between devices: 40.2 us -> 41.7 us  [exchange(): lax.all_to_all(split, AXES, split_axis=0, concat_axis=0, tiled=True)]
  transfers between devices with their start and end apart: 7 -> 7, of which waited for: 4 -> 4; matrix products, arithmetic and copies ran while one was open for 0% -> 0% of each run, Pallas kernels for 3% -> 2%
where the time goes in v2:
time: 131 us; the launch traced here: 130 us
  starting transfers between devices  74.4 us (57%)
  waiting for transfers between devices  38 us (29%)
  Pallas kernels  16.4 us (13%)
    all_to_all x3, starting transfers between devices, exchange(): lax.all_to_all(split, AXES, split_axis=0, concat_axis=0, tiled=True)  41.7 us
    ppermute x4, starting transfers between devices, passed_along(): lax.ppermute(block, AXES, [((i - distance) % n_devices, i) for i in range...  32.7 us
    ppermute x4, waiting for transfers between devices, passed_along(): lax.ppermute(block, AXES, [((i - distance) % n_devices, i) for i in range...  31.7 us
    pallas_call x5, Pallas kernels, call(): pl.pallas_call(kernel, name=name, out_shape=[jax.ShapeDtypeStruct(s, d) f...  16.4 us
    all_to_all x3, waiting for transfers between devices, exchange(): lax.all_to_all(split, AXES, split_axis=0, concat_axis=0, tiled=True)  6.37 us
  transfers between devices with their start and end apart: 7, of which 4 were waited for; matrix products, arithmetic and copies ran while one was open for 0% of the time, Pallas kernels for 2%

profile of v2, /device:TPU:1, one launch (start us, length us, event | category | flops | bytes accessed | tf_op | source)
XLA Modules:
  0.0 130.3 jit_solution(7655442709583741304)
XLA Ops:
  0.6 4.6 %slots.1 = (bf16[2048,128]{1,0:T(8,128)(2,1)}, bf16[4,512,128]{2,1,0:T(8,128)(2,1)}, bf16[144,128]{1,0:T(8,128)(2,1)}, f32[128,128]{1,0:T(8,128)}) custom-call(s32[2,5,8,16]{3,2,1,0:T(8,128)} %bitcast.20, s32[2,5,8,16]{3,2,1,0:T(8,128)} %bitcast.21, s32[2,2,8]{2,1,0:T(2,128)} %bitcast.23, s32[2,8,2,16]{3,2,1,0:T(2,128)} %bitcast.22, bf16[512,128]{1,0:T(8,128)(2,1)} %table_ref.4), custom_call_target="tpu_custom_call" | custom-call | flops 600000000 | bytes 4000000 | tf_op jit(solution)/shard_map/slots/pallas_call | solution.py:306
  5.2 0.0 copy-start.2
  5.2 0.0 copy-start.6
  5.2 22.2 %all-to-all-start = ((bf16[512,4,128]{2,1,0:T(4,128)(2,1)}), bf16[512,4,128]{2,1,0:T(4,128)(2,1)S(1)}, u32[]{:S(2)}, u32[]{:S(2)}) async-start(bf16[512,4,128]{2,1,0:T(4,128)(2,1)} %bitcast.19), calls=%async_computation | async-start | bytes 1048576 | tf_op jit(solution)/shard_map/all_to_all | solution.py:321
  27.4 0.0 copy-done.2
  27.4 0.0 copy-start.4
  27.4 4.8 %collective-permute-start.1 = (bf16[512,128]{1,0:T(8,128)(2,1)S(1)}, bf16[512,128]{1,0:T(8,128)(2,1)S(1)}, u32[]{:S(2)}, u32[]{:S(2)}) collective-permute-start(bf16[512,128]{1,0:T(8,128)(2,1)S(1)} %copy-done.2), channel_id=1, source_target_pairs={{507,0},{508,1},{509,2},{510,3},{511,4},{0,5},{1,6},{2,7},{3,8},{4... | collective-permute-start | bytes 393224 | tf_op jit(solution)/shard_map/ppermute | solution.py:325
  32.3 0.0 copy-done.6
  32.3 9.9 %collective-permute-start = (bf16[144,128]{1,0:T(8,128)(2,1)S(1)}, bf16[144,128]{1,0:T(8,128)(2,1)S(1)}, u32[]{:S(2)}, u32[]{:S(2)}) collective-permute-start(bf16[144,128]{1,0:T(8,128)(2,1)S(1)} %copy-done.6), channel_id=1, source_target_pairs={{5,0},{6,1},{7,2},{8,3},{9,4},{10,5},{11,6},{12,7},{13,8},{14,9},{... | collective-permute-start | bytes 110600 | tf_op jit(solution)/shard_map/ppermute | solution.py:325
  42.2 1.0 collective-permute-done.pair_ref
  43.3 6.5 %collective-permute-done.1.partner_ref = bf16[512,128]{1,0:T(8,128)(2,1)S(1)} collective-permute-done((bf16[512,128]{1,0:T(8,128)(2,1)S(1)}, bf16[512,128]{1,0:T(8,128)(2,1)S(1)}, u32[]{:S(2)}, u32[]{:S(2)}) %collective-permute-start.1) | collective-permute-done | bytes 131104 | tf_op jit(solution)/shard_map/ppermute | solution.py:325
  49.8 0.0 all-to-all-done
  49.8 0.0 copy-done.4
  49.8 4.2 %context_first.1 = (bf16[3072,128]{1,0:T(8,128)(2,1)}, bf16[512,128]{1,0:T(8,128)(2,1)S(1)}, bf16[512,128]{1,0:T(8,128)(2,1)S(1)}, f32[4,128]{1,0:T(4,128)S(1)}) custom-call(bf16[2048,128]{1,0:T(8,128)(2,1)S(1)} %bitcast.16, bf16[144,128]{1,0:T(8,128)(2,1)S(1)} %collective-permute-done.pair_ref, bf16[512,128]{1,0:T(8,128)(2,1)S(1)} %copy-done.2, ...), custom_call_target="tpu_custom_call" | custom-call | flops 600000000 | bytes 4000000 | tf_op jit(solution)/shard_map/context_first/pallas_call | solution.py:306
  54.0 0.0 copy-start
  54.0 0.0 copy-start.1
  54.0 0.0 copy-start.3
  54.0 10.4 %all-to-all-start.1 = ((bf16[512,3,2,128]{3,2,1,0:T(2,128)(2,1)}), bf16[512,3,2,128]{3,2,1,0:T(2,128)(2,1)S(1)}, u32[]{:S(2)}, u32[]{:S(2)}) async-start(bf16[512,3,2,128]{3,2,1,0:T(2,128)(2,1)} %bitcast.7), calls=%async_computation.1 | async-start | bytes 1572864 | tf_op jit(solution)/shard_map/all_to_all | solution.py:321
  64.5 4.8 %collective-permute-start.2 = (bf16[512,128]{1,0:T(8,128)(2,1)S(1)}, bf16[512,128]{1,0:T(8,128)(2,1)S(1)}, u32[]{:S(2)}, u32[]{:S(2)}) collective-permute-start(bf16[512,128]{1,0:T(8,128)(2,1)S(1)} %get-tuple-element.40.context_ref.table_ref), channel_id=1, source_target_pairs={{503,0},{504,1},{505,2},{506,3},{507,4},{508,5},{509,6},{510,7},{5... | collective-permute-start | bytes 393224 | tf_op jit(solution)/shard_map/ppermute | solution.py:325
  69.3 24.1 %collective-permute-done.2.partner_ref = bf16[512,128]{1,0:T(8,128)(2,1)S(1)} collective-permute-done((bf16[512,128]{1,0:T(8,128)(2,1)S(1)}, bf16[512,128]{1,0:T(8,128)(2,1)S(1)}, u32[]{:S(2)}, u32[]{:S(2)}) %collective-permute-start.2) | collective-permute-done | bytes 131104 | tf_op jit(solution)/shard_map/ppermute | solution.py:325
  93.4 0.0 all-to-all-done.1
  93.4 0.0 copy-done
  93.4 0.0 copy-done.1
  93.4 0.0 copy-done.3
  93.4 0.7 copy-done.5
  94.1 3.3 %vertex_first.1 = (bf16[2048,128]{1,0:T(8,128)(2,1)}, bf16[3,512,128]{2,1,0:T(8,128)(2,1)S(1)}, bf16[6,512,128]{2,1,0:T(8,128)(2,1)S(1)}, bf16[144,128]{1,0:T(8,...) custom-call(bf16[3072,128]{1,0:T(8,128)(2,1)S(1)} %bitcast.14, bf16[4,512,128]{2,1,0:T(8,128)(2,1)S(1)} %copy-done, ...), custom_call_target="tpu_custom_call" | custom-call | flops 600000000 | bytes 4000000 | tf_op jit(solution)/shard_map/vertex_first/pallas_call | solution.py:306
  97.4 9.1 %all-to-all-start.2 = ((bf16[512,4,128]{2,1,0:T(4,128)(2,1)}), bf16[512,4,128]{2,1,0:T(4,128)(2,1)S(1)}, u32[]{:S(2)}, u32[]{:S(2)}) async-start(bf16[512,4,128]{2,1,0:T(4,128)(2,1)} %bitcast.10), calls=%async_computation.2 | async-start | bytes 1048576 | tf_op jit(solution)/shard_map/all_to_all | solution.py:321
  106.4 13.1 %collective-permute-start.3 = (bf16[144,128]{1,0:T(8,128)(2,1)S(1)}, bf16[144,128]{1,0:T(8,128)(2,1)S(1)}, u32[]{:S(2)}, u32[]{:S(2)}) collective-permute-start(bf16[144,128]{1,0:T(8,128)(2,1)S(1)} %get-tuple-element.55), channel_id=1, source_target_pairs={{9,0},{10,1},{11,2},{12,3},{13,4},{14,5},{15,6},{16,7},{17,8},{18,... | collective-permute-start | bytes 110600 | tf_op jit(solution)/shard_map/ppermute | solution.py:325
  119.6 2.4 %vertex_last.1 = (bf16[512,128]{1,0:T(8,128)(2,1)}, f32[4,128]{1,0:T(4,128)}, bf16[3,512,128]{2,1,0:T(8,128)(2,1)S(1)}, f32[128,512]{1,0:T(8,128)S(1)}) custom-call(bf16[6,512,128]{2,1,0:T(8,128)(2,1)S(1)} %get-tuple-element.45.got_ref, bf16[3,512,128]{2,1,0:T(8,128)(2,1)S(1)} %get-tuple-element.46.rows_ref, bf16[4,512,128]{2,1,0:T(8,128)(2,1)S(1)} %copy-done, ...), custom_call_target="tpu_custom_call" | custom-call | flops 600000000 | bytes 4000000 | tf_op jit(solution)/shard_map/vertex_last/pallas_call | solution.py:306
  122.0 0.0 collective-permute-done.3.pair_ref
  122.0 6.4 %all-to-all-done.2 = bf16[512,4,128]{2,1,0:T(4,128)(2,1)S(1)} async-done(((bf16[512,4,128]{2,1,0:T(4,128)(2,1)}), bf16[512,4,128]{2,1,0:T(4,128)(2,1)S(1)}, u32[]{:S(2)}, u32[]{:S(2)}) %all-to-all-start.2) | async-done | bytes 524320 | tf_op jit(solution)/shard_map/all_to_all | solution.py:321
  128.4 1.9 %context_last.1 = (bf16[512,128]{1,0:T(8,128)(2,1)}, f32[4,128]{1,0:T(4,128)}) custom-call(bf16[2048,128]{1,0:T(8,128)(2,1)S(1)} %bitcast.15, bf16[3,512,128]{2,1,0:T(8,128)(2,1)S(1)} %get-tuple-element.53.rows_ref, f32[128,512]{1,0:T(8,128)S(1)} %get-tuple-element.54.turned_ref, bf16[144,128]{1,0:T(8,128)(2,1)S(1)} %collective-permute-done.3.pair_ref, ...), custom_call_target="tpu_custom_call" | custom-call | flops 600000000 | bytes 4000000 | tf_op jit(solution)/shard_map/context_last/pallas_call | solution.py:306
  (1 shorter events, 0.0 us)
Async XLA Ops:
  5.2 22.2 %copy-start.2 = (bf16[512,128]{1,0:T(8,128)(2,1)S(1)}, bf16[512,128]{1,0:T(8,128)(2,1)}, u32[]{:S(2)}) copy-start(bf16[512,128]{1,0:T(8,128)(2,1)} %table_ref.3) | copy-start | bytes 393220
  5.2 27.1 %copy-start.6 = (bf16[144,128]{1,0:T(8,128)(2,1)S(1)}, bf16[144,128]{1,0:T(8,128)(2,1)}, u32[]{:S(2)}) copy-start(bf16[144,128]{1,0:T(8,128)(2,1)} %get-tuple-element.35) | copy-start | bytes 110596
  5.2 44.6 %all-to-all-start = ((bf16[512,4,128]{2,1,0:T(4,128)(2,1)}), bf16[512,4,128]{2,1,0:T(4,128)(2,1)S(1)}, u32[]{:S(2)}, u32[]{:S(2)}) async-start(bf16[512,4,128]{2,1,0:T(4,128)(2,1)} %bitcast.19), calls=%async_computation | async-start | bytes 1048576 | tf_op jit(solution)/shard_map/all_to_all | solution.py:321
  27.4 22.4 %copy-start.4 = (f32[512]{0:T(512)S(1)}, f32[512]{0:T(512)}, u32[]{:S(2)}) copy-start(f32[512]{0:T(512)} %param.11) | copy-start | bytes 6148
  27.4 22.4 %collective-permute-start.1 = (bf16[512,128]{1,0:T(8,128)(2,1)S(1)}, bf16[512,128]{1,0:T(8,128)(2,1)S(1)}, u32[]{:S(2)}, u32[]{:S(2)}) collective-permute-start(bf16[512,128]{1,0:T(8,128)(2,1)S(1)} %copy-done.2), channel_id=1, source_target_pairs={{507,0},{508,1},{509,2},{510,3},{511,4},{0,5},{1,6},{2,7},{3,8},{4... | collective-permute-start | bytes 393224 | tf_op jit(solution)/shard_map/ppermute | solution.py:325
  32.3 11.0 %collective-permute-start = (bf16[144,128]{1,0:T(8,128)(2,1)S(1)}, bf16[144,128]{1,0:T(8,128)(2,1)S(1)}, u32[]{:S(2)}, u32[]{:S(2)}) collective-permute-start(bf16[144,128]{1,0:T(8,128)(2,1)S(1)} %copy-done.6), channel_id=1, source_target_pairs={{5,0},{6,1},{7,2},{8,3},{9,4},{10,5},{11,6},{12,7},{13,8},{14,9},{... | collective-permute-start | bytes 110600 | tf_op jit(solution)/shard_map/ppermute | solution.py:325
  54.0 39.4 %copy-start = (bf16[4,512,128]{2,1,0:T(8,128)(2,1)S(1)}, bf16[4,512,128]{2,1,0:T(8,128)(2,1)}, u32[]{:S(2)}) copy-start(bf16[4,512,128]{2,1,0:T(8,128)(2,1)} %get-tuple-element.42.sent_ref) | copy-start | bytes 1572868
  54.0 39.4 %copy-start.1 = (f32[128,128]{1,0:T(8,128)S(1)}, f32[128,128]{1,0:T(8,128)}, u32[]{:S(2)}) copy-start(f32[128,128]{1,0:T(8,128)} %get-tuple-element.43.pairs_ref) | copy-start | bytes 196612
  54.0 39.4 %copy-start.3 = (bf16[512,128]{1,0:T(8,128)(2,1)S(1)}, bf16[512,128]{1,0:T(8,128)(2,1)}, u32[]{:S(2)}) copy-start(bf16[512,128]{1,0:T(8,128)(2,1)} %table_ref.4) | copy-start | bytes 393220
  54.0 39.4 %all-to-all-start.1 = ((bf16[512,3,2,128]{3,2,1,0:T(2,128)(2,1)}), bf16[512,3,2,128]{3,2,1,0:T(2,128)(2,1)S(1)}, u32[]{:S(2)}, u32[]{:S(2)}) async-start(bf16[512,3,2,128]{3,2,1,0:T(2,128)(2,1)} %bitcast.7), calls=%async_computation.1 | async-start | bytes 1572864 | tf_op jit(solution)/shard_map/all_to_all | solution.py:321
  64.5 28.9 %collective-permute-start.2 = (bf16[512,128]{1,0:T(8,128)(2,1)S(1)}, bf16[512,128]{1,0:T(8,128)(2,1)S(1)}, u32[]{:S(2)}, u32[]{:S(2)}) collective-permute-start(bf16[512,128]{1,0:T(8,128)(2,1)S(1)} %get-tuple-element.40.context_ref.table_ref), channel_id=1, source_target_pairs={{503,0},{504,1},{505,2},{506,3},{507,4},{508,5},{509,6},{510,7},{5... | collective-permute-start | bytes 393224 | tf_op jit(solution)/shard_map/ppermute | solution.py:325
  93.4 0.7 copy-start.5
  97.4 31.0 %all-to-all-start.2 = ((bf16[512,4,128]{2,1,0:T(4,128)(2,1)}), bf16[512,4,128]{2,1,0:T(4,128)(2,1)S(1)}, u32[]{:S(2)}, u32[]{:S(2)}) async-start(bf16[512,4,128]{2,1,0:T(4,128)(2,1)} %bitcast.10), calls=%async_computation.2 | async-start | bytes 1048576 | tf_op jit(solution)/shard_map/all_to_all | solution.py:321
  106.4 15.6 %collective-permute-start.3 = (bf16[144,128]{1,0:T(8,128)(2,1)S(1)}, bf16[144,128]{1,0:T(8,128)(2,1)S(1)}, u32[]{:S(2)}, u32[]{:S(2)}) collective-permute-start(bf16[144,128]{1,0:T(8,128)(2,1)S(1)} %get-tuple-element.55), channel_id=1, source_target_pairs={{9,0},{10,1},{11,2},{12,3},{13,4},{14,5},{15,6},{16,7},{17,8},{18,... | collective-permute-start | bytes 110600 | tf_op jit(solution)/shard_map/ppermute | solution.py:325

commit v3 on v2

--- a/solution.py
+++ b/solution.py
@@ -43,12 +43,18 @@
     return jnp.sum(jnp.where(eye(), row, 0.0), axis=1, keepdims=True)
 
 
+def short(x):
+    return x.astype(jnp.int32).astype(jnp.int16)
+
+
 def one_hot_of_col(col, rows):
-    return ones_where(col == fiota((col.shape[0], rows), 1))
+    at = lax.broadcasted_iota(jnp.int16, (col.shape[0], rows), 1)
+    return jnp.where(short(col) == at, BF16(1), BF16(0))
 
 
 def one_hot_of_row(row, rows, first):
-    return ones_where(row == fiota((rows, row.shape[1]), 0) + first)
+    at = lax.broadcasted_iota(jnp.int16, (rows, row.shape[1]), 0)
+    return jnp.where(short(row - first) == at, BF16(1), BF16(0))
 
 
 def lane_of(episode, slot, part):
@@ -143,16 +149,16 @@
     blocks(table_ref.shape[0], TILE, step)
 
 
-def pairs_out(pairs_ref, episode, table_ref, out_ref):
-    n = pairs_ref.shape[0]
-    pairs = pairs_ref[:, 2 * episode : 2 * episode + 2]
-    rows = dot(one_hot_of_col(pairs[:, 0:1], table_ref.shape[0]), table_ref[...])
-    out_ref[0:n, :] = rows.astype(BF16)
-    high = jnp.floor(pairs[:, 1:2] * (1.0 / 256.0))
-    low = pairs[:, 1:2] - high * 256.0
+def numbers_of(pairs_ref, episode):
+    column = pairs_ref[0:LANES, 2 * episode + 1 : 2 * episode + 2]
+    high = jnp.floor(column * (1.0 / 256.0))
     which = iota((16, LANES), 0)
-    tail = jnp.where(which == 0, to_row(high), jnp.where(which == 1, to_row(low), 0.0))
-    out_ref[n : n + 16, :] = tail.astype(BF16)
+    low = column - high * 256.0
+    return jnp.where(which == 0, to_row(high), jnp.where(which == 1, to_row(low), 0.0)).astype(BF16)
+
+
+def rows_of(column, table_ref):
+    return dot(one_hot_of_col(column, table_ref.shape[0]), table_ref[...])
 
 
 def pair_terms_of(here, there):
@@ -175,9 +181,12 @@
     return [groups[i // 8][:, i % 8 : i % 8 + 1] for i in range(len(grids))]
 
 
-def first_kernel(owner_ref, row_ref, block_ref, offset_ref, table_ref, flat_ref, rows_ref, pair_ref, pairs_ref):
+def first_kernel(
+    owner_ref, row_ref, block_ref, offset_ref, table_ref, vertex_state_ref, context_state_ref,
+    flat_ref, rows_ref, pair_ref, pairs_ref, numbers_ref,
+):
     episodes, negatives = owner_ref.shape[:2]
-    pairs = pairs_ref.shape[0]
+    pairs = pair_ref.shape[0] - 16
     owners = rows_ref.shape[1]
     lane = iota((pairs, LANES), 1)
     part = lane % 4
@@ -194,7 +203,11 @@
             block = jnp.sum(jnp.where(here, which, 0.0), axis=1, keepdims=True)
             column = block * float(TILE) + columns[2 * episodes * negatives + 2 * e + w]
             wide = jnp.where(lane == 2 * e + w, column, wide)
-    pairs_ref[...] = wide
+    pairs_ref[0:pairs, :] = wide
+    pairs_ref[pairs : pairs + 16, :] = jnp.zeros((16, LANES), F32)
+    tiles = vertex_state_ref.shape[0]
+    pairs_ref[pairs : pairs + tiles, :] = vertex_state_ref[...]
+    pairs_ref[pairs + 8 : pairs + 8 + tiles, :] = context_state_ref[...]
     owner_rows, values = [], []
     for e in range(episodes):
         vertex = wide[:, 2 * e : 2 * e + 1] + 1.0
@@ -215,35 +228,33 @@
             values.append(jnp.where(mine, value, 0.0).astype(BF16))
             owner_rows.append(rows[k])
 
+    owner_row, value = jnp.concatenate(owner_rows, axis=1), jnp.concatenate(values, axis=0)
     for o in range(0, owners, TILE):
-        total = jnp.zeros((TILE, LANES), F32)
-        for row, value in zip(owner_rows, values):
-            total += dot(one_hot_of_row(row, TILE, float(o)), value)
+        total = dot(one_hot_of_row(owner_row, TILE, float(o)), value)
         rows_ref[CAP, o : o + TILE, :] = total.astype(BF16)
     gather_slots(table_ref, rows_ref.at[CAP], rows_ref, 0, 0, 2)
     by_owner(rows_ref, flat_ref, CAP + 1, CAP + 1)
-    pairs_out(pairs_ref, 0, table_ref, pair_ref)
-
-
-def context_side(pair_ref, table_ref):
-    n = pair_ref.shape[0] - 16
-    tail = pair_ref[n : n + 16, :].astype(F32)
-    row = tail[0:1, :] * 256.0 + tail[1:2, :]
-    mine = dot(one_hot_of_col(to_col(row), table_ref.shape[0]), table_ref[...])
-    return row, pair_terms_of(mine, pair_ref[0:n, :].astype(F32))
-
-
-def vertex_side(pairs_ref, episode, table_ref, partner_ref):
-    pairs = pairs_ref[:, 2 * episode : 2 * episode + 2]
-    mine = dot(one_hot_of_col(pairs[:, 0:1], table_ref.shape[0]), table_ref[...])
-    theirs = dot(one_hot_of_col(pairs[:, 1:2], partner_ref.shape[0]), partner_ref[...])
-    return to_row(pairs[:, 0:1]), pair_terms_of(mine, theirs)
+    pair_ref[0:pairs, :] = rows_of(wide[:, 0:1], table_ref).astype(BF16)
+    pair_ref[pairs : pairs + 16, :] = numbers_of(pairs_ref, 0)
+    numbers_ref[...] = numbers_of(pairs_ref, 1)
+
+
+def row_numbers(digits):
+    digits = digits.astype(F32)
+    return digits[0:1, :] * 256.0 + digits[1:2, :]
+
+
+def vertex_side(pairs_ref, episode, table_ref, theirs_ref):
+    column = pairs_ref[0:LANES, 2 * episode : 2 * episode + 1]
+    return to_row(column), pair_terms_of(rows_of(column, table_ref), theirs_ref[...].astype(F32))
 
 
 def context_first(
-    flat_ref, pair_ref, table_ref, state_ref,
-    send_ref, slots_ref, new_ref, new_state_ref, rows_ref, got_ref, turned_ref, terms_ref,
-):
+    flat_ref, pair_ref, numbers_ref, table_ref, pairs_ref,
+    send_ref, slots_ref, new_ref, new_state_ref, pair_0_ref, pair_1_ref,
+    rows_ref, got_ref, turned_ref, terms_ref,
+):
+    state_ref = pairs_ref.at[LANES + 8 : LANES + 16]
     by_slot(flat_ref, got_ref, CAP + 1, CAP + 1)
     slots_ref[...] = got_ref[CAP]
     turn(slots_ref, turned_ref)
@@ -253,18 +264,24 @@
         terms_ref[s, pl.ds(at, BLOCK), :] = (jax.nn.sigmoid(row_dot(mine, there)) * there).astype(BF16)
 
     gather_slots(table_ref, slots_ref, rows_ref, 0, 0, 0, weigh)
-    row, pair_terms = context_side(pair_ref, table_ref)
+    n = pair_ref.shape[0] - 16
+    row = row_numbers(pair_ref[n : n + 16, :])
+    mine = rows_of(to_col(row), table_ref)
+    pair_0_ref[...] = mine.astype(BF16)
+    pair_terms = pair_terms_of(mine, pair_ref[0:n, :].astype(F32))
     adagrad(
         table_ref, state_ref, new_ref, new_state_ref, turned_ref, terms_ref, lane_of(0, 0, 0), row, pair_terms
     )
+    pair_1_ref[...] = rows_of(to_col(row_numbers(numbers_ref[...])), new_ref).astype(BF16)
     gather_slots(new_ref, slots_ref, rows_ref, CAP, 1, 0)
     by_owner(rows_ref, send_ref, 2 * CAP, 2 * CAP)
 
 
 def vertex_first(
-    flat_ref, sent_ref, pairs_ref, partner_ref, table_ref, state_ref,
+    flat_ref, sent_ref, pairs_ref, partner_ref, table_ref,
     send_ref, rows_ref, got_ref, pair_ref, new_ref, new_state_ref, turned_ref, terms_ref,
 ):
+    state_ref = pairs_ref.at[LANES : LANES + 8]
     by_slot(flat_ref, got_ref, 2 * CAP, 2 * CAP)
     turn(sent_ref.at[CAP], turned_ref)
     weigh_slots(sent_ref, 0, got_ref, 0, terms_ref)
@@ -274,7 +291,7 @@
     )
     gather_slots(new_ref, sent_ref.at[CAP], rows_ref, 0, 1, 2)
     by_owner(rows_ref, send_ref, CAP, CAP + 1)
-    pairs_out(pairs_ref, 1, new_ref, pair_ref)
+    pair_ref[...] = rows_of(pairs_ref[0:LANES, 2:3], new_ref).astype(BF16)
 
 
 def vertex_last(
@@ -292,11 +309,13 @@
 
 
 def context_last(
-    flat_ref, rows_ref, turned_ref, pair_ref, table_ref, state_ref, new_ref, new_state_ref, got_ref, terms_ref
+    flat_ref, rows_ref, turned_ref, pair_ref, numbers_ref, mine_ref, table_ref, state_ref,
+    new_ref, new_state_ref, got_ref, terms_ref,
 ):
     by_slot(flat_ref, got_ref, CAP, CAP + 1)
     weigh_slots(rows_ref, 0, got_ref, 0, terms_ref)
-    row, pair_terms = context_side(pair_ref, table_ref)
+    row = row_numbers(numbers_ref[...])
+    pair_terms = pair_terms_of(mine_ref[...].astype(F32), pair_ref[...].astype(F32))
     adagrad(
         table_ref, state_ref, new_ref, new_state_ref, turned_ref, terms_ref, lane_of(1, 0, 0), row, pair_terms
     )
@@ -343,7 +362,6 @@
 
     table = ((rows, width), BF16)
     state = ((rows // TILE, TILE), F32)
-    pair_rows = ((n_pairs + 16, width), BF16)
 
     def flat(slots):
         return ((n * slots, width), BF16)
@@ -354,37 +372,40 @@
     turned = pltpu.VMEM((LANES, n), F32)
     terms = pltpu.VMEM((CAP, n, width), BF16)
 
-    flat_a, rows_a, pair_a, pairs = call(
-        first_kernel, "slots", [flat(CAP + 1), slots(CAP + 1), pair_rows, ((n_pairs, LANES), F32)], [],
-        owner, target, block, offset, vertex_table, mib=60,
-    )
-    context_table, pair_a, flat_a = lax.optimization_barrier((context_table, pair_a, flat_a))
-    partner_0 = passed_along(context_table, shifts[0], n)
+    pair_rows = ((n_pairs, width), BF16)
+    assert n_pairs == LANES
+    flat_a, rows_a, pair_a, pairs, numbers = call(
+        first_kernel, "slots",
+        [flat(CAP + 1), slots(CAP + 1), ((n_pairs + 16, width), BF16), ((n_pairs + 16, LANES), F32), ((16, LANES), BF16)],
+        [], owner, target, block, offset, vertex_table, v_state, c_state, mib=60,
+    )
     got_pair_a = passed_along(pair_a, n - shifts[0], n)
+    got_numbers = passed_along(numbers, n - shifts[1], n)
     got_a = exchange(flat_a, n)
-    got_a, got_pair_a, partner_0 = lax.optimization_barrier((got_a, got_pair_a, partner_0))
-    flat_b, slots_b, context_1, c_state_1 = call(
-        context_first, "context_first", [flat(2 * CAP), ((n, LANES), BF16), table, state],
+    flat_b, slots_b, context_1, c_state_1, pair_b0, pair_b1 = call(
+        context_first, "context_first",
+        [flat(2 * CAP), ((n, LANES), BF16), table, state, pair_rows, pair_rows],
         [pltpu.VMEM((2 * CAP, n, width), BF16), pltpu.VMEM((CAP + 1, n, width), BF16), turned, terms],
-        got_a, got_pair_a, context_table, c_state,
-    )
-    partner_1 = passed_along(context_1, shifts[1], n)
+        got_a, got_pair_a, got_numbers, context_table, pairs,
+    )
+    theirs_0 = passed_along(pair_b0, shifts[0], n)
+    theirs_1 = passed_along(pair_b1, shifts[1], n)
     got_b = exchange(flat_b, n)
-    got_b, partner_1 = lax.optimization_barrier((got_b, partner_1))
+    got_b, theirs_0, theirs_1 = lax.optimization_barrier((got_b, theirs_0, theirs_1))
     flat_c, rows_c, rows_got_b, pair_c, vertex_1, v_state_1 = call(
         vertex_first, "vertex_first", [flat(CAP + 1), slots(CAP), slots(2 * CAP), pair_rows, table, state],
         [turned, terms],
-        got_b, rows_a, pairs, partner_0, vertex_table, v_state,
+        got_b, rows_a, pairs, theirs_0, vertex_table,
     )
     got_pair_c = passed_along(pair_c, n - shifts[1], n)
     got_c = exchange(flat_c, n)
     vertex_2, v_state_2, rows_b, turned_b = call(
         vertex_last, "vertex_last", [table, state, slots(CAP), ((LANES, n), F32)], [turned, terms],
-        rows_got_b, rows_c, rows_a, pairs, partner_1, vertex_1, v_state_1, slots_b, context_1,
+        rows_got_b, rows_c, rows_a, pairs, theirs_1, vertex_1, v_state_1, slots_b, context_1,
     )
     context_2, c_state_2 = call(
         context_last, "context_last", [table, state], [pltpu.VMEM((CAP, n, width), BF16), terms],
-        got_c, rows_b, turned_b, got_pair_c, context_1, c_state_1,
+        got_c, rows_b, turned_b, got_pair_c, got_numbers, pair_b1, context_1, c_state_1,
     )
     return vertex_2, context_2, v_state_2.reshape(rows), c_state_2.reshape(rows)
 

time: 131 us -> 126 us (0.962)
  waiting for transfers between devices: 38 us -> 30.3 us
  starting transfers between devices: 74.4 us -> 79 us
    ppermute x4 -> x5, waiting for transfers between devices: 31.7 us -> 19.5 us  [passed_along(): lax.ppermute(block, AXES, [((i - distance) % n_devices, i) for i in range...]
    ppermute x4 -> x5, starting transfers between devices: 32.7 us -> 38.9 us  [passed_along(): lax.ppermute(block, AXES, [((i - distance) % n_devices, i) for i in range...]
    all_to_all x3, waiting for transfers between devices: 6.37 us -> 10.8 us  [exchange(): lax.all_to_all(split, AXES, split_axis=0, concat_axis=0, tiled=True)]
    all_to_all x3, starting transfers between devices: 41.7 us -> 40.1 us  [exchange(): lax.all_to_all(split, AXES, split_axis=0, concat_axis=0, tiled=True)]
  transfers between devices with their start and end apart: 7 -> 8, of which waited for: 4 -> 6; matrix products, arithmetic and copies ran while one was open for 0% -> 0% of each run, Pallas kernels for 2% -> 2%
where the time goes in v3:
time: 126 us
  starting transfers between devices  79 us (63%)
  waiting for transfers between devices  30.3 us (24%)
  Pallas kernels  16 us (13%)
    all_to_all x3, starting transfers between devices, exchange(): lax.all_to_all(split, AXES, split_axis=0, concat_axis=0, tiled=True)  40.1 us
    ppermute x5, starting transfers between devices, passed_along(): lax.ppermute(block, AXES, [((i - distance) % n_devices, i) for i in range...  38.9 us
    ppermute x5, waiting for transfers between devices, passed_along(): lax.ppermute(block, AXES, [((i - distance) % n_devices, i) for i in range...  19.5 us
    pallas_call x5, Pallas kernels, call(): pl.pallas_call(kernel, name=name, out_shape=[jax.ShapeDtypeStruct(s, d) f...  16 us
    all_to_all x3, waiting for transfers between devices, exchange(): lax.all_to_all(split, AXES, split_axis=0, concat_axis=0, tiled=True)  10.8 us
  transfers between devices with their start and end apart: 8, of which 6 were waited for; matrix products, arithmetic and copies ran while one was open for 0% of the time, Pallas kernels for 2%

profile of v3, /device:TPU:1, one launch (start us, length us, event | category | flops | bytes accessed | tf_op | source)
XLA Modules:
  0.0 126.0 jit_solution(5491813879623581923)
XLA Ops:
  0.6 4.6 %slots.1 = (bf16[2048,128]{1,0:T(8,128)(2,1)}, bf16[4,512,128]{2,1,0:T(8,128)(2,1)}, bf16[144,128]{1,0:T(8,128)(2,1)}, f32[144,128]{1,0:T(8,128)}, bf16[16,128]{1,0:T(8,128)(2,1)}) custom-call(s32[2,5,8,16]{3,2,1,0:T(8,128)} %bitcast.18, s32[2,5,8,16]{3,2,1,0:T(8,128)} %bitcast.19, s32[2,2,8]{2,1,0:T(2,128)} %bitcast.21, s32[2,8,2,16]{3,2,1,0:T(2,128)} %bitcast.20, ...), custom_call_target="tpu_custom_call" | custom-call | flops 600000000 | bytes 4000000 | tf_op jit(solution)/shard_map/slots/pallas_call | solution.py:325
  5.3 0.0 copy-start.5
  5.3 0.0 copy-start.6
  5.3 0.0 copy-start
  5.3 0.0 copy-start.3
  5.3 22.2 %all-to-all-start = ((bf16[512,4,128]{2,1,0:T(4,128)(2,1)}), bf16[512,4,128]{2,1,0:T(4,128)(2,1)S(1)}, u32[]{:S(2)}, u32[]{:S(2)}) async-start(bf16[512,4,128]{2,1,0:T(4,128)(2,1)} %bitcast.17), calls=%async_computation | async-start | bytes 1048576 | tf_op jit(solution)/shard_map/all_to_all | solution.py:340
  27.5 0.0 copy-done.5
  27.5 12.9 %collective-permute-start = (bf16[144,128]{1,0:T(8,128)(2,1)S(1)}, bf16[144,128]{1,0:T(8,128)(2,1)S(1)}, u32[]{:S(2)}, u32[]{:S(2)}) collective-permute-start(bf16[144,128]{1,0:T(8,128)(2,1)S(1)} %copy-done.5), channel_id=1, source_target_pairs={{5,0},{6,1},{7,2},{8,3},{9,4},{10,5},{11,6},{12,7},{13,8},{14,9},{... | collective-permute-start | bytes 110600 | tf_op jit(solution)/shard_map/ppermute | solution.py:344
  40.3 0.0 copy-done.6
  40.4 3.1 %collective-permute-start.1 = (bf16[16,128]{1,0:T(8,128)(2,1)S(1)}, bf16[16,128]{1,0:T(8,128)(2,1)S(1)}, u32[]{:S(2)}, u32[]{:S(2)}) collective-permute-start(bf16[16,128]{1,0:T(8,128)(2,1)S(1)} %copy-done.6), channel_id=1, source_target_pairs={{9,0},{10,1},{11,2},{12,3},{13,4},{14,5},{15,6},{16,7},{17,8},{18,... | collective-permute-start | bytes 12296 | tf_op jit(solution)/shard_map/ppermute | solution.py:344
  43.5 2.4 %collective-permute-done.1.numbers_ref = bf16[16,128]{1,0:T(8,128)(2,1)S(1)} collective-permute-done((bf16[16,128]{1,0:T(8,128)(2,1)S(1)}, bf16[16,128]{1,0:T(8,128)(2,1)S(1)}, u32[]{:S(2)}, u32[]{:S(2)}) %collective-permute-start.1) | collective-permute-done | bytes 4128 | tf_op jit(solution)/shard_map/ppermute | solution.py:344
  45.9 0.0 collective-permute-done.pair_ref
  45.9 3.5 %all-to-all-done = bf16[512,4,128]{2,1,0:T(4,128)(2,1)S(1)} async-done(((bf16[512,4,128]{2,1,0:T(4,128)(2,1)}), bf16[512,4,128]{2,1,0:T(4,128)(2,1)S(1)}, u32[]{:S(2)}, u32[]{:S(2)}) %all-to-all-start) | async-done | bytes 524320 | tf_op jit(solution)/shard_map/all_to_all | solution.py:340
  49.4 0.0 copy-done
  49.4 0.0 copy-done.3
  49.4 4.0 %context_first.1 = (bf16[3072,128]{1,0:T(8,128)(2,1)}, bf16[512,128]{1,0:T(8,128)(2,1)S(1)}, bf16[512,128]{1,0:T(8,128)(2,1)S(1)}, f32[4,128]{1,0:T(4,128)S(1)},...) custom-call(bf16[2048,128]{1,0:T(8,128)(2,1)S(1)} %bitcast.16, ...), custom_call_target="tpu_custom_call" | custom-call | flops 600000000 | bytes 4000000 | tf_op jit(solution)/shard_map/context_first/pallas_call | solution.py:325
  53.4 9.2 %all-to-all-start.1 = ((bf16[512,3,2,128]{3,2,1,0:T(2,128)(2,1)}), bf16[512,3,2,128]{3,2,1,0:T(2,128)(2,1)S(1)}, u32[]{:S(2)}, u32[]{:S(2)}) async-start(bf16[512,3,2,128]{3,2,1,0:T(2,128)(2,1)} %bitcast.8), calls=%async_computation.1 | async-start | bytes 1572864 | tf_op jit(solution)/shard_map/all_to_all | solution.py:340
  62.6 5.0 %collective-permute-start.2 = (bf16[128,128]{1,0:T(8,128)(2,1)S(1)}, bf16[128,128]{1,0:T(8,128)(2,1)S(1)}, u32[]{:S(2)}, u32[]{:S(2)}) collective-permute-start(bf16[128,128]{1,0:T(8,128)(2,1)S(1)} %get-tuple-element.35), channel_id=1, source_target_pairs={{507,0},{508,1},{509,2},{510,3},{511,4},{0,5},{1,6},{2,7},{3,8},{4... | collective-permute-start | bytes 98312 | tf_op jit(solution)/shard_map/ppermute | solution.py:344
  67.6 4.7 %collective-permute-start.3 = (bf16[128,128]{1,0:T(8,128)(2,1)S(1)}, bf16[128,128]{1,0:T(8,128)(2,1)S(1)}, u32[]{:S(2)}, u32[]{:S(2)}) collective-permute-start(bf16[128,128]{1,0:T(8,128)(2,1)S(1)} %get-tuple-element.36.mine_ref), channel_id=1, source_target_pairs={{503,0},{504,1},{505,2},{506,3},{507,4},{508,5},{509,6},{510,7},{5... | collective-permute-start | bytes 98312 | tf_op jit(solution)/shard_map/ppermute | solution.py:344
  72.3 15.0 %collective-permute-done.2.partner_ref = bf16[128,128]{1,0:T(8,128)(2,1)S(1)} collective-permute-done((bf16[128,128]{1,0:T(8,128)(2,1)S(1)}, bf16[128,128]{1,0:T(8,128)(2,1)S(1)}, u32[]{:S(2)}, u32[]{:S(2)}) %collective-permute-start.2) | collective-permute-done | bytes 32800 | tf_op jit(solution)/shard_map/ppermute | solution.py:344
  87.3 2.0 %collective-permute-done.3.partner_ref = bf16[128,128]{1,0:T(8,128)(2,1)S(1)} collective-permute-done((bf16[128,128]{1,0:T(8,128)(2,1)S(1)}, bf16[128,128]{1,0:T(8,128)(2,1)S(1)}, u32[]{:S(2)}, u32[]{:S(2)}) %collective-permute-start.3) | collective-permute-done | bytes 32800 | tf_op jit(solution)/shard_map/ppermute | solution.py:344
  89.3 0.8 all-to-all-done.1
  90.2 0.0 copy-done.1
  90.2 0.0 copy-done.2
  90.2 3.2 %vertex_first.1 = (bf16[2048,128]{1,0:T(8,128)(2,1)}, bf16[3,512,128]{2,1,0:T(8,128)(2,1)S(1)}, bf16[6,512,128]{2,1,0:T(8,128)(2,1)S(1)}, bf16[128,128]{1,0:T(8,...) custom-call(bf16[3072,128]{1,0:T(8,128)(2,1)S(1)} %bitcast.14, bf16[4,512,128]{2,1,0:T(8,128)(2,1)S(1)} %copy-done.2, ...), custom_call_target="tpu_custom_call" | custom-call | flops 600000000 | bytes 4000000 | tf_op jit(solution)/shard_map/vertex_first/pallas_call | solution.py:325
  93.4 8.8 %all-to-all-start.2 = ((bf16[512,4,128]{2,1,0:T(4,128)(2,1)}), bf16[512,4,128]{2,1,0:T(4,128)(2,1)S(1)}, u32[]{:S(2)}, u32[]{:S(2)}) async-start(bf16[512,4,128]{2,1,0:T(4,128)(2,1)} %bitcast.10), calls=%async_computation.2 | async-start | bytes 1048576 | tf_op jit(solution)/shard_map/all_to_all | solution.py:340
  102.2 13.2 %collective-permute-start.4 = (bf16[128,128]{1,0:T(8,128)(2,1)S(1)}, bf16[128,128]{1,0:T(8,128)(2,1)S(1)}, u32[]{:S(2)}, u32[]{:S(2)}) collective-permute-start(bf16[128,128]{1,0:T(8,128)(2,1)S(1)} %get-tuple-element.51), channel_id=1, source_target_pairs={{9,0},{10,1},{11,2},{12,3},{13,4},{14,5},{15,6},{16,7},{17,8},{18,... | collective-permute-start | bytes 98312 | tf_op jit(solution)/shard_map/ppermute | solution.py:344
  115.4 0.0 copy-done.4
  115.4 2.3 %vertex_last.1 = (bf16[512,128]{1,0:T(8,128)(2,1)}, f32[4,128]{1,0:T(4,128)}, bf16[3,512,128]{2,1,0:T(8,128)(2,1)S(1)}, f32[128,512]{1,0:T(8,128)S(1)}) custom-call(bf16[6,512,128]{2,1,0:T(8,128)(2,1)S(1)} %get-tuple-element.40.got_ref, bf16[3,512,128]{2,1,0:T(8,128)(2,1)S(1)} %get-tuple-element.41.rows_ref, bf16[4,512,128]{2,1,0:T(8,128)(2,1)S(1)} %copy-done.2, ...), custom_call_target="tpu_custom_call" | custom-call | flops 600000000 | bytes 4000000 | tf_op jit(solution)/shard_map/vertex_last/pallas_call | solution.py:325
  117.7 0.0 collective-permute-done.4.pair_ref
  117.7 6.5 %all-to-all-done.2 = bf16[512,4,128]{2,1,0:T(4,128)(2,1)S(1)} async-done(((bf16[512,4,128]{2,1,0:T(4,128)(2,1)}), bf16[512,4,128]{2,1,0:T(4,128)(2,1)S(1)}, u32[]{:S(2)}, u32[]{:S(2)}) %all-to-all-start.2) | async-done | bytes 524320 | tf_op jit(solution)/shard_map/all_to_all | solution.py:340
  124.2 1.8 %context_last.1 = (bf16[512,128]{1,0:T(8,128)(2,1)}, f32[4,128]{1,0:T(4,128)}) custom-call(bf16[2048,128]{1,0:T(8,128)(2,1)S(1)} %bitcast.15, bf16[3,512,128]{2,1,0:T(8,128)(2,1)S(1)} %get-tuple-element.49.rows_ref, f32[128,512]{1,0:T(8,128)S(1)} %get-tuple-element.50.turned_ref, bf16[128,128]{1,0:T(8,128)(2,1)S(1)} %collective-permute-done.4.pair_ref, ...), custom_call_target="tpu_custom_call" | custom-call | flops 600000000 | bytes 4000000 | tf_op jit(solution)/shard_map/context_last/pallas_call | solution.py:325
  (3 shorter events, 0.0 us)
Async XLA Ops:
  5.3 22.2 %copy-start.5 = (bf16[144,128]{1,0:T(8,128)(2,1)S(1)}, bf16[144,128]{1,0:T(8,128)(2,1)}, u32[]{:S(2)}) copy-start(bf16[144,128]{1,0:T(8,128)(2,1)} %get-tuple-element.31) | copy-start | bytes 110596
  5.3 35.1 %copy-start.6 = (bf16[16,128]{1,0:T(8,128)(2,1)S(1)}, bf16[16,128]{1,0:T(8,128)(2,1)}, u32[]{:S(2)}) copy-start(bf16[16,128]{1,0:T(8,128)(2,1)} %get-tuple-element.32) | copy-start | bytes 12292
  5.3 44.1 %copy-start = (bf16[512,128]{1,0:T(8,128)(2,1)S(1)}, bf16[512,128]{1,0:T(8,128)(2,1)}, u32[]{:S(2)}) copy-start(bf16[512,128]{1,0:T(8,128)(2,1)} %table_ref.4) | copy-start | bytes 393220
  5.3 44.1 %copy-start.3 = (f32[144,128]{1,0:T(8,128)S(1)}, f32[144,128]{1,0:T(8,128)}, u32[]{:S(2)}) copy-start(f32[144,128]{1,0:T(8,128)} %get-tuple-element.33.pairs_ref) | copy-start | bytes 221188
  5.3 44.1 %all-to-all-start = ((bf16[512,4,128]{2,1,0:T(4,128)(2,1)}), bf16[512,4,128]{2,1,0:T(4,128)(2,1)S(1)}, u32[]{:S(2)}, u32[]{:S(2)}) async-start(bf16[512,4,128]{2,1,0:T(4,128)(2,1)} %bitcast.17), calls=%async_computation | async-start | bytes 1048576 | tf_op jit(solution)/shard_map/all_to_all | solution.py:340
  27.5 18.4 %collective-permute-start = (bf16[144,128]{1,0:T(8,128)(2,1)S(1)}, bf16[144,128]{1,0:T(8,128)(2,1)S(1)}, u32[]{:S(2)}, u32[]{:S(2)}) collective-permute-start(bf16[144,128]{1,0:T(8,128)(2,1)S(1)} %copy-done.5), channel_id=1, source_target_pairs={{5,0},{6,1},{7,2},{8,3},{9,4},{10,5},{11,6},{12,7},{13,8},{14,9},{... | collective-permute-start | bytes 110600 | tf_op jit(solution)/shard_map/ppermute | solution.py:344
  40.4 5.6 %collective-permute-start.1 = (bf16[16,128]{1,0:T(8,128)(2,1)S(1)}, bf16[16,128]{1,0:T(8,128)(2,1)S(1)}, u32[]{:S(2)}, u32[]{:S(2)}) collective-permute-start(bf16[16,128]{1,0:T(8,128)(2,1)S(1)} %copy-done.6), channel_id=1, source_target_pairs={{9,0},{10,1},{11,2},{12,3},{13,4},{14,5},{15,6},{16,7},{17,8},{18,... | collective-permute-start | bytes 12296 | tf_op jit(solution)/shard_map/ppermute | solution.py:344
  53.4 36.8 %copy-start.1 = (bf16[512,128]{1,0:T(8,128)(2,1)S(1)}, bf16[512,128]{1,0:T(8,128)(2,1)}, u32[]{:S(2)}) copy-start(bf16[512,128]{1,0:T(8,128)(2,1)} %table_ref.5) | copy-start | bytes 393220
  53.4 36.8 %copy-start.2 = (bf16[4,512,128]{2,1,0:T(8,128)(2,1)S(1)}, bf16[4,512,128]{2,1,0:T(8,128)(2,1)}, u32[]{:S(2)}) copy-start(bf16[4,512,128]{2,1,0:T(8,128)(2,1)} %get-tuple-element.38.sent_ref) | copy-start | bytes 1572868
  53.4 36.8 %all-to-all-start.1 = ((bf16[512,3,2,128]{3,2,1,0:T(2,128)(2,1)}), bf16[512,3,2,128]{3,2,1,0:T(2,128)(2,1)S(1)}, u32[]{:S(2)}, u32[]{:S(2)}) async-start(bf16[512,3,2,128]{3,2,1,0:T(2,128)(2,1)} %bitcast.8), calls=%async_computation.1 | async-start | bytes 1572864 | tf_op jit(solution)/shard_map/all_to_all | solution.py:340
  62.6 24.8 %collective-permute-start.2 = (bf16[128,128]{1,0:T(8,128)(2,1)S(1)}, bf16[128,128]{1,0:T(8,128)(2,1)S(1)}, u32[]{:S(2)}, u32[]{:S(2)}) collective-permute-start(bf16[128,128]{1,0:T(8,128)(2,1)S(1)} %get-tuple-element.35), channel_id=1, source_target_pairs={{507,0},{508,1},{509,2},{510,3},{511,4},{0,5},{1,6},{2,7},{3,8},{4... | collective-permute-start | bytes 98312 | tf_op jit(solution)/shard_map/ppermute | solution.py:344
  67.6 21.8 %collective-permute-start.3 = (bf16[128,128]{1,0:T(8,128)(2,1)S(1)}, bf16[128,128]{1,0:T(8,128)(2,1)S(1)}, u32[]{:S(2)}, u32[]{:S(2)}) collective-permute-start(bf16[128,128]{1,0:T(8,128)(2,1)S(1)} %get-tuple-element.36.mine_ref), channel_id=1, source_target_pairs={{503,0},{504,1},{505,2},{506,3},{507,4},{508,5},{509,6},{510,7},{5... | collective-permute-start | bytes 98312 | tf_op jit(solution)/shard_map/ppermute | solution.py:344
  93.4 22.0 %copy-start.4 = (f32[144,128]{1,0:T(8,128)S(1)}, f32[144,128]{1,0:T(8,128)}, u32[]{:S(2)}) copy-start(f32[144,128]{1,0:T(8,128)} %get-tuple-element.33.pairs_ref) | copy-start | bytes 221188
  93.4 30.8 %all-to-all-start.2 = ((bf16[512,4,128]{2,1,0:T(4,128)(2,1)}), bf16[512,4,128]{2,1,0:T(4,128)(2,1)S(1)}, u32[]{:S(2)}, u32[]{:S(2)}) async-start(bf16[512,4,128]{2,1,0:T(4,128)(2,1)} %bitcast.10), calls=%async_computation.2 | async-start | bytes 1048576 | tf_op jit(solution)/shard_map/all_to_all | solution.py:340
  102.2 15.5 %collective-permute-start.4 = (bf16[128,128]{1,0:T(8,128)(2,1)S(1)}, bf16[128,128]{1,0:T(8,128)(2,1)S(1)}, u32[]{:S(2)}, u32[]{:S(2)}) collective-permute-start(bf16[128,128]{1,0:T(8,128)(2,1)S(1)} %get-tuple-element.51), channel_id=1, source_target_pairs={{9,0},{10,1},{11,2},{12,3},{13,4},{14,5},{15,6},{16,7},{17,8},{18,... | collective-permute-start | bytes 98312 | tf_op jit(solution)/shard_map/ppermute | solution.py:344

commit v4 on v3

--- a/solution.py
+++ b/solution.py
@@ -8,7 +8,6 @@
 AXES = ("dom", "type")
 TILE = 128
 CAP = 3
-PART = 64
 BLOCK = 128
 LANES = 128
 F32 = jnp.float32
@@ -78,27 +77,33 @@
         step(b * size, b)
 
 
+def part_of(group):
+    return 64 if group <= 4 else 32
+
+
 def by_owner(slots_ref, flat_ref, slots, group):
-    j = iota((group * PART, slots * PART), 1)
-    move = ones_where(iota((group * PART, slots * PART), 0) == (j % PART) * group + j // PART)
-
-    def step(at, b):
-        rows = jnp.concatenate([slots_ref[s, pl.ds(at, PART), :] for s in range(slots)], axis=0)
-        flat_ref[pl.ds(at * group, group * PART), :] = dot(move, rows).astype(BF16)
-
-    blocks(slots_ref.shape[1], PART, step)
-
-
-def by_slot(flat_ref, slots_ref, slots, group):
-    i = iota((slots * PART, group * PART), 0)
-    move = ones_where(iota((slots * PART, group * PART), 1) == (i % PART) * group + i // PART)
-
-    def step(at, b):
-        rows = dot(move, flat_ref[pl.ds(at * group, group * PART), :]).astype(BF16)
+    part = part_of(group)
+    j = iota((group * part, slots * part), 1)
+    move = ones_where(iota((group * part, slots * part), 0) == (j % part) * group + j // part)
+
+    def step(at, b):
+        rows = jnp.concatenate([slots_ref[s, pl.ds(at, part), :] for s in range(slots)], axis=0)
+        flat_ref[pl.ds(at * group, group * part), :] = dot(move, rows).astype(BF16)
+
+    blocks(slots_ref.shape[1], part, step)
+
+
+def by_slot(flat_ref, slots_ref, first, slots, group):
+    part = part_of(group)
+    i = iota((slots * part, group * part), 0)
+    move = ones_where(iota((slots * part, group * part), 1) == (i % part) * group + i // part + first)
+
+    def step(at, b):
+        rows = dot(move, flat_ref[pl.ds(at * group, group * part), :]).astype(BF16)
         for s in range(slots):
-            slots_ref[s, pl.ds(at, PART), :] = rows[s * PART : (s + 1) * PART, :]
-
-    blocks(slots_ref.shape[1], PART, step)
+            slots_ref[s, pl.ds(at, part), :] = rows[s * part : (s + 1) * part, :]
+
+    blocks(slots_ref.shape[1], part, step)
 
 
 def turn(table_ref, turned_ref):
@@ -129,17 +134,22 @@
     blocks(out_ref.shape[1], BLOCK, step)
 
 
-def adagrad(
-    table_ref, state_ref, new_ref, new_state_ref, turned_ref, terms_ref, lane0, pair_row, pair_terms
-):
+def scattered(turned_ref, terms_ref, lane0):
+    index = [slot_row(turned_ref, lane0 + 4 * s) for s in range(CAP)]
+
+    def grad_of(at, grad):
+        for s in range(CAP):
+            grad += dot(one_hot_of_row(index[s], TILE, float(at)), terms_ref[s])
+        return grad
+
+    return grad_of
+
+
+def adagrad(table_ref, state_ref, new_ref, new_state_ref, grad_of, pair_row, pair_terms):
     width = table_ref.shape[1]
-    index = [slot_row(turned_ref, lane0 + 4 * s) for s in range(CAP)]
-
-    def step(at, b):
-        first = jnp.asarray(at).astype(F32)
-        grad = dot(one_hot_of_row(pair_row, TILE, first), pair_terms)
-        for s in range(CAP):
-            grad += dot(one_hot_of_row(index[s], TILE, first), terms_ref[s])
+
+    def step(at, b):
+        grad = grad_of(at, dot(one_hot_of_row(pair_row, TILE, float(at)), pair_terms))
         state = jnp.transpose(jnp.broadcast_to(state_ref[pl.ds(b, 1), :], (TILE, TILE)))
         state = state + row_dot(grad, grad) * (1.0 / width)
         rows = table_ref[pl.ds(at, TILE), :].astype(F32) - 0.5 * grad / jnp.sqrt(state)
@@ -255,7 +265,7 @@
     rows_ref, got_ref, turned_ref, terms_ref,
 ):
     state_ref = pairs_ref.at[LANES + 8 : LANES + 16]
-    by_slot(flat_ref, got_ref, CAP + 1, CAP + 1)
+    by_slot(flat_ref, got_ref, 0, CAP + 1, CAP + 1)
     slots_ref[...] = got_ref[CAP]
     turn(slots_ref, turned_ref)
 
@@ -269,9 +279,8 @@
     mine = rows_of(to_col(row), table_ref)
     pair_0_ref[...] = mine.astype(BF16)
     pair_terms = pair_terms_of(mine, pair_ref[0:n, :].astype(F32))
-    adagrad(
-        table_ref, state_ref, new_ref, new_state_ref, turned_ref, terms_ref, lane_of(0, 0, 0), row, pair_terms
-    )
+    grad_of = scattered(turned_ref, terms_ref, lane_of(0, 0, 0))
+    adagrad(table_ref, state_ref, new_ref, new_state_ref, grad_of, row, pair_terms)
     pair_1_ref[...] = rows_of(to_col(row_numbers(numbers_ref[...])), new_ref).astype(BF16)
     gather_slots(new_ref, slots_ref, rows_ref, CAP, 1, 0)
     by_owner(rows_ref, send_ref, 2 * CAP, 2 * CAP)
@@ -279,46 +288,72 @@
 
 def vertex_first(
     flat_ref, sent_ref, pairs_ref, partner_ref, table_ref,
-    send_ref, rows_ref, got_ref, pair_ref, new_ref, new_state_ref, turned_ref, terms_ref,
+    send_ref, pair_ref, new_ref, new_state_ref, turned_ref, rows_ref, got_ref, terms_ref,
 ):
     state_ref = pairs_ref.at[LANES : LANES + 8]
-    by_slot(flat_ref, got_ref, 2 * CAP, 2 * CAP)
+    by_slot(flat_ref, got_ref, 0, CAP, 2 * CAP)
     turn(sent_ref.at[CAP], turned_ref)
     weigh_slots(sent_ref, 0, got_ref, 0, terms_ref)
     row, pair_terms = vertex_side(pairs_ref, 0, table_ref, partner_ref)
-    adagrad(
-        table_ref, state_ref, new_ref, new_state_ref, turned_ref, terms_ref, lane_of(0, 0, 2), row, pair_terms
-    )
+    grad_of = scattered(turned_ref, terms_ref, lane_of(0, 0, 2))
+    adagrad(table_ref, state_ref, new_ref, new_state_ref, grad_of, row, pair_terms)
     gather_slots(new_ref, sent_ref.at[CAP], rows_ref, 0, 1, 2)
     by_owner(rows_ref, send_ref, CAP, CAP + 1)
     pair_ref[...] = rows_of(pairs_ref[0:LANES, 2:3], new_ref).astype(BF16)
 
 
 def vertex_last(
-    got_ref, rows_ref, sent_ref, pairs_ref, partner_ref, table_ref, state_ref, slots_ref, context_ref,
-    new_ref, new_state_ref, context_rows_ref, context_turned_ref, turned_ref, terms_ref,
-):
-    gather_slots(context_ref, slots_ref, context_rows_ref, 0, 1, 0)
+    flat_ref, sent_ref, pairs_ref, partner_ref, table_ref, state_ref, slots_ref, context_ref,
+    new_ref, new_state_ref, context_flat_ref, place_ref,
+    got_ref, rows_ref, context_turned_ref, turned_ref, terms_ref,
+):
+    gather_slots(context_ref, slots_ref, rows_ref, 0, 1, 0)
+    by_owner(rows_ref, context_flat_ref, CAP, CAP + 1)
     turn(slots_ref, context_turned_ref)
+    group = CAP + 1
+    part = part_of(group)
+    i = iota((CAP * part, group * part), 0)
+    move = ones_where(iota((CAP * part, group * part), 1) == (i % part) * group + i // part)
+    lanes = [lane_of(1, s, 0) for s in range(CAP)]
+
+    def step(at, b):
+        digits = [
+            jnp.concatenate([context_turned_ref[k + d : k + d + 1, at : at + part] for k in lanes], axis=1)
+            for d in range(2)
+        ]
+        which = iota((16, CAP * part), 0)
+        both = jnp.where(which == 0, digits[0], jnp.where(which == 1, digits[1], 0.0)).astype(BF16)
+        moved = dot(both, move)
+        place_ref[:, at * group : (at + part) * group] = moved[0:1, :] * 256.0 + moved[1:2, :] - 1.0
+
+    blocks(slots_ref.shape[0], part, step)
+
     turn(sent_ref.at[CAP], turned_ref)
-    weigh_slots(rows_ref, 0, got_ref, CAP, terms_ref)
+    by_slot(flat_ref, got_ref, CAP, CAP, 2 * CAP)
+    gather_slots(table_ref, sent_ref.at[CAP], rows_ref, 0, 1, 2)
+    weigh_slots(rows_ref, 0, got_ref, 0, terms_ref)
     row, pair_terms = vertex_side(pairs_ref, 1, table_ref, partner_ref)
-    adagrad(
-        table_ref, state_ref, new_ref, new_state_ref, turned_ref, terms_ref, lane_of(1, 0, 2), row, pair_terms
-    )
+    grad_of = scattered(turned_ref, terms_ref, lane_of(1, 0, 2))
+    adagrad(table_ref, state_ref, new_ref, new_state_ref, grad_of, row, pair_terms)
 
 
 def context_last(
-    flat_ref, rows_ref, turned_ref, pair_ref, numbers_ref, mine_ref, table_ref, state_ref,
-    new_ref, new_state_ref, got_ref, terms_ref,
-):
-    by_slot(flat_ref, got_ref, CAP, CAP + 1)
-    weigh_slots(rows_ref, 0, got_ref, 0, terms_ref)
+    flat_ref, rows_ref, place_ref, pair_ref, numbers_ref, mine_ref, table_ref, state_ref,
+    new_ref, new_state_ref, terms_ref,
+):
+    def weigh(at, b):
+        there = flat_ref[pl.ds(at, BLOCK), :].astype(F32)
+        weight = jax.nn.sigmoid(row_dot(rows_ref[pl.ds(at, BLOCK), :].astype(F32), there))
+        terms_ref[pl.ds(at, BLOCK), :] = (weight * there).astype(BF16)
+
+    blocks(flat_ref.shape[0], BLOCK, weigh)
     row = row_numbers(numbers_ref[...])
     pair_terms = pair_terms_of(mine_ref[...].astype(F32), pair_ref[...].astype(F32))
-    adagrad(
-        table_ref, state_ref, new_ref, new_state_ref, turned_ref, terms_ref, lane_of(1, 0, 0), row, pair_terms
-    )
+
+    def grad_of(at, grad):
+        return grad + dot(one_hot_of_row(place_ref[...], TILE, float(at)), terms_ref[...])
+
+    adagrad(table_ref, state_ref, new_ref, new_state_ref, grad_of, row, pair_terms)
 
 
 def call(kernel, name, outs, scratch, *args, mib=24):
@@ -392,20 +427,20 @@
     theirs_1 = passed_along(pair_b1, shifts[1], n)
     got_b = exchange(flat_b, n)
     got_b, theirs_0, theirs_1 = lax.optimization_barrier((got_b, theirs_0, theirs_1))
-    flat_c, rows_c, rows_got_b, pair_c, vertex_1, v_state_1 = call(
-        vertex_first, "vertex_first", [flat(CAP + 1), slots(CAP), slots(2 * CAP), pair_rows, table, state],
-        [turned, terms],
+    flat_c, pair_c, vertex_1, v_state_1 = call(
+        vertex_first, "vertex_first", [flat(CAP + 1), pair_rows, table, state], [turned, terms, terms, terms],
         got_b, rows_a, pairs, theirs_0, vertex_table,
     )
     got_pair_c = passed_along(pair_c, n - shifts[1], n)
     got_c = exchange(flat_c, n)
-    vertex_2, v_state_2, rows_b, turned_b = call(
-        vertex_last, "vertex_last", [table, state, slots(CAP), ((LANES, n), F32)], [turned, terms],
-        rows_got_b, rows_c, rows_a, pairs, theirs_1, vertex_1, v_state_1, slots_b, context_1,
+    vertex_2, v_state_2, rows_b, place_b = call(
+        vertex_last, "vertex_last", [table, state, flat(CAP + 1), ((1, n * (CAP + 1)), F32)],
+        [terms, terms, turned, turned, terms],
+        got_b, rows_a, pairs, theirs_1, vertex_1, v_state_1, slots_b, context_1,
     )
     context_2, c_state_2 = call(
-        context_last, "context_last", [table, state], [pltpu.VMEM((CAP, n, width), BF16), terms],
-        got_c, rows_b, turned_b, got_pair_c, got_numbers, pair_b1, context_1, c_state_1,
+        context_last, "context_last", [table, state], [pltpu.VMEM((n * (CAP + 1), width), BF16)],
+        got_c, rows_b, place_b, got_pair_c, got_numbers, pair_b1, context_1, c_state_1,
     )
     return vertex_2, context_2, v_state_2.reshape(rows), c_state_2.reshape(rows)
 

time: 126 us -> 126 us (level)
  transfers between devices with their start and end apart: 8 -> 8, of which waited for: 6 -> 6; matrix products, arithmetic and copies ran while one was open for 0% -> 0% of each run, Pallas kernels for 2% -> 3%
where the time goes in v4:
time: 126 us
  starting transfers between devices  79 us (63%)
  waiting for transfers between devices  29.4 us (23%)
  Pallas kernels  16.5 us (13%)
    all_to_all x3, starting transfers between devices, exchange(): lax.all_to_all(split, AXES, split_axis=0, concat_axis=0, tiled=True)  40.2 us
    ppermute x5, starting transfers between devices, passed_along(): lax.ppermute(block, AXES, [((i - distance) % n_devices, i) for i in range...  38.8 us
    ppermute x5, waiting for transfers between devices, passed_along(): lax.ppermute(block, AXES, [((i - distance) % n_devices, i) for i in range...  19.5 us
    pallas_call x5, Pallas kernels, call(): pl.pallas_call(kernel, name=name, out_shape=[jax.ShapeDtypeStruct(s, d) f...  16.5 us
    all_to_all x3, waiting for transfers between devices, exchange(): lax.all_to_all(split, AXES, split_axis=0, concat_axis=0, tiled=True)  9.95 us
  transfers between devices with their start and end apart: 8, of which 6 were waited for; matrix products, arithmetic and copies ran while one was open for 0% of the time, Pallas kernels for 3%

profile of v4, /device:TPU:1, one launch (start us, length us, event | category | flops | bytes accessed | tf_op | source)
XLA Modules:
  0.0 125.7 jit_solution(10796457421230075625)
XLA Ops:
  0.6 4.6 %slots.1 = (bf16[2048,128]{1,0:T(8,128)(2,1)}, bf16[4,512,128]{2,1,0:T(8,128)(2,1)}, bf16[144,128]{1,0:T(8,128)(2,1)}, f32[144,128]{1,0:T(8,128)}, bf16[16,128]{1,0:T(8,128)(2,1)}) custom-call(s32[2,5,8,16]{3,2,1,0:T(8,128)} %bitcast.19, s32[2,5,8,16]{3,2,1,0:T(8,128)} %bitcast.20, s32[2,2,8]{2,1,0:T(2,128)} %bitcast.22, s32[2,8,2,16]{3,2,1,0:T(2,128)} %bitcast.21, ...), custom_call_target="tpu_custom_call" | custom-call | flops 600000000 | bytes 4000000 | tf_op jit(solution)/shard_map/slots/pallas_call | solution.py:360
  5.3 0.0 copy-start.4
  5.3 0.0 copy-start.5
  5.3 0.0 copy-start
  5.3 0.0 copy-start.3
  5.3 22.2 %all-to-all-start = ((bf16[512,4,128]{2,1,0:T(4,128)(2,1)}), bf16[512,4,128]{2,1,0:T(4,128)(2,1)S(1)}, u32[]{:S(2)}, u32[]{:S(2)}) async-start(bf16[512,4,128]{2,1,0:T(4,128)(2,1)} %bitcast.18), calls=%async_computation | async-start | bytes 1048576 | tf_op jit(solution)/shard_map/all_to_all | solution.py:375
  27.5 0.0 copy-done.4
  27.5 12.9 %collective-permute-start = (bf16[144,128]{1,0:T(8,128)(2,1)S(1)}, bf16[144,128]{1,0:T(8,128)(2,1)S(1)}, u32[]{:S(2)}, u32[]{:S(2)}) collective-permute-start(bf16[144,128]{1,0:T(8,128)(2,1)S(1)} %copy-done.4), channel_id=1, source_target_pairs={{5,0},{6,1},{7,2},{8,3},{9,4},{10,5},{11,6},{12,7},{13,8},{14,9},{... | collective-permute-start | bytes 110600 | tf_op jit(solution)/shard_map/ppermute | solution.py:379
  40.3 0.0 copy-done.5
  40.4 3.1 %collective-permute-start.1 = (bf16[16,128]{1,0:T(8,128)(2,1)S(1)}, bf16[16,128]{1,0:T(8,128)(2,1)S(1)}, u32[]{:S(2)}, u32[]{:S(2)}) collective-permute-start(bf16[16,128]{1,0:T(8,128)(2,1)S(1)} %copy-done.5), channel_id=1, source_target_pairs={{9,0},{10,1},{11,2},{12,3},{13,4},{14,5},{15,6},{16,7},{17,8},{18,... | collective-permute-start | bytes 12296 | tf_op jit(solution)/shard_map/ppermute | solution.py:379
  43.5 2.4 %collective-permute-done.1.numbers_ref = bf16[16,128]{1,0:T(8,128)(2,1)S(1)} collective-permute-done((bf16[16,128]{1,0:T(8,128)(2,1)S(1)}, bf16[16,128]{1,0:T(8,128)(2,1)S(1)}, u32[]{:S(2)}, u32[]{:S(2)}) %collective-permute-start.1) | collective-permute-done | bytes 4128 | tf_op jit(solution)/shard_map/ppermute | solution.py:379
  45.9 0.0 collective-permute-done.pair_ref
  45.9 3.5 %all-to-all-done = bf16[512,4,128]{2,1,0:T(4,128)(2,1)S(1)} async-done(((bf16[512,4,128]{2,1,0:T(4,128)(2,1)}), bf16[512,4,128]{2,1,0:T(4,128)(2,1)S(1)}, u32[]{:S(2)}, u32[]{:S(2)}) %all-to-all-start) | async-done | bytes 524320 | tf_op jit(solution)/shard_map/all_to_all | solution.py:375
  49.4 0.0 copy-done
  49.4 0.0 copy-done.3
  49.4 3.7 %context_first.1 = (bf16[3072,128]{1,0:T(8,128)(2,1)}, bf16[512,128]{1,0:T(8,128)(2,1)S(1)}, bf16[512,128]{1,0:T(8,128)(2,1)S(1)}, f32[4,128]{1,0:T(4,128)S(1)},...) custom-call(bf16[2048,128]{1,0:T(8,128)(2,1)S(1)} %bitcast.17, ...), custom_call_target="tpu_custom_call" | custom-call | flops 600000000 | bytes 4000000 | tf_op jit(solution)/shard_map/context_first/pallas_call | solution.py:360
  53.1 0.0 copy-start.1
  53.1 9.2 %all-to-all-start.1 = ((bf16[512,3,2,128]{3,2,1,0:T(2,128)(2,1)}), bf16[512,3,2,128]{3,2,1,0:T(2,128)(2,1)S(1)}, u32[]{:S(2)}, u32[]{:S(2)}) async-start(bf16[512,3,2,128]{3,2,1,0:T(2,128)(2,1)} %bitcast.8), calls=%async_computation.1 | async-start | bytes 1572864 | tf_op jit(solution)/shard_map/all_to_all | solution.py:375
  62.4 5.0 %collective-permute-start.2 = (bf16[128,128]{1,0:T(8,128)(2,1)S(1)}, bf16[128,128]{1,0:T(8,128)(2,1)S(1)}, u32[]{:S(2)}, u32[]{:S(2)}) collective-permute-start(bf16[128,128]{1,0:T(8,128)(2,1)S(1)} %get-tuple-element.33), channel_id=1, source_target_pairs={{507,0},{508,1},{509,2},{510,3},{511,4},{0,5},{1,6},{2,7},{3,8},{4... | collective-permute-start | bytes 98312 | tf_op jit(solution)/shard_map/ppermute | solution.py:379
  67.4 4.7 %collective-permute-start.3 = (bf16[128,128]{1,0:T(8,128)(2,1)S(1)}, bf16[128,128]{1,0:T(8,128)(2,1)S(1)}, u32[]{:S(2)}, u32[]{:S(2)}) collective-permute-start(bf16[128,128]{1,0:T(8,128)(2,1)S(1)} %get-tuple-element.34.mine_ref), channel_id=1, source_target_pairs={{503,0},{504,1},{505,2},{506,3},{507,4},{508,5},{509,6},{510,7},{5... | collective-permute-start | bytes 98312 | tf_op jit(solution)/shard_map/ppermute | solution.py:379
  72.1 15.0 %collective-permute-done.2.partner_ref = bf16[128,128]{1,0:T(8,128)(2,1)S(1)} collective-permute-done((bf16[128,128]{1,0:T(8,128)(2,1)S(1)}, bf16[128,128]{1,0:T(8,128)(2,1)S(1)}, u32[]{:S(2)}, u32[]{:S(2)}) %collective-permute-start.2) | collective-permute-done | bytes 32800 | tf_op jit(solution)/shard_map/ppermute | solution.py:379
  87.1 2.0 %collective-permute-done.3.partner_ref = bf16[128,128]{1,0:T(8,128)(2,1)S(1)} collective-permute-done((bf16[128,128]{1,0:T(8,128)(2,1)S(1)}, bf16[128,128]{1,0:T(8,128)(2,1)S(1)}, u32[]{:S(2)}, u32[]{:S(2)}) %collective-permute-start.3) | collective-permute-done | bytes 32800 | tf_op jit(solution)/shard_map/ppermute | solution.py:379
  89.1 0.8 all-to-all-done.1
  90.0 0.0 copy-done.1
  90.0 0.0 copy-done.2
  90.0 3.0 %vertex_first.1 = (bf16[2048,128]{1,0:T(8,128)(2,1)}, bf16[128,128]{1,0:T(8,128)(2,1)S(1)}, bf16[512,128]{1,0:T(8,128)(2,1)S(1)}, f32[4,128]{1,0:T(4,128)S(1)}) custom-call(bf16[3072,128]{1,0:T(8,128)(2,1)S(1)} %bitcast.14, bf16[4,512,128]{2,1,0:T(8,128)(2,1)S(1)} %copy-done.2, f32[144,128]{1,0:T(8,128)S(1)} %copy-done.3, ...), custom_call_target="tpu_custom_call" | custom-call | flops 600000000 | bytes 4000000 | tf_op jit(solution)/shard_map/vertex_first/pallas_call | solution.py:360
  92.9 8.8 %all-to-all-start.2 = ((bf16[512,4,128]{2,1,0:T(4,128)(2,1)}), bf16[512,4,128]{2,1,0:T(4,128)(2,1)S(1)}, u32[]{:S(2)}, u32[]{:S(2)}) async-start(bf16[512,4,128]{2,1,0:T(4,128)(2,1)} %bitcast.10), calls=%async_computation.2 | async-start | bytes 1048576 | tf_op jit(solution)/shard_map/all_to_all | solution.py:375
  101.8 13.1 %collective-permute-start.4 = (bf16[128,128]{1,0:T(8,128)(2,1)S(1)}, bf16[128,128]{1,0:T(8,128)(2,1)S(1)}, u32[]{:S(2)}, u32[]{:S(2)}) collective-permute-start(bf16[128,128]{1,0:T(8,128)(2,1)S(1)} %get-tuple-element.47), channel_id=1, source_target_pairs={{9,0},{10,1},{11,2},{12,3},{13,4},{14,5},{15,6},{16,7},{17,8},{18,... | collective-permute-start | bytes 98312 | tf_op jit(solution)/shard_map/ppermute | solution.py:379
  114.9 3.2 %vertex_last.1 = (bf16[512,128]{1,0:T(8,128)(2,1)}, f32[4,128]{1,0:T(4,128)}, bf16[2048,128]{1,0:T(8,128)(2,1)S(1)}, f32[1,2048]{1,0:T(1,128)S(1)}) custom-call(bf16[3072,128]{1,0:T(8,128)(2,1)S(1)} %bitcast.15, bf16[4,512,128]{2,1,0:T(8,128)(2,1)S(1)} %copy-done.2, f32[144,128]{1,0:T(8,128)S(1)} %copy-done.3, ...), custom_call_target="tpu_custom_call" | custom-call | flops 600000000 | bytes 4000000 | tf_op jit(solution)/shard_map/vertex_last/pallas_call | solution.py:360
  118.1 0.0 collective-permute-done.4.pair_ref
  118.1 5.6 %all-to-all-done.2 = bf16[512,4,128]{2,1,0:T(4,128)(2,1)S(1)} async-done(((bf16[512,4,128]{2,1,0:T(4,128)(2,1)}), bf16[512,4,128]{2,1,0:T(4,128)(2,1)S(1)}, u32[]{:S(2)}, u32[]{:S(2)}) %all-to-all-start.2) | async-done | bytes 524320 | tf_op jit(solution)/shard_map/all_to_all | solution.py:375
  123.7 2.0 %context_last.1 = (bf16[512,128]{1,0:T(8,128)(2,1)}, f32[4,128]{1,0:T(4,128)}) custom-call(bf16[2048,128]{1,0:T(8,128)(2,1)S(1)} %bitcast.16, bf16[2048,128]{1,0:T(8,128)(2,1)S(1)} %get-tuple-element.45.rows_ref, f32[1,2048]{1,0:T(1,128)S(1)} %get-tuple-element.46.place_ref, bf16[128,128]{1,0:T(8,128)(2,1)S(1)} %collective-permute-done.4.pair_ref, ...), custom_call_target="tpu_custom_call" | custom-call | flops 600000000 | bytes 4000000 | tf_op jit(solution)/shard_map/context_last/pallas_call | solution.py:360
  (1 shorter events, 0.0 us)
Async XLA Ops:
  5.3 22.2 %copy-start.4 = (bf16[144,128]{1,0:T(8,128)(2,1)S(1)}, bf16[144,128]{1,0:T(8,128)(2,1)}, u32[]{:S(2)}) copy-start(bf16[144,128]{1,0:T(8,128)(2,1)} %get-tuple-element.29) | copy-start | bytes 110596
  5.3 35.1 %copy-start.5 = (bf16[16,128]{1,0:T(8,128)(2,1)S(1)}, bf16[16,128]{1,0:T(8,128)(2,1)}, u32[]{:S(2)}) copy-start(bf16[16,128]{1,0:T(8,128)(2,1)} %get-tuple-element.30) | copy-start | bytes 12292
  5.3 44.1 %copy-start = (bf16[512,128]{1,0:T(8,128)(2,1)S(1)}, bf16[512,128]{1,0:T(8,128)(2,1)}, u32[]{:S(2)}) copy-start(bf16[512,128]{1,0:T(8,128)(2,1)} %table_ref.4) | copy-start | bytes 393220
  5.3 44.1 %copy-start.3 = (f32[144,128]{1,0:T(8,128)S(1)}, f32[144,128]{1,0:T(8,128)}, u32[]{:S(2)}) copy-start(f32[144,128]{1,0:T(8,128)} %get-tuple-element.31.pairs_ref) | copy-start | bytes 221188
  5.3 44.1 %all-to-all-start = ((bf16[512,4,128]{2,1,0:T(4,128)(2,1)}), bf16[512,4,128]{2,1,0:T(4,128)(2,1)S(1)}, u32[]{:S(2)}, u32[]{:S(2)}) async-start(bf16[512,4,128]{2,1,0:T(4,128)(2,1)} %bitcast.18), calls=%async_computation | async-start | bytes 1048576 | tf_op jit(solution)/shard_map/all_to_all | solution.py:375
  27.5 18.4 %collective-permute-start = (bf16[144,128]{1,0:T(8,128)(2,1)S(1)}, bf16[144,128]{1,0:T(8,128)(2,1)S(1)}, u32[]{:S(2)}, u32[]{:S(2)}) collective-permute-start(bf16[144,128]{1,0:T(8,128)(2,1)S(1)} %copy-done.4), channel_id=1, source_target_pairs={{5,0},{6,1},{7,2},{8,3},{9,4},{10,5},{11,6},{12,7},{13,8},{14,9},{... | collective-permute-start | bytes 110600 | tf_op jit(solution)/shard_map/ppermute | solution.py:379
  40.4 5.5 %collective-permute-start.1 = (bf16[16,128]{1,0:T(8,128)(2,1)S(1)}, bf16[16,128]{1,0:T(8,128)(2,1)S(1)}, u32[]{:S(2)}, u32[]{:S(2)}) collective-permute-start(bf16[16,128]{1,0:T(8,128)(2,1)S(1)} %copy-done.5), channel_id=1, source_target_pairs={{9,0},{10,1},{11,2},{12,3},{13,4},{14,5},{15,6},{16,7},{17,8},{18,... | collective-permute-start | bytes 12296 | tf_op jit(solution)/shard_map/ppermute | solution.py:379
  53.1 36.9 %copy-start.1 = (bf16[512,128]{1,0:T(8,128)(2,1)S(1)}, bf16[512,128]{1,0:T(8,128)(2,1)}, u32[]{:S(2)}) copy-start(bf16[512,128]{1,0:T(8,128)(2,1)} %table_ref.5) | copy-start | bytes 393220
  53.1 36.9 %copy-start.2 = (bf16[4,512,128]{2,1,0:T(8,128)(2,1)S(1)}, bf16[4,512,128]{2,1,0:T(8,128)(2,1)}, u32[]{:S(2)}) copy-start(bf16[4,512,128]{2,1,0:T(8,128)(2,1)} %get-tuple-element.36.sent_ref) | copy-start | bytes 1572868
  53.1 36.8 %all-to-all-start.1 = ((bf16[512,3,2,128]{3,2,1,0:T(2,128)(2,1)}), bf16[512,3,2,128]{3,2,1,0:T(2,128)(2,1)S(1)}, u32[]{:S(2)}, u32[]{:S(2)}) async-start(bf16[512,3,2,128]{3,2,1,0:T(2,128)(2,1)} %bitcast.8), calls=%async_computation.1 | async-start | bytes 1572864 | tf_op jit(solution)/shard_map/all_to_all | solution.py:375
  62.4 24.8 %collective-permute-start.2 = (bf16[128,128]{1,0:T(8,128)(2,1)S(1)}, bf16[128,128]{1,0:T(8,128)(2,1)S(1)}, u32[]{:S(2)}, u32[]{:S(2)}) collective-permute-start(bf16[128,128]{1,0:T(8,128)(2,1)S(1)} %get-tuple-element.33), channel_id=1, source_target_pairs={{507,0},{508,1},{509,2},{510,3},{511,4},{0,5},{1,6},{2,7},{3,8},{4... | collective-permute-start | bytes 98312 | tf_op jit(solution)/shard_map/ppermute | solution.py:379
  67.4 21.8 %collective-permute-start.3 = (bf16[128,128]{1,0:T(8,128)(2,1)S(1)}, bf16[128,128]{1,0:T(8,128)(2,1)S(1)}, u32[]{:S(2)}, u32[]{:S(2)}) collective-permute-start(bf16[128,128]{1,0:T(8,128)(2,1)S(1)} %get-tuple-element.34.mine_ref), channel_id=1, source_target_pairs={{503,0},{504,1},{505,2},{506,3},{507,4},{508,5},{509,6},{510,7},{5... | collective-permute-start | bytes 98312 | tf_op jit(solution)/shard_map/ppermute | solution.py:379
  92.9 30.7 %all-to-all-start.2 = ((bf16[512,4,128]{2,1,0:T(4,128)(2,1)}), bf16[512,4,128]{2,1,0:T(4,128)(2,1)S(1)}, u32[]{:S(2)}, u32[]{:S(2)}) async-start(bf16[512,4,128]{2,1,0:T(4,128)(2,1)} %bitcast.10), calls=%async_computation.2 | async-start | bytes 1048576 | tf_op jit(solution)/shard_map/all_to_all | solution.py:375
  101.8 16.3 %collective-permute-start.4 = (bf16[128,128]{1,0:T(8,128)(2,1)S(1)}, bf16[128,128]{1,0:T(8,128)(2,1)S(1)}, u32[]{:S(2)}, u32[]{:S(2)}) collective-permute-start(bf16[128,128]{1,0:T(8,128)(2,1)S(1)} %get-tuple-element.47), channel_id=1, source_target_pairs={{9,0},{10,1},{11,2},{12,3},{13,4},{14,5},{15,6},{16,7},{17,8},{18,... | collective-permute-start | bytes 98312 | tf_op jit(solution)/shard_map/ppermute | solution.py:379

commit v5 on v4

--- a/solution.py
+++ b/solution.py
@@ -152,7 +152,7 @@
         grad = grad_of(at, dot(one_hot_of_row(pair_row, TILE, float(at)), pair_terms))
         state = jnp.transpose(jnp.broadcast_to(state_ref[pl.ds(b, 1), :], (TILE, TILE)))
         state = state + row_dot(grad, grad) * (1.0 / width)
-        rows = table_ref[pl.ds(at, TILE), :].astype(F32) - 0.5 * grad / jnp.sqrt(state)
+        rows = table_ref[pl.ds(at, TILE), :].astype(F32) - grad * (0.5 * lax.rsqrt(state))
         new_ref[pl.ds(at, TILE), :] = rows.astype(BF16)
         new_state_ref[pl.ds(b, 1), :] = jnp.transpose(state)[0:1, :]
 
@@ -175,20 +175,15 @@
     return ((jax.nn.sigmoid(row_dot(here, there)) - 1.0) * there).astype(BF16)
 
 
-def columns_of(grids):
-    high_part, groups = LANES // 8, []
-    spread = ones_where(iota((LANES, 8), 0) // high_part == iota((LANES, 8), 1))
-    keep = iota((LANES, LANES), 1) % high_part == iota((LANES, LANES), 0) % high_part
-    collect = ones_where(iota((LANES, LANES), 0) // high_part == iota((LANES, LANES), 1))
-    for g in range(0, len(grids), 8):
-        wide = jnp.concatenate(grids[g : g + 8], axis=1)
-        high = jnp.floor(wide * (1.0 / 256.0))
-        total = 0.0
-        for digit, scale in ((high, 256.0), (wide - 256.0 * high, 1.0)):
-            kept = jnp.where(keep, dot(spread, digit.astype(BF16)), 0.0).astype(BF16)
-            total = total + scale * dot(kept, collect)
-        groups.append(total)
-    return [groups[i // 8][:, i % 8 : i % 8 + 1] for i in range(len(grids))]
+def rows_of_grids(grids):
+    count, wide = len(grids), LANES // 8
+    stack = jnp.concatenate(grids, axis=0)
+    repeat = ones_where(iota((wide, LANES), 1) % wide == iota((wide, LANES), 0))
+    high = jnp.floor(stack * (1.0 / 256.0))
+    low = stack - 256.0 * high
+    spread = 256.0 * dot(high.astype(BF16), repeat) + dot(low.astype(BF16), repeat)
+    mine = iota((8 * count, LANES), 0) % 8 == iota((8 * count, LANES), 1) // wide
+    return jnp.sum(jnp.where(mine, spread, 0.0).reshape(count, 8, LANES), axis=1)
 
 
 def first_kernel(
@@ -204,26 +199,29 @@
     earlier = iota((pairs, pairs), 1) < iota((pairs, pairs), 0)
     grids = [r[e, k].astype(F32) for r in (owner_ref, row_ref) for e in range(episodes) for k in range(negatives)]
     grids += [offset_ref[e, :, w, :].astype(F32) for e in range(episodes) for w in range(2)]
-    columns = columns_of(grids)
-    wide = jnp.zeros((pairs, LANES), F32)
-    for e in range(episodes):
-        for w in range(2):
-            which = block_ref[e, w : w + 1, :].astype(F32)
-            here = iota((pairs, 8), 1) == iota((pairs, 8), 0) // (pairs // 8)
-            block = jnp.sum(jnp.where(here, which, 0.0), axis=1, keepdims=True)
-            column = block * float(TILE) + columns[2 * episodes * negatives + 2 * e + w]
-            wide = jnp.where(lane == 2 * e + w, column, wide)
-    pairs_ref[0:pairs, :] = wide
+    lines = rows_of_grids(grids)
+    of_block = ones_where(iota((8, LANES), 0) == iota((8, LANES), 1) // (LANES // 8))
+    blocks_of = jnp.concatenate([block_ref[e].astype(F32) for e in range(episodes)], axis=0)
+    n_lists = 2 * episodes * negatives
+    offsets = lines[n_lists:] + float(TILE) * dot(blocks_of.astype(BF16), of_block)
+    lines = jnp.concatenate([lines[:n_lists], offsets], axis=0)
+    turned = jnp.transpose(jnp.concatenate([lines, jnp.zeros((LANES - lines.shape[0], LANES), F32)], axis=0))
+    columns = [turned[:, i : i + 1] for i in range(n_lists)]
+    wide = turned[:, n_lists : n_lists + 2 * episodes]
+    pairs_ref[0:pairs, :] = jnp.zeros((pairs, LANES), F32)
+    pairs_ref[0:pairs, 0 : 2 * episodes] = wide
     pairs_ref[pairs : pairs + 16, :] = jnp.zeros((16, LANES), F32)
     tiles = vertex_state_ref.shape[0]
     pairs_ref[pairs : pairs + tiles, :] = vertex_state_ref[...]
     pairs_ref[pairs + 8 : pairs + 8 + tiles, :] = context_state_ref[...]
+    vectors = rows_of(wide[:, 0:1], table_ref)
+    pair_ref[0:pairs, :] = vectors.astype(BF16)
     owner_rows, values = [], []
     for e in range(episodes):
         vertex = wide[:, 2 * e : 2 * e + 1] + 1.0
         vertex_high = jnp.floor(vertex * (1.0 / 256.0))
         cols = columns[e * negatives : (e + 1) * negatives]
-        rows = [to_row(c) for c in cols]
+        rows = [lines[e * negatives + k : e * negatives + k + 1, :] for k in range(negatives)]
         for k in range(negatives):
             same = jnp.where((cols[k] == rows[k]) & earlier, 1.0, 0.0)
             for j in range(k):
@@ -235,16 +233,21 @@
             value = jnp.where(part == 2, vertex_high, value)
             value = jnp.where(part == 3, vertex - 256.0 * vertex_high, value)
             mine = (slot_of_lane == rank) & (lane // 16 == e)
-            values.append(jnp.where(mine, value, 0.0).astype(BF16))
+            value = jnp.where(mine, value, 0.0).astype(BF16)
+            if e == 0:
+                value = [value] + [jnp.where(rank == s, vectors, 0.0).astype(BF16) for s in range(CAP)]
+                value = jnp.concatenate(value, axis=1)
+            values.append(value)
             owner_rows.append(rows[k])
 
-    owner_row, value = jnp.concatenate(owner_rows, axis=1), jnp.concatenate(values, axis=0)
+    hot = [jnp.concatenate(owner_rows[e * negatives : (e + 1) * negatives], axis=1) for e in range(episodes)]
+    value = [jnp.concatenate(values[e * negatives : (e + 1) * negatives], axis=0) for e in range(episodes)]
     for o in range(0, owners, TILE):
-        total = dot(one_hot_of_row(owner_row, TILE, float(o)), value)
-        rows_ref[CAP, o : o + TILE, :] = total.astype(BF16)
-    gather_slots(table_ref, rows_ref.at[CAP], rows_ref, 0, 0, 2)
+        first, second = [dot(one_hot_of_row(h, TILE, float(o)), v) for h, v in zip(hot, value)]
+        rows_ref[CAP, o : o + TILE, :] = (first[:, 0:LANES] + second).astype(BF16)
+        for s in range(CAP):
+            rows_ref[s, o : o + TILE, :] = first[:, (s + 1) * LANES : (s + 2) * LANES].astype(BF16)
     by_owner(rows_ref, flat_ref, CAP + 1, CAP + 1)
-    pair_ref[0:pairs, :] = rows_of(wide[:, 0:1], table_ref).astype(BF16)
     pair_ref[pairs : pairs + 16, :] = numbers_of(pairs_ref, 0)
     numbers_ref[...] = numbers_of(pairs_ref, 1)
 
@@ -304,29 +307,11 @@
 
 def vertex_last(
     flat_ref, sent_ref, pairs_ref, partner_ref, table_ref, state_ref, slots_ref, context_ref,
-    new_ref, new_state_ref, context_flat_ref, place_ref,
-    got_ref, rows_ref, context_turned_ref, turned_ref, terms_ref,
-):
-    gather_slots(context_ref, slots_ref, rows_ref, 0, 1, 0)
-    by_owner(rows_ref, context_flat_ref, CAP, CAP + 1)
+    new_ref, new_state_ref, context_rows_ref, context_turned_ref,
+    got_ref, rows_ref, turned_ref, terms_ref,
+):
+    gather_slots(context_ref, slots_ref, context_rows_ref, 0, 1, 0)
     turn(slots_ref, context_turned_ref)
-    group = CAP + 1
-    part = part_of(group)
-    i = iota((CAP * part, group * part), 0)
-    move = ones_where(iota((CAP * part, group * part), 1) == (i % part) * group + i // part)
-    lanes = [lane_of(1, s, 0) for s in range(CAP)]
-
-    def step(at, b):
-        digits = [
-            jnp.concatenate([context_turned_ref[k + d : k + d + 1, at : at + part] for k in lanes], axis=1)
-            for d in range(2)
-        ]
-        which = iota((16, CAP * part), 0)
-        both = jnp.where(which == 0, digits[0], jnp.where(which == 1, digits[1], 0.0)).astype(BF16)
-        moved = dot(both, move)
-        place_ref[:, at * group : (at + part) * group] = moved[0:1, :] * 256.0 + moved[1:2, :] - 1.0
-
-    blocks(slots_ref.shape[0], part, step)
 
     turn(sent_ref.at[CAP], turned_ref)
     by_slot(flat_ref, got_ref, CAP, CAP, 2 * CAP)
@@ -338,21 +323,14 @@
 
 
 def context_last(
-    flat_ref, rows_ref, place_ref, pair_ref, numbers_ref, mine_ref, table_ref, state_ref,
-    new_ref, new_state_ref, terms_ref,
-):
-    def weigh(at, b):
-        there = flat_ref[pl.ds(at, BLOCK), :].astype(F32)
-        weight = jax.nn.sigmoid(row_dot(rows_ref[pl.ds(at, BLOCK), :].astype(F32), there))
-        terms_ref[pl.ds(at, BLOCK), :] = (weight * there).astype(BF16)
-
-    blocks(flat_ref.shape[0], BLOCK, weigh)
+    flat_ref, rows_ref, turned_ref, pair_ref, numbers_ref, mine_ref, table_ref, state_ref,
+    new_ref, new_state_ref, got_ref, terms_ref,
+):
+    by_slot(flat_ref, got_ref, 0, CAP, CAP + 1)
+    weigh_slots(rows_ref, 0, got_ref, 0, terms_ref)
     row = row_numbers(numbers_ref[...])
     pair_terms = pair_terms_of(mine_ref[...].astype(F32), pair_ref[...].astype(F32))
-
-    def grad_of(at, grad):
-        return grad + dot(one_hot_of_row(place_ref[...], TILE, float(at)), terms_ref[...])
-
+    grad_of = scattered(turned_ref, terms_ref, lane_of(1, 0, 0))
     adagrad(table_ref, state_ref, new_ref, new_state_ref, grad_of, row, pair_terms)
 
 
@@ -433,14 +411,13 @@
     )
     got_pair_c = passed_along(pair_c, n - shifts[1], n)
     got_c = exchange(flat_c, n)
-    vertex_2, v_state_2, rows_b, place_b = call(
-        vertex_last, "vertex_last", [table, state, flat(CAP + 1), ((1, n * (CAP + 1)), F32)],
-        [terms, terms, turned, turned, terms],
+    vertex_2, v_state_2, rows_b, turned_b = call(
+        vertex_last, "vertex_last", [table, state, slots(CAP), ((LANES, n), F32)], [terms, terms, turned, terms],
         got_b, rows_a, pairs, theirs_1, vertex_1, v_state_1, slots_b, context_1,
     )
     context_2, c_state_2 = call(
-        context_last, "context_last", [table, state], [pltpu.VMEM((n * (CAP + 1), width), BF16)],
-        got_c, rows_b, place_b, got_pair_c, got_numbers, pair_b1, context_1, c_state_1,
+        context_last, "context_last", [table, state], [terms, terms],
+        got_c, rows_b, turned_b, got_pair_c, got_numbers, pair_b1, context_1, c_state_1,
     )
     return vertex_2, context_2, v_state_2.reshape(rows), c_state_2.reshape(rows)
 

time: 126 us -> 126 us (level)
  transfers between devices with their start and end apart: 8 -> 8, of which waited for: 6 -> 6; matrix products, arithmetic and copies ran while one was open for 0% -> 0% of each run, Pallas kernels for 3% -> 2%
where the time goes in v5:
time: 126 us; the launch traced here: 125 us
  starting transfers between devices  79 us (63%)
  waiting for transfers between devices  29.8 us (24%)
  Pallas kernels  15.6 us (12%)
    all_to_all x3, starting transfers between devices, exchange(): lax.all_to_all(split, AXES, split_axis=0, concat_axis=0, tiled=True)  40.2 us
    ppermute x5, starting transfers between devices, passed_along(): lax.ppermute(block, AXES, [((i - distance) % n_devices, i) for i in range...  38.8 us
    ppermute x5, waiting for transfers between devices, passed_along(): lax.ppermute(block, AXES, [((i - distance) % n_devices, i) for i in range...  19.5 us
    pallas_call x5, Pallas kernels, call(): pl.pallas_call(kernel, name=name, out_shape=[jax.ShapeDtypeStruct(s, d) f...  15.6 us
    all_to_all x3, waiting for transfers between devices, exchange(): lax.all_to_all(split, AXES, split_axis=0, concat_axis=0, tiled=True)  10.4 us
  transfers between devices with their start and end apart: 8, of which 6 were waited for; matrix products, arithmetic and copies ran while one was open for 0% of the time, Pallas kernels for 2%

profile of v5, /device:TPU:1, one launch (start us, length us, event | category | flops | bytes accessed | tf_op | source)
XLA Modules:
  0.0 125.2 jit_solution(14672361789316314891)
XLA Ops:
  0.6 4.3 %slots.1 = (bf16[2048,128]{1,0:T(8,128)(2,1)}, bf16[4,512,128]{2,1,0:T(8,128)(2,1)}, bf16[144,128]{1,0:T(8,128)(2,1)}, f32[144,128]{1,0:T(8,128)}, bf16[16,128]{1,0:T(8,128)(2,1)}) custom-call(s32[2,5,8,16]{3,2,1,0:T(8,128)} %bitcast.19, s32[2,5,8,16]{3,2,1,0:T(8,128)} %bitcast.20, s32[2,2,8]{2,1,0:T(2,128)} %bitcast.22, s32[2,8,2,16]{3,2,1,0:T(2,128)} %bitcast.21, ...), custom_call_target="tpu_custom_call" | custom-call | flops 600000000 | bytes 4000000 | tf_op jit(solution)/shard_map/slots/pallas_call | solution.py:338
  4.9 0.0 copy-start.4
  4.9 0.0 copy-start.5
  4.9 0.0 copy-start
  5.0 0.0 copy-start.3
  5.0 22.2 %all-to-all-start = ((bf16[512,4,128]{2,1,0:T(4,128)(2,1)}), bf16[512,4,128]{2,1,0:T(4,128)(2,1)S(1)}, u32[]{:S(2)}, u32[]{:S(2)}) async-start(bf16[512,4,128]{2,1,0:T(4,128)(2,1)} %bitcast.18), calls=%async_computation | async-start | bytes 1048576 | tf_op jit(solution)/shard_map/all_to_all | solution.py:353
  27.1 0.0 copy-done.4
  27.1 12.9 %collective-permute-start = (bf16[144,128]{1,0:T(8,128)(2,1)S(1)}, bf16[144,128]{1,0:T(8,128)(2,1)S(1)}, u32[]{:S(2)}, u32[]{:S(2)}) collective-permute-start(bf16[144,128]{1,0:T(8,128)(2,1)S(1)} %copy-done.4), channel_id=1, source_target_pairs={{5,0},{6,1},{7,2},{8,3},{9,4},{10,5},{11,6},{12,7},{13,8},{14,9},{... | collective-permute-start | bytes 110600 | tf_op jit(solution)/shard_map/ppermute | solution.py:357
  40.0 0.0 copy-done.5
  40.0 3.1 %collective-permute-start.1 = (bf16[16,128]{1,0:T(8,128)(2,1)S(1)}, bf16[16,128]{1,0:T(8,128)(2,1)S(1)}, u32[]{:S(2)}, u32[]{:S(2)}) collective-permute-start(bf16[16,128]{1,0:T(8,128)(2,1)S(1)} %copy-done.5), channel_id=1, source_target_pairs={{9,0},{10,1},{11,2},{12,3},{13,4},{14,5},{15,6},{16,7},{17,8},{18,... | collective-permute-start | bytes 12296 | tf_op jit(solution)/shard_map/ppermute | solution.py:357
  43.2 2.4 %collective-permute-done.1.numbers_ref = bf16[16,128]{1,0:T(8,128)(2,1)S(1)} collective-permute-done((bf16[16,128]{1,0:T(8,128)(2,1)S(1)}, bf16[16,128]{1,0:T(8,128)(2,1)S(1)}, u32[]{:S(2)}, u32[]{:S(2)}) %collective-permute-start.1) | collective-permute-done | bytes 4128 | tf_op jit(solution)/shard_map/ppermute | solution.py:357
  45.6 0.0 collective-permute-done.pair_ref
  45.6 3.5 %all-to-all-done = bf16[512,4,128]{2,1,0:T(4,128)(2,1)S(1)} async-done(((bf16[512,4,128]{2,1,0:T(4,128)(2,1)}), bf16[512,4,128]{2,1,0:T(4,128)(2,1)S(1)}, u32[]{:S(2)}, u32[]{:S(2)}) %all-to-all-start) | async-done | bytes 524320 | tf_op jit(solution)/shard_map/all_to_all | solution.py:353
  49.1 0.0 copy-done
  49.1 0.0 copy-done.3
  49.1 3.7 %context_first.1 = (bf16[3072,128]{1,0:T(8,128)(2,1)}, bf16[512,128]{1,0:T(8,128)(2,1)S(1)}, bf16[512,128]{1,0:T(8,128)(2,1)S(1)}, f32[4,128]{1,0:T(4,128)S(1)},...) custom-call(bf16[2048,128]{1,0:T(8,128)(2,1)S(1)} %bitcast.17, ...), custom_call_target="tpu_custom_call" | custom-call | flops 600000000 | bytes 4000000 | tf_op jit(solution)/shard_map/context_first/pallas_call | solution.py:338
  52.8 0.0 copy-start.1
  52.8 9.2 %all-to-all-start.1 = ((bf16[512,3,2,128]{3,2,1,0:T(2,128)(2,1)}), bf16[512,3,2,128]{3,2,1,0:T(2,128)(2,1)S(1)}, u32[]{:S(2)}, u32[]{:S(2)}) async-start(bf16[512,3,2,128]{3,2,1,0:T(2,128)(2,1)} %bitcast.8), calls=%async_computation.1 | async-start | bytes 1572864 | tf_op jit(solution)/shard_map/all_to_all | solution.py:353
  62.1 5.0 %collective-permute-start.2 = (bf16[128,128]{1,0:T(8,128)(2,1)S(1)}, bf16[128,128]{1,0:T(8,128)(2,1)S(1)}, u32[]{:S(2)}, u32[]{:S(2)}) collective-permute-start(bf16[128,128]{1,0:T(8,128)(2,1)S(1)} %get-tuple-element.33), channel_id=1, source_target_pairs={{507,0},{508,1},{509,2},{510,3},{511,4},{0,5},{1,6},{2,7},{3,8},{4... | collective-permute-start | bytes 98312 | tf_op jit(solution)/shard_map/ppermute | solution.py:357
  67.1 4.7 %collective-permute-start.3 = (bf16[128,128]{1,0:T(8,128)(2,1)S(1)}, bf16[128,128]{1,0:T(8,128)(2,1)S(1)}, u32[]{:S(2)}, u32[]{:S(2)}) collective-permute-start(bf16[128,128]{1,0:T(8,128)(2,1)S(1)} %get-tuple-element.34.mine_ref), channel_id=1, source_target_pairs={{503,0},{504,1},{505,2},{506,3},{507,4},{508,5},{509,6},{510,7},{5... | collective-permute-start | bytes 98312 | tf_op jit(solution)/shard_map/ppermute | solution.py:357
  71.8 15.0 %collective-permute-done.2.partner_ref = bf16[128,128]{1,0:T(8,128)(2,1)S(1)} collective-permute-done((bf16[128,128]{1,0:T(8,128)(2,1)S(1)}, bf16[128,128]{1,0:T(8,128)(2,1)S(1)}, u32[]{:S(2)}, u32[]{:S(2)}) %collective-permute-start.2) | collective-permute-done | bytes 32800 | tf_op jit(solution)/shard_map/ppermute | solution.py:357
  86.8 2.0 %collective-permute-done.3.partner_ref = bf16[128,128]{1,0:T(8,128)(2,1)S(1)} collective-permute-done((bf16[128,128]{1,0:T(8,128)(2,1)S(1)}, bf16[128,128]{1,0:T(8,128)(2,1)S(1)}, u32[]{:S(2)}, u32[]{:S(2)}) %collective-permute-start.3) | collective-permute-done | bytes 32800 | tf_op jit(solution)/shard_map/ppermute | solution.py:357
  88.8 0.8 all-to-all-done.1
  89.7 0.0 copy-done.1
  89.7 0.0 copy-done.2
  89.7 3.0 %vertex_first.1 = (bf16[2048,128]{1,0:T(8,128)(2,1)}, bf16[128,128]{1,0:T(8,128)(2,1)S(1)}, bf16[512,128]{1,0:T(8,128)(2,1)S(1)}, f32[4,128]{1,0:T(4,128)S(1)}) custom-call(bf16[3072,128]{1,0:T(8,128)(2,1)S(1)} %bitcast.14, bf16[4,512,128]{2,1,0:T(8,128)(2,1)S(1)} %copy-done.2, f32[144,128]{1,0:T(8,128)S(1)} %copy-done.3, ...), custom_call_target="tpu_custom_call" | custom-call | flops 600000000 | bytes 4000000 | tf_op jit(solution)/shard_map/vertex_first/pallas_call | solution.py:338
  92.6 8.8 %all-to-all-start.2 = ((bf16[512,4,128]{2,1,0:T(4,128)(2,1)}), bf16[512,4,128]{2,1,0:T(4,128)(2,1)S(1)}, u32[]{:S(2)}, u32[]{:S(2)}) async-start(bf16[512,4,128]{2,1,0:T(4,128)(2,1)} %bitcast.10), calls=%async_computation.2 | async-start | bytes 1048576 | tf_op jit(solution)/shard_map/all_to_all | solution.py:353
  101.4 13.1 %collective-permute-start.4 = (bf16[128,128]{1,0:T(8,128)(2,1)S(1)}, bf16[128,128]{1,0:T(8,128)(2,1)S(1)}, u32[]{:S(2)}, u32[]{:S(2)}) collective-permute-start(bf16[128,128]{1,0:T(8,128)(2,1)S(1)} %get-tuple-element.47), channel_id=1, source_target_pairs={{9,0},{10,1},{11,2},{12,3},{13,4},{14,5},{15,6},{16,7},{17,8},{18,... | collective-permute-start | bytes 98312 | tf_op jit(solution)/shard_map/ppermute | solution.py:357
  114.5 2.8 %vertex_last.1 = (bf16[512,128]{1,0:T(8,128)(2,1)}, f32[4,128]{1,0:T(4,128)}, bf16[3,512,128]{2,1,0:T(8,128)(2,1)S(1)}, f32[128,512]{1,0:T(8,128)S(1)}) custom-call(bf16[3072,128]{1,0:T(8,128)(2,1)S(1)} %bitcast.15, bf16[4,512,128]{2,1,0:T(8,128)(2,1)S(1)} %copy-done.2, f32[144,128]{1,0:T(8,128)S(1)} %copy-done.3, ...), custom_call_target="tpu_custom_call" | custom-call | flops 600000000 | bytes 4000000 | tf_op jit(solution)/shard_map/vertex_last/pallas_call | solution.py:338
  117.3 0.0 collective-permute-done.4.pair_ref
  117.3 6.0 %all-to-all-done.2 = bf16[512,4,128]{2,1,0:T(4,128)(2,1)S(1)} async-done(((bf16[512,4,128]{2,1,0:T(4,128)(2,1)}), bf16[512,4,128]{2,1,0:T(4,128)(2,1)S(1)}, u32[]{:S(2)}, u32[]{:S(2)}) %all-to-all-start.2) | async-done | bytes 524320 | tf_op jit(solution)/shard_map/all_to_all | solution.py:353
  123.4 1.8 %context_last.1 = (bf16[512,128]{1,0:T(8,128)(2,1)}, f32[4,128]{1,0:T(4,128)}) custom-call(bf16[2048,128]{1,0:T(8,128)(2,1)S(1)} %bitcast.16, bf16[3,512,128]{2,1,0:T(8,128)(2,1)S(1)} %get-tuple-element.45.rows_ref, f32[128,512]{1,0:T(8,128)S(1)} %get-tuple-element.46.turned_ref, bf16[128,128]{1,0:T(8,128)(2,1)S(1)} %collective-permute-done.4.pair_ref, ...), custom_call_target="tpu_custom_call" | custom-call | flops 600000000 | bytes 4000000 | tf_op jit(solution)/shard_map/context_last/pallas_call | solution.py:338
  (1 shorter events, 0.0 us)
Async XLA Ops:
  4.9 22.2 %copy-start.4 = (bf16[144,128]{1,0:T(8,128)(2,1)S(1)}, bf16[144,128]{1,0:T(8,128)(2,1)}, u32[]{:S(2)}) copy-start(bf16[144,128]{1,0:T(8,128)(2,1)} %get-tuple-element.29) | copy-start | bytes 110596
  4.9 35.1 %copy-start.5 = (bf16[16,128]{1,0:T(8,128)(2,1)S(1)}, bf16[16,128]{1,0:T(8,128)(2,1)}, u32[]{:S(2)}) copy-start(bf16[16,128]{1,0:T(8,128)(2,1)} %get-tuple-element.30) | copy-start | bytes 12292
  4.9 44.1 %copy-start = (bf16[512,128]{1,0:T(8,128)(2,1)S(1)}, bf16[512,128]{1,0:T(8,128)(2,1)}, u32[]{:S(2)}) copy-start(bf16[512,128]{1,0:T(8,128)(2,1)} %table_ref.4) | copy-start | bytes 393220
  5.0 44.1 %copy-start.3 = (f32[144,128]{1,0:T(8,128)S(1)}, f32[144,128]{1,0:T(8,128)}, u32[]{:S(2)}) copy-start(f32[144,128]{1,0:T(8,128)} %get-tuple-element.31.pairs_ref) | copy-start | bytes 221188
  5.0 44.1 %all-to-all-start = ((bf16[512,4,128]{2,1,0:T(4,128)(2,1)}), bf16[512,4,128]{2,1,0:T(4,128)(2,1)S(1)}, u32[]{:S(2)}, u32[]{:S(2)}) async-start(bf16[512,4,128]{2,1,0:T(4,128)(2,1)} %bitcast.18), calls=%async_computation | async-start | bytes 1048576 | tf_op jit(solution)/shard_map/all_to_all | solution.py:353
  27.1 18.4 %collective-permute-start = (bf16[144,128]{1,0:T(8,128)(2,1)S(1)}, bf16[144,128]{1,0:T(8,128)(2,1)S(1)}, u32[]{:S(2)}, u32[]{:S(2)}) collective-permute-start(bf16[144,128]{1,0:T(8,128)(2,1)S(1)} %copy-done.4), channel_id=1, source_target_pairs={{5,0},{6,1},{7,2},{8,3},{9,4},{10,5},{11,6},{12,7},{13,8},{14,9},{... | collective-permute-start | bytes 110600 | tf_op jit(solution)/shard_map/ppermute | solution.py:357
  40.0 5.5 %collective-permute-start.1 = (bf16[16,128]{1,0:T(8,128)(2,1)S(1)}, bf16[16,128]{1,0:T(8,128)(2,1)S(1)}, u32[]{:S(2)}, u32[]{:S(2)}) collective-permute-start(bf16[16,128]{1,0:T(8,128)(2,1)S(1)} %copy-done.5), channel_id=1, source_target_pairs={{9,0},{10,1},{11,2},{12,3},{13,4},{14,5},{15,6},{16,7},{17,8},{18,... | collective-permute-start | bytes 12296 | tf_op jit(solution)/shard_map/ppermute | solution.py:357
  52.8 36.9 %copy-start.1 = (bf16[512,128]{1,0:T(8,128)(2,1)S(1)}, bf16[512,128]{1,0:T(8,128)(2,1)}, u32[]{:S(2)}) copy-start(bf16[512,128]{1,0:T(8,128)(2,1)} %table_ref.5) | copy-start | bytes 393220
  52.8 36.9 %copy-start.2 = (bf16[4,512,128]{2,1,0:T(8,128)(2,1)S(1)}, bf16[4,512,128]{2,1,0:T(8,128)(2,1)}, u32[]{:S(2)}) copy-start(bf16[4,512,128]{2,1,0:T(8,128)(2,1)} %get-tuple-element.36.sent_ref) | copy-start | bytes 1572868
  52.8 36.8 %all-to-all-start.1 = ((bf16[512,3,2,128]{3,2,1,0:T(2,128)(2,1)}), bf16[512,3,2,128]{3,2,1,0:T(2,128)(2,1)S(1)}, u32[]{:S(2)}, u32[]{:S(2)}) async-start(bf16[512,3,2,128]{3,2,1,0:T(2,128)(2,1)} %bitcast.8), calls=%async_computation.1 | async-start | bytes 1572864 | tf_op jit(solution)/shard_map/all_to_all | solution.py:353
  62.1 24.8 %collective-permute-start.2 = (bf16[128,128]{1,0:T(8,128)(2,1)S(1)}, bf16[128,128]{1,0:T(8,128)(2,1)S(1)}, u32[]{:S(2)}, u32[]{:S(2)}) collective-permute-start(bf16[128,128]{1,0:T(8,128)(2,1)S(1)} %get-tuple-element.33), channel_id=1, source_target_pairs={{507,0},{508,1},{509,2},{510,3},{511,4},{0,5},{1,6},{2,7},{3,8},{4... | collective-permute-start | bytes 98312 | tf_op jit(solution)/shard_map/ppermute | solution.py:357
  67.1 21.8 %collective-permute-start.3 = (bf16[128,128]{1,0:T(8,128)(2,1)S(1)}, bf16[128,128]{1,0:T(8,128)(2,1)S(1)}, u32[]{:S(2)}, u32[]{:S(2)}) collective-permute-start(bf16[128,128]{1,0:T(8,128)(2,1)S(1)} %get-tuple-element.34.mine_ref), channel_id=1, source_target_pairs={{503,0},{504,1},{505,2},{506,3},{507,4},{508,5},{509,6},{510,7},{5... | collective-permute-start | bytes 98312 | tf_op jit(solution)/shard_map/ppermute | solution.py:357
  92.6 30.7 %all-to-all-start.2 = ((bf16[512,4,128]{2,1,0:T(4,128)(2,1)}), bf16[512,4,128]{2,1,0:T(4,128)(2,1)S(1)}, u32[]{:S(2)}, u32[]{:S(2)}) async-start(bf16[512,4,128]{2,1,0:T(4,128)(2,1)} %bitcast.10), calls=%async_computation.2 | async-start | bytes 1048576 | tf_op jit(solution)/shard_map/all_to_all | solution.py:353
  101.4 15.9 %collective-permute-start.4 = (bf16[128,128]{1,0:T(8,128)(2,1)S(1)}, bf16[128,128]{1,0:T(8,128)(2,1)S(1)}, u32[]{:S(2)}, u32[]{:S(2)}) collective-permute-start(bf16[128,128]{1,0:T(8,128)(2,1)S(1)} %get-tuple-element.47), channel_id=1, source_target_pairs={{9,0},{10,1},{11,2},{12,3},{13,4},{14,5},{15,6},{16,7},{17,8},{18,... | collective-permute-start | bytes 98312 | tf_op jit(solution)/shard_map/ppermute | solution.py:357

commit v6 on v5

--- a/solution.py
+++ b/solution.py
@@ -77,33 +77,18 @@
         step(b * size, b)
 
 
-def part_of(group):
-    return 64 if group <= 4 else 32
-
-
-def by_owner(slots_ref, flat_ref, slots, group):
-    part = part_of(group)
-    j = iota((group * part, slots * part), 1)
-    move = ones_where(iota((group * part, slots * part), 0) == (j % part) * group + j // part)
-
-    def step(at, b):
-        rows = jnp.concatenate([slots_ref[s, pl.ds(at, part), :] for s in range(slots)], axis=0)
-        flat_ref[pl.ds(at * group, group * part), :] = dot(move, rows).astype(BF16)
-
-    blocks(slots_ref.shape[1], part, step)
-
-
-def by_slot(flat_ref, slots_ref, first, slots, group):
-    part = part_of(group)
-    i = iota((slots * part, group * part), 0)
-    move = ones_where(iota((slots * part, group * part), 1) == (i % part) * group + i // part + first)
-
-    def step(at, b):
-        rows = dot(move, flat_ref[pl.ds(at * group, group * part), :]).astype(BF16)
-        for s in range(slots):
-            slots_ref[s, pl.ds(at, part), :] = rows[s * part : (s + 1) * part, :]
-
-    blocks(slots_ref.shape[1], part, step)
+def by_owner(slots_ref, flat_ref, wide_ref, slots, group):
+    owners = slots_ref.shape[1]
+    for s in range(group):
+        rows = slots_ref[s].astype(F32) if s < slots else jnp.zeros((owners, flat_ref.shape[1]), F32)
+        wide_ref[pl.ds(s, owners, stride=group), :] = rows
+    flat_ref[...] = wide_ref[...].astype(BF16)
+
+
+def by_slot(flat_ref, slots_ref, wide_ref, first, slots, group):
+    wide_ref[...] = flat_ref[...].astype(F32)
+    for s in range(slots):
+        slots_ref[s] = wide_ref[pl.ds(first + s, slots_ref.shape[1], stride=group), :].astype(BF16)
 
 
 def turn(table_ref, turned_ref):
@@ -188,7 +173,7 @@
 
 def first_kernel(
     owner_ref, row_ref, block_ref, offset_ref, table_ref, vertex_state_ref, context_state_ref,
-    flat_ref, rows_ref, pair_ref, pairs_ref, numbers_ref,
+    flat_ref, rows_ref, pair_ref, pairs_ref, numbers_ref, wide_ref,
 ):
     episodes, negatives = owner_ref.shape[:2]
     pairs = pair_ref.shape[0] - 16
@@ -247,7 +232,7 @@
         rows_ref[CAP, o : o + TILE, :] = (first[:, 0:LANES] + second).astype(BF16)
         for s in range(CAP):
             rows_ref[s, o : o + TILE, :] = first[:, (s + 1) * LANES : (s + 2) * LANES].astype(BF16)
-    by_owner(rows_ref, flat_ref, CAP + 1, CAP + 1)
+    by_owner(rows_ref, flat_ref, wide_ref, CAP + 1, CAP + 1)
     pair_ref[pairs : pairs + 16, :] = numbers_of(pairs_ref, 0)
     numbers_ref[...] = numbers_of(pairs_ref, 1)
 
@@ -265,10 +250,10 @@
 def context_first(
     flat_ref, pair_ref, numbers_ref, table_ref, pairs_ref,
     send_ref, slots_ref, new_ref, new_state_ref, pair_0_ref, pair_1_ref,
-    rows_ref, got_ref, turned_ref, terms_ref,
+    rows_ref, got_ref, turned_ref, terms_ref, wide_ref, got_wide_ref,
 ):
     state_ref = pairs_ref.at[LANES + 8 : LANES + 16]
-    by_slot(flat_ref, got_ref, 0, CAP + 1, CAP + 1)
+    by_slot(flat_ref, got_ref, got_wide_ref, 0, CAP + 1, CAP + 1)
     slots_ref[...] = got_ref[CAP]
     turn(slots_ref, turned_ref)
 
@@ -286,35 +271,35 @@
     adagrad(table_ref, state_ref, new_ref, new_state_ref, grad_of, row, pair_terms)
     pair_1_ref[...] = rows_of(to_col(row_numbers(numbers_ref[...])), new_ref).astype(BF16)
     gather_slots(new_ref, slots_ref, rows_ref, CAP, 1, 0)
-    by_owner(rows_ref, send_ref, 2 * CAP, 2 * CAP)
+    by_owner(rows_ref, send_ref, wide_ref, 2 * CAP, 2 * CAP)
 
 
 def vertex_first(
     flat_ref, sent_ref, pairs_ref, partner_ref, table_ref,
-    send_ref, pair_ref, new_ref, new_state_ref, turned_ref, rows_ref, got_ref, terms_ref,
+    send_ref, pair_ref, new_ref, new_state_ref, turned_ref, rows_ref, got_ref, terms_ref, wide_ref, got_wide_ref,
 ):
     state_ref = pairs_ref.at[LANES : LANES + 8]
-    by_slot(flat_ref, got_ref, 0, CAP, 2 * CAP)
+    by_slot(flat_ref, got_ref, got_wide_ref, 0, CAP, 2 * CAP)
     turn(sent_ref.at[CAP], turned_ref)
     weigh_slots(sent_ref, 0, got_ref, 0, terms_ref)
     row, pair_terms = vertex_side(pairs_ref, 0, table_ref, partner_ref)
     grad_of = scattered(turned_ref, terms_ref, lane_of(0, 0, 2))
     adagrad(table_ref, state_ref, new_ref, new_state_ref, grad_of, row, pair_terms)
     gather_slots(new_ref, sent_ref.at[CAP], rows_ref, 0, 1, 2)
-    by_owner(rows_ref, send_ref, CAP, CAP + 1)
+    by_owner(rows_ref, send_ref, wide_ref, CAP, CAP + 1)
     pair_ref[...] = rows_of(pairs_ref[0:LANES, 2:3], new_ref).astype(BF16)
 
 
 def vertex_last(
     flat_ref, sent_ref, pairs_ref, partner_ref, table_ref, state_ref, slots_ref, context_ref,
     new_ref, new_state_ref, context_rows_ref, context_turned_ref,
-    got_ref, rows_ref, turned_ref, terms_ref,
+    got_ref, rows_ref, turned_ref, terms_ref, got_wide_ref,
 ):
     gather_slots(context_ref, slots_ref, context_rows_ref, 0, 1, 0)
     turn(slots_ref, context_turned_ref)
 
     turn(sent_ref.at[CAP], turned_ref)
-    by_slot(flat_ref, got_ref, CAP, CAP, 2 * CAP)
+    by_slot(flat_ref, got_ref, got_wide_ref, CAP, CAP, 2 * CAP)
     gather_slots(table_ref, sent_ref.at[CAP], rows_ref, 0, 1, 2)
     weigh_slots(rows_ref, 0, got_ref, 0, terms_ref)
     row, pair_terms = vertex_side(pairs_ref, 1, table_ref, partner_ref)
@@ -324,9 +309,9 @@
 
 def context_last(
     flat_ref, rows_ref, turned_ref, pair_ref, numbers_ref, mine_ref, table_ref, state_ref,
-    new_ref, new_state_ref, got_ref, terms_ref,
-):
-    by_slot(flat_ref, got_ref, 0, CAP, CAP + 1)
+    new_ref, new_state_ref, got_ref, terms_ref, got_wide_ref,
+):
+    by_slot(flat_ref, got_ref, got_wide_ref, 0, CAP, CAP + 1)
     weigh_slots(rows_ref, 0, got_ref, 0, terms_ref)
     row = row_numbers(numbers_ref[...])
     pair_terms = pair_terms_of(mine_ref[...].astype(F32), pair_ref[...].astype(F32))
@@ -382,6 +367,9 @@
     def slots(number):
         return ((number, n, width), BF16)
 
+    def wide(slots):
+        return pltpu.VMEM((n * slots, width), F32)
+
     turned = pltpu.VMEM((LANES, n), F32)
     terms = pltpu.VMEM((CAP, n, width), BF16)
 
@@ -390,7 +378,7 @@
     flat_a, rows_a, pair_a, pairs, numbers = call(
         first_kernel, "slots",
         [flat(CAP + 1), slots(CAP + 1), ((n_pairs + 16, width), BF16), ((n_pairs + 16, LANES), F32), ((16, LANES), BF16)],
-        [], owner, target, block, offset, vertex_table, v_state, c_state, mib=60,
+        [wide(CAP + 1)], owner, target, block, offset, vertex_table, v_state, c_state, mib=60,
     )
     got_pair_a = passed_along(pair_a, n - shifts[0], n)
     got_numbers = passed_along(numbers, n - shifts[1], n)
@@ -398,7 +386,7 @@
     flat_b, slots_b, context_1, c_state_1, pair_b0, pair_b1 = call(
         context_first, "context_first",
         [flat(2 * CAP), ((n, LANES), BF16), table, state, pair_rows, pair_rows],
-        [pltpu.VMEM((2 * CAP, n, width), BF16), pltpu.VMEM((CAP + 1, n, width), BF16), turned, terms],
+        [pltpu.VMEM((2 * CAP, n, width), BF16), pltpu.VMEM((CAP + 1, n, width), BF16), turned, terms, wide(2 * CAP), wide(CAP + 1)],
         got_a, got_pair_a, got_numbers, context_table, pairs,
     )
     theirs_0 = passed_along(pair_b0, shifts[0], n)
@@ -406,17 +394,19 @@
     got_b = exchange(flat_b, n)
     got_b, theirs_0, theirs_1 = lax.optimization_barrier((got_b, theirs_0, theirs_1))
     flat_c, pair_c, vertex_1, v_state_1 = call(
-        vertex_first, "vertex_first", [flat(CAP + 1), pair_rows, table, state], [turned, terms, terms, terms],
+        vertex_first, "vertex_first", [flat(CAP + 1), pair_rows, table, state],
+        [turned, terms, terms, terms, wide(CAP + 1), wide(2 * CAP)],
         got_b, rows_a, pairs, theirs_0, vertex_table,
     )
     got_pair_c = passed_along(pair_c, n - shifts[1], n)
     got_c = exchange(flat_c, n)
     vertex_2, v_state_2, rows_b, turned_b = call(
-        vertex_last, "vertex_last", [table, state, slots(CAP), ((LANES, n), F32)], [terms, terms, turned, terms],
+        vertex_last, "vertex_last", [table, state, slots(CAP), ((LANES, n), F32)],
+        [terms, terms, turned, terms, wide(2 * CAP)],
         got_b, rows_a, pairs, theirs_1, vertex_1, v_state_1, slots_b, context_1,
     )
     context_2, c_state_2 = call(
-        context_last, "context_last", [table, state], [terms, terms],
+        context_last, "context_last", [table, state], [terms, terms, wide(CAP + 1)],
         got_c, rows_b, turned_b, got_pair_c, got_numbers, pair_b1, context_1, c_state_1,
     )
     return vertex_2, context_2, v_state_2.reshape(rows), c_state_2.reshape(rows)

time: 126 us -> 125 us (level)
  no operation moved by 1% of the time
where the time goes in v6:
time: 125 us; the launch traced here: 124 us
  starting transfers between devices  78.9 us (63%)
  waiting for transfers between devices  30.1 us (24%)
  Pallas kernels  14.5 us (12%)
    all_to_all x3, starting transfers between devices, exchange(): lax.all_to_all(split, AXES, split_axis=0, concat_axis=0, tiled=True)  40.2 us
    ppermute x5, starting transfers between devices, passed_along(): lax.ppermute(block, AXES, [((i - distance) % n_devices, i) for i in range...  38.7 us
    ppermute x5, waiting for transfers between devices, passed_along(): lax.ppermute(block, AXES, [((i - distance) % n_devices, i) for i in range...  19.6 us
    pallas_call x5, Pallas kernels, call(): pl.pallas_call(kernel, name=name, out_shape=[jax.ShapeDtypeStruct(s, d) f...  14.5 us
    all_to_all x3, waiting for transfers between devices, exchange(): lax.all_to_all(split, AXES, split_axis=0, concat_axis=0, tiled=True)  10.5 us
  transfers between devices with their start and end apart: 8, of which 6 were waited for; matrix products, arithmetic and copies ran while one was open for 0% of the time, Pallas kernels for 2%

profile of v6, /device:TPU:1, one launch (start us, length us, event | category | flops | bytes accessed | tf_op | source)
XLA Modules:
  0.0 124.3 jit_solution(13617952086444799147)
XLA Ops:
  0.6 4.2 %slots.1 = (bf16[2048,128]{1,0:T(8,128)(2,1)}, bf16[4,512,128]{2,1,0:T(8,128)(2,1)}, bf16[144,128]{1,0:T(8,128)(2,1)}, f32[144,128]{1,0:T(8,128)}, bf16[16,128]{1,0:T(8,128)(2,1)}) custom-call(s32[2,5,8,16]{3,2,1,0:T(8,128)} %bitcast.19, s32[2,5,8,16]{3,2,1,0:T(8,128)} %bitcast.20, s32[2,2,8]{2,1,0:T(2,128)} %bitcast.22, s32[2,8,2,16]{3,2,1,0:T(2,128)} %bitcast.21, ...), custom_call_target="tpu_custom_call" | custom-call | flops 600000000 | bytes 4000000 | tf_op jit(solution)/shard_map/slots/pallas_call | solution.py:323
  4.8 0.0 copy-start.4
  4.9 0.0 copy-start.5
  4.9 0.0 copy-start
  4.9 0.0 copy-start.3
  4.9 22.2 %all-to-all-start = ((bf16[512,4,128]{2,1,0:T(4,128)(2,1)}), bf16[512,4,128]{2,1,0:T(4,128)(2,1)S(1)}, u32[]{:S(2)}, u32[]{:S(2)}) async-start(bf16[512,4,128]{2,1,0:T(4,128)(2,1)} %bitcast.18), calls=%async_computation | async-start | bytes 1048576 | tf_op jit(solution)/shard_map/all_to_all | solution.py:338
  27.1 0.0 copy-done.4
  27.1 12.9 %collective-permute-start = (bf16[144,128]{1,0:T(8,128)(2,1)S(1)}, bf16[144,128]{1,0:T(8,128)(2,1)S(1)}, u32[]{:S(2)}, u32[]{:S(2)}) collective-permute-start(bf16[144,128]{1,0:T(8,128)(2,1)S(1)} %copy-done.4), channel_id=1, source_target_pairs={{5,0},{6,1},{7,2},{8,3},{9,4},{10,5},{11,6},{12,7},{13,8},{14,9},{... | collective-permute-start | bytes 110600 | tf_op jit(solution)/shard_map/ppermute | solution.py:342
  39.9 0.0 copy-done.5
  40.0 3.1 %collective-permute-start.1 = (bf16[16,128]{1,0:T(8,128)(2,1)S(1)}, bf16[16,128]{1,0:T(8,128)(2,1)S(1)}, u32[]{:S(2)}, u32[]{:S(2)}) collective-permute-start(bf16[16,128]{1,0:T(8,128)(2,1)S(1)} %copy-done.5), channel_id=1, source_target_pairs={{9,0},{10,1},{11,2},{12,3},{13,4},{14,5},{15,6},{16,7},{17,8},{18,... | collective-permute-start | bytes 12296 | tf_op jit(solution)/shard_map/ppermute | solution.py:342
  43.1 2.4 %collective-permute-done.1.numbers_ref = bf16[16,128]{1,0:T(8,128)(2,1)S(1)} collective-permute-done((bf16[16,128]{1,0:T(8,128)(2,1)S(1)}, bf16[16,128]{1,0:T(8,128)(2,1)S(1)}, u32[]{:S(2)}, u32[]{:S(2)}) %collective-permute-start.1) | collective-permute-done | bytes 4128 | tf_op jit(solution)/shard_map/ppermute | solution.py:342
  45.5 0.0 collective-permute-done.pair_ref
  45.5 3.5 %all-to-all-done = bf16[512,4,128]{2,1,0:T(4,128)(2,1)S(1)} async-done(((bf16[512,4,128]{2,1,0:T(4,128)(2,1)}), bf16[512,4,128]{2,1,0:T(4,128)(2,1)S(1)}, u32[]{:S(2)}, u32[]{:S(2)}) %all-to-all-start) | async-done | bytes 524320 | tf_op jit(solution)/shard_map/all_to_all | solution.py:338
  49.0 0.0 copy-done
  49.0 0.0 copy-done.3
  49.0 3.2 %context_first.1 = (bf16[3072,128]{1,0:T(8,128)(2,1)}, bf16[512,128]{1,0:T(8,128)(2,1)S(1)}, bf16[512,128]{1,0:T(8,128)(2,1)S(1)}, f32[4,128]{1,0:T(4,128)S(1)},...) custom-call(bf16[2048,128]{1,0:T(8,128)(2,1)S(1)} %bitcast.17, ...), custom_call_target="tpu_custom_call" | custom-call | flops 600000000 | bytes 4000000 | tf_op jit(solution)/shard_map/context_first/pallas_call | solution.py:323
  52.2 0.0 copy-start.1
  52.2 9.2 %all-to-all-start.1 = ((bf16[512,3,2,128]{3,2,1,0:T(2,128)(2,1)}), bf16[512,3,2,128]{3,2,1,0:T(2,128)(2,1)S(1)}, u32[]{:S(2)}, u32[]{:S(2)}) async-start(bf16[512,3,2,128]{3,2,1,0:T(2,128)(2,1)} %bitcast.8), calls=%async_computation.1 | async-start | bytes 1572864 | tf_op jit(solution)/shard_map/all_to_all | solution.py:338
  61.4 5.0 %collective-permute-start.2 = (bf16[128,128]{1,0:T(8,128)(2,1)S(1)}, bf16[128,128]{1,0:T(8,128)(2,1)S(1)}, u32[]{:S(2)}, u32[]{:S(2)}) collective-permute-start(bf16[128,128]{1,0:T(8,128)(2,1)S(1)} %get-tuple-element.33), channel_id=1, source_target_pairs={{507,0},{508,1},{509,2},{510,3},{511,4},{0,5},{1,6},{2,7},{3,8},{4... | collective-permute-start | bytes 98312 | tf_op jit(solution)/shard_map/ppermute | solution.py:342
  66.4 4.5 %collective-permute-start.3 = (bf16[128,128]{1,0:T(8,128)(2,1)S(1)}, bf16[128,128]{1,0:T(8,128)(2,1)S(1)}, u32[]{:S(2)}, u32[]{:S(2)}) collective-permute-start(bf16[128,128]{1,0:T(8,128)(2,1)S(1)} %get-tuple-element.34.mine_ref), channel_id=1, source_target_pairs={{503,0},{504,1},{505,2},{506,3},{507,4},{508,5},{509,6},{510,7},{5... | collective-permute-start | bytes 98312 | tf_op jit(solution)/shard_map/ppermute | solution.py:342
  71.0 15.2 %collective-permute-done.2.partner_ref = bf16[128,128]{1,0:T(8,128)(2,1)S(1)} collective-permute-done((bf16[128,128]{1,0:T(8,128)(2,1)S(1)}, bf16[128,128]{1,0:T(8,128)(2,1)S(1)}, u32[]{:S(2)}, u32[]{:S(2)}) %collective-permute-start.2) | collective-permute-done | bytes 32800 | tf_op jit(solution)/shard_map/ppermute | solution.py:342
  86.2 2.0 %collective-permute-done.3.partner_ref = bf16[128,128]{1,0:T(8,128)(2,1)S(1)} collective-permute-done((bf16[128,128]{1,0:T(8,128)(2,1)S(1)}, bf16[128,128]{1,0:T(8,128)(2,1)S(1)}, u32[]{:S(2)}, u32[]{:S(2)}) %collective-permute-start.3) | collective-permute-done | bytes 32800 | tf_op jit(solution)/shard_map/ppermute | solution.py:342
  88.2 0.8 all-to-all-done.1
  89.0 0.0 copy-done.1
  89.0 0.0 copy-done.2
  89.0 2.7 %vertex_first.1 = (bf16[2048,128]{1,0:T(8,128)(2,1)}, bf16[128,128]{1,0:T(8,128)(2,1)S(1)}, bf16[512,128]{1,0:T(8,128)(2,1)S(1)}, f32[4,128]{1,0:T(4,128)S(1)}) custom-call(bf16[3072,128]{1,0:T(8,128)(2,1)S(1)} %bitcast.14, bf16[4,512,128]{2,1,0:T(8,128)(2,1)S(1)} %copy-done.2, f32[144,128]{1,0:T(8,128)S(1)} %copy-done.3, ...), custom_call_target="tpu_custom_call" | custom-call | flops 600000000 | bytes 4000000 | tf_op jit(solution)/shard_map/vertex_first/pallas_call | solution.py:323
  91.8 8.8 %all-to-all-start.2 = ((bf16[512,4,128]{2,1,0:T(4,128)(2,1)}), bf16[512,4,128]{2,1,0:T(4,128)(2,1)S(1)}, u32[]{:S(2)}, u32[]{:S(2)}) async-start(bf16[512,4,128]{2,1,0:T(4,128)(2,1)} %bitcast.10), calls=%async_computation.2 | async-start | bytes 1048576 | tf_op jit(solution)/shard_map/all_to_all | solution.py:338
  100.6 13.2 %collective-permute-start.4 = (bf16[128,128]{1,0:T(8,128)(2,1)S(1)}, bf16[128,128]{1,0:T(8,128)(2,1)S(1)}, u32[]{:S(2)}, u32[]{:S(2)}) collective-permute-start(bf16[128,128]{1,0:T(8,128)(2,1)S(1)} %get-tuple-element.47), channel_id=1, source_target_pairs={{9,0},{10,1},{11,2},{12,3},{13,4},{14,5},{15,6},{16,7},{17,8},{18,... | collective-permute-start | bytes 98312 | tf_op jit(solution)/shard_map/ppermute | solution.py:342
  113.8 2.6 %vertex_last.1 = (bf16[512,128]{1,0:T(8,128)(2,1)}, f32[4,128]{1,0:T(4,128)}, bf16[3,512,128]{2,1,0:T(8,128)(2,1)S(1)}, f32[128,512]{1,0:T(8,128)S(1)}) custom-call(bf16[3072,128]{1,0:T(8,128)(2,1)S(1)} %bitcast.15, bf16[4,512,128]{2,1,0:T(8,128)(2,1)S(1)} %copy-done.2, f32[144,128]{1,0:T(8,128)S(1)} %copy-done.3, ...), custom_call_target="tpu_custom_call" | custom-call | flops 600000000 | bytes 4000000 | tf_op jit(solution)/shard_map/vertex_last/pallas_call | solution.py:323
  116.4 0.0 collective-permute-done.4.pair_ref
  116.4 6.2 %all-to-all-done.2 = bf16[512,4,128]{2,1,0:T(4,128)(2,1)S(1)} async-done(((bf16[512,4,128]{2,1,0:T(4,128)(2,1)}), bf16[512,4,128]{2,1,0:T(4,128)(2,1)S(1)}, u32[]{:S(2)}, u32[]{:S(2)}) %all-to-all-start.2) | async-done | bytes 524320 | tf_op jit(solution)/shard_map/all_to_all | solution.py:338
  122.6 1.7 %context_last.1 = (bf16[512,128]{1,0:T(8,128)(2,1)}, f32[4,128]{1,0:T(4,128)}) custom-call(bf16[2048,128]{1,0:T(8,128)(2,1)S(1)} %bitcast.16, bf16[3,512,128]{2,1,0:T(8,128)(2,1)S(1)} %get-tuple-element.45.rows_ref, f32[128,512]{1,0:T(8,128)S(1)} %get-tuple-element.46.turned_ref, bf16[128,128]{1,0:T(8,128)(2,1)S(1)} %collective-permute-done.4.pair_ref, ...), custom_call_target="tpu_custom_call" | custom-call | flops 600000000 | bytes 4000000 | tf_op jit(solution)/shard_map/context_last/pallas_call | solution.py:323
  (1 shorter events, 0.0 us)
Async XLA Ops:
  4.8 22.2 %copy-start.4 = (bf16[144,128]{1,0:T(8,128)(2,1)S(1)}, bf16[144,128]{1,0:T(8,128)(2,1)}, u32[]{:S(2)}) copy-start(bf16[144,128]{1,0:T(8,128)(2,1)} %get-tuple-element.29) | copy-start | bytes 110596
  4.9 35.1 %copy-start.5 = (bf16[16,128]{1,0:T(8,128)(2,1)S(1)}, bf16[16,128]{1,0:T(8,128)(2,1)}, u32[]{:S(2)}) copy-start(bf16[16,128]{1,0:T(8,128)(2,1)} %get-tuple-element.30) | copy-start | bytes 12292
  4.9 44.1 %copy-start = (bf16[512,128]{1,0:T(8,128)(2,1)S(1)}, bf16[512,128]{1,0:T(8,128)(2,1)}, u32[]{:S(2)}) copy-start(bf16[512,128]{1,0:T(8,128)(2,1)} %table_ref.4) | copy-start | bytes 393220
  4.9 44.1 %copy-start.3 = (f32[144,128]{1,0:T(8,128)S(1)}, f32[144,128]{1,0:T(8,128)}, u32[]{:S(2)}) copy-start(f32[144,128]{1,0:T(8,128)} %get-tuple-element.31.pairs_ref) | copy-start | bytes 221188
  4.9 44.1 %all-to-all-start = ((bf16[512,4,128]{2,1,0:T(4,128)(2,1)}), bf16[512,4,128]{2,1,0:T(4,128)(2,1)S(1)}, u32[]{:S(2)}, u32[]{:S(2)}) async-start(bf16[512,4,128]{2,1,0:T(4,128)(2,1)} %bitcast.18), calls=%async_computation | async-start | bytes 1048576 | tf_op jit(solution)/shard_map/all_to_all | solution.py:338
  27.1 18.4 %collective-permute-start = (bf16[144,128]{1,0:T(8,128)(2,1)S(1)}, bf16[144,128]{1,0:T(8,128)(2,1)S(1)}, u32[]{:S(2)}, u32[]{:S(2)}) collective-permute-start(bf16[144,128]{1,0:T(8,128)(2,1)S(1)} %copy-done.4), channel_id=1, source_target_pairs={{5,0},{6,1},{7,2},{8,3},{9,4},{10,5},{11,6},{12,7},{13,8},{14,9},{... | collective-permute-start | bytes 110600 | tf_op jit(solution)/shard_map/ppermute | solution.py:342
  40.0 5.5 %collective-permute-start.1 = (bf16[16,128]{1,0:T(8,128)(2,1)S(1)}, bf16[16,128]{1,0:T(8,128)(2,1)S(1)}, u32[]{:S(2)}, u32[]{:S(2)}) collective-permute-start(bf16[16,128]{1,0:T(8,128)(2,1)S(1)} %copy-done.5), channel_id=1, source_target_pairs={{9,0},{10,1},{11,2},{12,3},{13,4},{14,5},{15,6},{16,7},{17,8},{18,... | collective-permute-start | bytes 12296 | tf_op jit(solution)/shard_map/ppermute | solution.py:342
  52.2 36.9 %copy-start.1 = (bf16[512,128]{1,0:T(8,128)(2,1)S(1)}, bf16[512,128]{1,0:T(8,128)(2,1)}, u32[]{:S(2)}) copy-start(bf16[512,128]{1,0:T(8,128)(2,1)} %table_ref.5) | copy-start | bytes 393220
  52.2 36.9 %copy-start.2 = (bf16[4,512,128]{2,1,0:T(8,128)(2,1)S(1)}, bf16[4,512,128]{2,1,0:T(8,128)(2,1)}, u32[]{:S(2)}) copy-start(bf16[4,512,128]{2,1,0:T(8,128)(2,1)} %get-tuple-element.36.sent_ref) | copy-start | bytes 1572868
  52.2 36.8 %all-to-all-start.1 = ((bf16[512,3,2,128]{3,2,1,0:T(2,128)(2,1)}), bf16[512,3,2,128]{3,2,1,0:T(2,128)(2,1)S(1)}, u32[]{:S(2)}, u32[]{:S(2)}) async-start(bf16[512,3,2,128]{3,2,1,0:T(2,128)(2,1)} %bitcast.8), calls=%async_computation.1 | async-start | bytes 1572864 | tf_op jit(solution)/shard_map/all_to_all | solution.py:338
  61.4 24.8 %collective-permute-start.2 = (bf16[128,128]{1,0:T(8,128)(2,1)S(1)}, bf16[128,128]{1,0:T(8,128)(2,1)S(1)}, u32[]{:S(2)}, u32[]{:S(2)}) collective-permute-start(bf16[128,128]{1,0:T(8,128)(2,1)S(1)} %get-tuple-element.33), channel_id=1, source_target_pairs={{507,0},{508,1},{509,2},{510,3},{511,4},{0,5},{1,6},{2,7},{3,8},{4... | collective-permute-start | bytes 98312 | tf_op jit(solution)/shard_map/ppermute | solution.py:342
  66.4 21.8 %collective-permute-start.3 = (bf16[128,128]{1,0:T(8,128)(2,1)S(1)}, bf16[128,128]{1,0:T(8,128)(2,1)S(1)}, u32[]{:S(2)}, u32[]{:S(2)}) collective-permute-start(bf16[128,128]{1,0:T(8,128)(2,1)S(1)} %get-tuple-element.34.mine_ref), channel_id=1, source_target_pairs={{503,0},{504,1},{505,2},{506,3},{507,4},{508,5},{509,6},{510,7},{5... | collective-permute-start | bytes 98312 | tf_op jit(solution)/shard_map/ppermute | solution.py:342
  91.8 30.8 %all-to-all-start.2 = ((bf16[512,4,128]{2,1,0:T(4,128)(2,1)}), bf16[512,4,128]{2,1,0:T(4,128)(2,1)S(1)}, u32[]{:S(2)}, u32[]{:S(2)}) async-start(bf16[512,4,128]{2,1,0:T(4,128)(2,1)} %bitcast.10), calls=%async_computation.2 | async-start | bytes 1048576 | tf_op jit(solution)/shard_map/all_to_all | solution.py:338
  100.6 15.9 %collective-permute-start.4 = (bf16[128,128]{1,0:T(8,128)(2,1)S(1)}, bf16[128,128]{1,0:T(8,128)(2,1)S(1)}, u32[]{:S(2)}, u32[]{:S(2)}) collective-permute-start(bf16[128,128]{1,0:T(8,128)(2,1)S(1)} %get-tuple-element.47), channel_id=1, source_target_pairs={{9,0},{10,1},{11,2},{12,3},{13,4},{14,5},{15,6},{16,7},{17,8},{18,... | collective-permute-start | bytes 98312 | tf_op jit(solution)/shard_map/ppermute | solution.py:342

commit v7 on v6

--- a/solution.py
+++ b/solution.py
@@ -114,6 +114,18 @@
         for s in range(CAP):
             here = here_ref[first_here + s, pl.ds(at, BLOCK), :].astype(F32)
             there = there_ref[first_there + s, pl.ds(at, BLOCK), :].astype(F32)
+            out_ref[s, pl.ds(at, BLOCK), :] = (jax.nn.sigmoid(row_dot(here, there)) * there).astype(BF16)
+
+    blocks(out_ref.shape[1], BLOCK, step)
+
+
+def weigh_flat(here_ref, first_here, flat_ref, wide_ref, group, out_ref):
+    wide_ref[...] = flat_ref[...].astype(F32)
+
+    def step(at, b):
+        for s in range(CAP):
+            here = here_ref[first_here + s, pl.ds(at, BLOCK), :].astype(F32)
+            there = wide_ref[pl.ds(at * group + s, BLOCK, stride=group), :]
             out_ref[s, pl.ds(at, BLOCK), :] = (jax.nn.sigmoid(row_dot(here, there)) * there).astype(BF16)
 
     blocks(out_ref.shape[1], BLOCK, step)
@@ -276,12 +288,11 @@
 
 def vertex_first(
     flat_ref, sent_ref, pairs_ref, partner_ref, table_ref,
-    send_ref, pair_ref, new_ref, new_state_ref, turned_ref, rows_ref, got_ref, terms_ref, wide_ref, got_wide_ref,
+    send_ref, pair_ref, new_ref, new_state_ref, turned_ref, rows_ref, terms_ref, wide_ref, got_wide_ref,
 ):
     state_ref = pairs_ref.at[LANES : LANES + 8]
-    by_slot(flat_ref, got_ref, got_wide_ref, 0, CAP, 2 * CAP)
     turn(sent_ref.at[CAP], turned_ref)
-    weigh_slots(sent_ref, 0, got_ref, 0, terms_ref)
+    weigh_flat(sent_ref, 0, flat_ref, got_wide_ref, 2 * CAP, terms_ref)
     row, pair_terms = vertex_side(pairs_ref, 0, table_ref, partner_ref)
     grad_of = scattered(turned_ref, terms_ref, lane_of(0, 0, 2))
     adagrad(table_ref, state_ref, new_ref, new_state_ref, grad_of, row, pair_terms)
@@ -309,10 +320,9 @@
 
 def context_last(
     flat_ref, rows_ref, turned_ref, pair_ref, numbers_ref, mine_ref, table_ref, state_ref,
-    new_ref, new_state_ref, got_ref, terms_ref, got_wide_ref,
-):
-    by_slot(flat_ref, got_ref, got_wide_ref, 0, CAP, CAP + 1)
-    weigh_slots(rows_ref, 0, got_ref, 0, terms_ref)
+    new_ref, new_state_ref, terms_ref, got_wide_ref,
+):
+    weigh_flat(rows_ref, 0, flat_ref, got_wide_ref, CAP + 1, terms_ref)
     row = row_numbers(numbers_ref[...])
     pair_terms = pair_terms_of(mine_ref[...].astype(F32), pair_ref[...].astype(F32))
     grad_of = scattered(turned_ref, terms_ref, lane_of(1, 0, 0))
@@ -395,7 +405,7 @@
     got_b, theirs_0, theirs_1 = lax.optimization_barrier((got_b, theirs_0, theirs_1))
     flat_c, pair_c, vertex_1, v_state_1 = call(
         vertex_first, "vertex_first", [flat(CAP + 1), pair_rows, table, state],
-        [turned, terms, terms, terms, wide(CAP + 1), wide(2 * CAP)],
+        [turned, terms, terms, wide(CAP + 1), wide(2 * CAP)],
         got_b, rows_a, pairs, theirs_0, vertex_table,
     )
     got_pair_c = passed_along(pair_c, n - shifts[1], n)
@@ -406,7 +416,7 @@
         got_b, rows_a, pairs, theirs_1, vertex_1, v_state_1, slots_b, context_1,
     )
     context_2, c_state_2 = call(
-        context_last, "context_last", [table, state], [terms, terms, wide(CAP + 1)],
+        context_last, "context_last", [table, state], [terms, wide(CAP + 1)],
         got_c, rows_b, turned_b, got_pair_c, got_numbers, pair_b1, context_1, c_state_1,
     )
     return vertex_2, context_2, v_state_2.reshape(rows), c_state_2.reshape(rows)

time: 125 us -> 125 us (level)
  no operation moved by 1% of the time
where the time goes in v7:
time: 125 us; the launch traced here: 124 us
  starting transfers between devices  78.9 us (63%)
  waiting for transfers between devices  30.1 us (24%)
  Pallas kernels  14.5 us (12%)
    all_to_all x3, starting transfers between devices, exchange(): lax.all_to_all(split, AXES, split_axis=0, concat_axis=0, tiled=True)  40.2 us
    ppermute x5, starting transfers between devices, passed_along(): lax.ppermute(block, AXES, [((i - distance) % n_devices, i) for i in range...  38.7 us
    ppermute x5, waiting for transfers between devices, passed_along(): lax.ppermute(block, AXES, [((i - distance) % n_devices, i) for i in range...  19.6 us
    pallas_call x5, Pallas kernels, call(): pl.pallas_call(kernel, name=name, out_shape=[jax.ShapeDtypeStruct(s, d) f...  14.5 us
    all_to_all x3, waiting for transfers between devices, exchange(): lax.all_to_all(split, AXES, split_axis=0, concat_axis=0, tiled=True)  10.5 us
  transfers between devices with their start and end apart: 8, of which 6 were waited for; matrix products, arithmetic and copies ran while one was open for 0% of the time, Pallas kernels for 2%

profile of v7, /device:TPU:1, one launch (start us, length us, event | category | flops | bytes accessed | tf_op | source)
XLA Modules:
  0.0 124.3 jit_solution(12532354396447014538)
XLA Ops:
  0.6 4.2 %slots.1 = (bf16[2048,128]{1,0:T(8,128)(2,1)}, bf16[4,512,128]{2,1,0:T(8,128)(2,1)}, bf16[144,128]{1,0:T(8,128)(2,1)}, f32[144,128]{1,0:T(8,128)}, bf16[16,128]{1,0:T(8,128)(2,1)}) custom-call(s32[2,5,8,16]{3,2,1,0:T(8,128)} %bitcast.19, s32[2,5,8,16]{3,2,1,0:T(8,128)} %bitcast.20, s32[2,2,8]{2,1,0:T(2,128)} %bitcast.22, s32[2,8,2,16]{3,2,1,0:T(2,128)} %bitcast.21, ...), custom_call_target="tpu_custom_call" | custom-call | flops 600000000 | bytes 4000000 | tf_op jit(solution)/shard_map/slots/pallas_call | solution.py:333
  4.8 0.0 copy-start.4
  4.9 0.0 copy-start
  4.9 0.0 copy-start.3
  4.9 22.2 %all-to-all-start = ((bf16[512,4,128]{2,1,0:T(4,128)(2,1)}), bf16[512,4,128]{2,1,0:T(4,128)(2,1)S(1)}, u32[]{:S(2)}, u32[]{:S(2)}) async-start(bf16[512,4,128]{2,1,0:T(4,128)(2,1)} %bitcast.18), calls=%async_computation | async-start | bytes 1048576 | tf_op jit(solution)/shard_map/all_to_all | solution.py:348
  27.1 0.0 copy-done.4
  27.1 12.9 %collective-permute-start = (bf16[144,128]{1,0:T(8,128)(2,1)S(1)}, bf16[144,128]{1,0:T(8,128)(2,1)S(1)}, u32[]{:S(2)}, u32[]{:S(2)}) collective-permute-start(bf16[144,128]{1,0:T(8,128)(2,1)S(1)} %copy-done.4), channel_id=1, source_target_pairs={{5,0},{6,1},{7,2},{8,3},{9,4},{10,5},{11,6},{12,7},{13,8},{14,9},{... | collective-permute-start | bytes 110600 | tf_op jit(solution)/shard_map/ppermute | solution.py:352
  39.9 0.0 copy-done.5
  40.0 3.1 %collective-permute-start.1 = (bf16[16,128]{1,0:T(8,128)(2,1)S(1)}, bf16[16,128]{1,0:T(8,128)(2,1)S(1)}, u32[]{:S(2)}, u32[]{:S(2)}) collective-permute-start(bf16[16,128]{1,0:T(8,128)(2,1)S(1)} %copy-done.5), channel_id=1, source_target_pairs={{9,0},{10,1},{11,2},{12,3},{13,4},{14,5},{15,6},{16,7},{17,8},{18,... | collective-permute-start | bytes 12296 | tf_op jit(solution)/shard_map/ppermute | solution.py:352
  43.1 2.4 %collective-permute-done.1.numbers_ref = bf16[16,128]{1,0:T(8,128)(2,1)S(1)} collective-permute-done((bf16[16,128]{1,0:T(8,128)(2,1)S(1)}, bf16[16,128]{1,0:T(8,128)(2,1)S(1)}, u32[]{:S(2)}, u32[]{:S(2)}) %collective-permute-start.1) | collective-permute-done | bytes 4128 | tf_op jit(solution)/shard_map/ppermute | solution.py:352
  45.5 0.0 collective-permute-done.pair_ref
  45.5 3.5 %all-to-all-done = bf16[512,4,128]{2,1,0:T(4,128)(2,1)S(1)} async-done(((bf16[512,4,128]{2,1,0:T(4,128)(2,1)}), bf16[512,4,128]{2,1,0:T(4,128)(2,1)S(1)}, u32[]{:S(2)}, u32[]{:S(2)}) %all-to-all-start) | async-done | bytes 524320 | tf_op jit(solution)/shard_map/all_to_all | solution.py:348
  49.0 0.0 copy-done
  49.0 0.0 copy-done.3
  49.0 3.2 %context_first.1 = (bf16[3072,128]{1,0:T(8,128)(2,1)}, bf16[512,128]{1,0:T(8,128)(2,1)S(1)}, bf16[512,128]{1,0:T(8,128)(2,1)S(1)}, f32[4,128]{1,0:T(4,128)S(1)},...) custom-call(bf16[2048,128]{1,0:T(8,128)(2,1)S(1)} %bitcast.17, ...), custom_call_target="tpu_custom_call" | custom-call | flops 600000000 | bytes 4000000 | tf_op jit(solution)/shard_map/context_first/pallas_call | solution.py:333
  52.2 0.0 copy-start.1
  52.2 0.0 copy-start.2
  52.2 9.2 %all-to-all-start.1 = ((bf16[512,3,2,128]{3,2,1,0:T(2,128)(2,1)}), bf16[512,3,2,128]{3,2,1,0:T(2,128)(2,1)S(1)}, u32[]{:S(2)}, u32[]{:S(2)}) async-start(bf16[512,3,2,128]{3,2,1,0:T(2,128)(2,1)} %bitcast.8), calls=%async_computation.1 | async-start | bytes 1572864 | tf_op jit(solution)/shard_map/all_to_all | solution.py:348
  61.4 5.0 %collective-permute-start.2 = (bf16[128,128]{1,0:T(8,128)(2,1)S(1)}, bf16[128,128]{1,0:T(8,128)(2,1)S(1)}, u32[]{:S(2)}, u32[]{:S(2)}) collective-permute-start(bf16[128,128]{1,0:T(8,128)(2,1)S(1)} %get-tuple-element.33), channel_id=1, source_target_pairs={{507,0},{508,1},{509,2},{510,3},{511,4},{0,5},{1,6},{2,7},{3,8},{4... | collective-permute-start | bytes 98312 | tf_op jit(solution)/shard_map/ppermute | solution.py:352
  66.4 4.5 %collective-permute-start.3 = (bf16[128,128]{1,0:T(8,128)(2,1)S(1)}, bf16[128,128]{1,0:T(8,128)(2,1)S(1)}, u32[]{:S(2)}, u32[]{:S(2)}) collective-permute-start(bf16[128,128]{1,0:T(8,128)(2,1)S(1)} %get-tuple-element.34.mine_ref), channel_id=1, source_target_pairs={{503,0},{504,1},{505,2},{506,3},{507,4},{508,5},{509,6},{510,7},{5... | collective-permute-start | bytes 98312 | tf_op jit(solution)/shard_map/ppermute | solution.py:352
  71.0 15.2 %collective-permute-done.2.partner_ref = bf16[128,128]{1,0:T(8,128)(2,1)S(1)} collective-permute-done((bf16[128,128]{1,0:T(8,128)(2,1)S(1)}, bf16[128,128]{1,0:T(8,128)(2,1)S(1)}, u32[]{:S(2)}, u32[]{:S(2)}) %collective-permute-start.2) | collective-permute-done | bytes 32800 | tf_op jit(solution)/shard_map/ppermute | solution.py:352
  86.2 2.0 %collective-permute-done.3.partner_ref = bf16[128,128]{1,0:T(8,128)(2,1)S(1)} collective-permute-done((bf16[128,128]{1,0:T(8,128)(2,1)S(1)}, bf16[128,128]{1,0:T(8,128)(2,1)S(1)}, u32[]{:S(2)}, u32[]{:S(2)}) %collective-permute-start.3) | collective-permute-done | bytes 32800 | tf_op jit(solution)/shard_map/ppermute | solution.py:352
  88.2 0.8 all-to-all-done.1
  89.0 0.0 copy-done.1
  89.0 0.0 copy-done.2
  89.0 2.7 %vertex_first.1 = (bf16[2048,128]{1,0:T(8,128)(2,1)}, bf16[128,128]{1,0:T(8,128)(2,1)S(1)}, bf16[512,128]{1,0:T(8,128)(2,1)S(1)}, f32[4,128]{1,0:T(4,128)S(1)}) custom-call(bf16[3072,128]{1,0:T(8,128)(2,1)S(1)} %bitcast.14, bf16[4,512,128]{2,1,0:T(8,128)(2,1)S(1)} %copy-done.2, f32[144,128]{1,0:T(8,128)S(1)} %copy-done.3, ...), custom_call_target="tpu_custom_call" | custom-call | flops 600000000 | bytes 4000000 | tf_op jit(solution)/shard_map/vertex_first/pallas_call | solution.py:333
  91.8 8.8 %all-to-all-start.2 = ((bf16[512,4,128]{2,1,0:T(4,128)(2,1)}), bf16[512,4,128]{2,1,0:T(4,128)(2,1)S(1)}, u32[]{:S(2)}, u32[]{:S(2)}) async-start(bf16[512,4,128]{2,1,0:T(4,128)(2,1)} %bitcast.10), calls=%async_computation.2 | async-start | bytes 1048576 | tf_op jit(solution)/shard_map/all_to_all | solution.py:348
  100.6 13.2 %collective-permute-start.4 = (bf16[128,128]{1,0:T(8,128)(2,1)S(1)}, bf16[128,128]{1,0:T(8,128)(2,1)S(1)}, u32[]{:S(2)}, u32[]{:S(2)}) collective-permute-start(bf16[128,128]{1,0:T(8,128)(2,1)S(1)} %get-tuple-element.47), channel_id=1, source_target_pairs={{9,0},{10,1},{11,2},{12,3},{13,4},{14,5},{15,6},{16,7},{17,8},{18,... | collective-permute-start | bytes 98312 | tf_op jit(solution)/shard_map/ppermute | solution.py:352
  113.8 2.6 %vertex_last.1 = (bf16[512,128]{1,0:T(8,128)(2,1)}, f32[4,128]{1,0:T(4,128)}, bf16[3,512,128]{2,1,0:T(8,128)(2,1)S(1)}, f32[128,512]{1,0:T(8,128)S(1)}) custom-call(bf16[3072,128]{1,0:T(8,128)(2,1)S(1)} %bitcast.15, bf16[4,512,128]{2,1,0:T(8,128)(2,1)S(1)} %copy-done.2, f32[144,128]{1,0:T(8,128)S(1)} %copy-done.3, ...), custom_call_target="tpu_custom_call" | custom-call | flops 600000000 | bytes 4000000 | tf_op jit(solution)/shard_map/vertex_last/pallas_call | solution.py:333
  116.4 0.0 collective-permute-done.4.pair_ref
  116.4 6.2 %all-to-all-done.2 = bf16[512,4,128]{2,1,0:T(4,128)(2,1)S(1)} async-done(((bf16[512,4,128]{2,1,0:T(4,128)(2,1)}), bf16[512,4,128]{2,1,0:T(4,128)(2,1)S(1)}, u32[]{:S(2)}, u32[]{:S(2)}) %all-to-all-start.2) | async-done | bytes 524320 | tf_op jit(solution)/shard_map/all_to_all | solution.py:348
  122.6 1.7 %context_last.1 = (bf16[512,128]{1,0:T(8,128)(2,1)}, f32[4,128]{1,0:T(4,128)}) custom-call(bf16[2048,128]{1,0:T(8,128)(2,1)S(1)} %bitcast.16, bf16[3,512,128]{2,1,0:T(8,128)(2,1)S(1)} %get-tuple-element.45.rows_ref, f32[128,512]{1,0:T(8,128)S(1)} %get-tuple-element.46.turned_ref, bf16[128,128]{1,0:T(8,128)(2,1)S(1)} %collective-permute-done.4.pair_ref, ...), custom_call_target="tpu_custom_call" | custom-call | flops 600000000 | bytes 4000000 | tf_op jit(solution)/shard_map/context_last/pallas_call | solution.py:333
  (1 shorter events, 0.0 us)
Async XLA Ops:
  4.8 22.2 %copy-start.4 = (bf16[144,128]{1,0:T(8,128)(2,1)S(1)}, bf16[144,128]{1,0:T(8,128)(2,1)}, u32[]{:S(2)}) copy-start(bf16[144,128]{1,0:T(8,128)(2,1)} %get-tuple-element.29) | copy-start | bytes 110596
  4.9 35.1 %copy-start.5 = (bf16[16,128]{1,0:T(8,128)(2,1)S(1)}, bf16[16,128]{1,0:T(8,128)(2,1)}, u32[]{:S(2)}) copy-start(bf16[16,128]{1,0:T(8,128)(2,1)} %get-tuple-element.30) | copy-start | bytes 12292
  4.9 44.1 %copy-start = (bf16[512,128]{1,0:T(8,128)(2,1)S(1)}, bf16[512,128]{1,0:T(8,128)(2,1)}, u32[]{:S(2)}) copy-start(bf16[512,128]{1,0:T(8,128)(2,1)} %table_ref.4) | copy-start | bytes 393220
  4.9 44.1 %copy-start.3 = (f32[144,128]{1,0:T(8,128)S(1)}, f32[144,128]{1,0:T(8,128)}, u32[]{:S(2)}) copy-start(f32[144,128]{1,0:T(8,128)} %get-tuple-element.31.pairs_ref) | copy-start | bytes 221188
  4.9 44.1 %all-to-all-start = ((bf16[512,4,128]{2,1,0:T(4,128)(2,1)}), bf16[512,4,128]{2,1,0:T(4,128)(2,1)S(1)}, u32[]{:S(2)}, u32[]{:S(2)}) async-start(bf16[512,4,128]{2,1,0:T(4,128)(2,1)} %bitcast.18), calls=%async_computation | async-start | bytes 1048576 | tf_op jit(solution)/shard_map/all_to_all | solution.py:348
  27.1 18.4 %collective-permute-start = (bf16[144,128]{1,0:T(8,128)(2,1)S(1)}, bf16[144,128]{1,0:T(8,128)(2,1)S(1)}, u32[]{:S(2)}, u32[]{:S(2)}) collective-permute-start(bf16[144,128]{1,0:T(8,128)(2,1)S(1)} %copy-done.4), channel_id=1, source_target_pairs={{5,0},{6,1},{7,2},{8,3},{9,4},{10,5},{11,6},{12,7},{13,8},{14,9},{... | collective-permute-start | bytes 110600 | tf_op jit(solution)/shard_map/ppermute | solution.py:352
  40.0 5.5 %collective-permute-start.1 = (bf16[16,128]{1,0:T(8,128)(2,1)S(1)}, bf16[16,128]{1,0:T(8,128)(2,1)S(1)}, u32[]{:S(2)}, u32[]{:S(2)}) collective-permute-start(bf16[16,128]{1,0:T(8,128)(2,1)S(1)} %copy-done.5), channel_id=1, source_target_pairs={{9,0},{10,1},{11,2},{12,3},{13,4},{14,5},{15,6},{16,7},{17,8},{18,... | collective-permute-start | bytes 12296 | tf_op jit(solution)/shard_map/ppermute | solution.py:352
  52.2 36.9 %copy-start.1 = (bf16[512,128]{1,0:T(8,128)(2,1)S(1)}, bf16[512,128]{1,0:T(8,128)(2,1)}, u32[]{:S(2)}) copy-start(bf16[512,128]{1,0:T(8,128)(2,1)} %table_ref.5) | copy-start | bytes 393220
  52.2 36.9 %copy-start.2 = (bf16[4,512,128]{2,1,0:T(8,128)(2,1)S(1)}, bf16[4,512,128]{2,1,0:T(8,128)(2,1)}, u32[]{:S(2)}) copy-start(bf16[4,512,128]{2,1,0:T(8,128)(2,1)} %get-tuple-element.36.sent_ref) | copy-start | bytes 1572868
  52.2 36.8 %all-to-all-start.1 = ((bf16[512,3,2,128]{3,2,1,0:T(2,128)(2,1)}), bf16[512,3,2,128]{3,2,1,0:T(2,128)(2,1)S(1)}, u32[]{:S(2)}, u32[]{:S(2)}) async-start(bf16[512,3,2,128]{3,2,1,0:T(2,128)(2,1)} %bitcast.8), calls=%async_computation.1 | async-start | bytes 1572864 | tf_op jit(solution)/shard_map/all_to_all | solution.py:348
  61.4 24.8 %collective-permute-start.2 = (bf16[128,128]{1,0:T(8,128)(2,1)S(1)}, bf16[128,128]{1,0:T(8,128)(2,1)S(1)}, u32[]{:S(2)}, u32[]{:S(2)}) collective-permute-start(bf16[128,128]{1,0:T(8,128)(2,1)S(1)} %get-tuple-element.33), channel_id=1, source_target_pairs={{507,0},{508,1},{509,2},{510,3},{511,4},{0,5},{1,6},{2,7},{3,8},{4... | collective-permute-start | bytes 98312 | tf_op jit(solution)/shard_map/ppermute | solution.py:352
  66.4 21.8 %collective-permute-start.3 = (bf16[128,128]{1,0:T(8,128)(2,1)S(1)}, bf16[128,128]{1,0:T(8,128)(2,1)S(1)}, u32[]{:S(2)}, u32[]{:S(2)}) collective-permute-start(bf16[128,128]{1,0:T(8,128)(2,1)S(1)} %get-tuple-element.34.mine_ref), channel_id=1, source_target_pairs={{503,0},{504,1},{505,2},{506,3},{507,4},{508,5},{509,6},{510,7},{5... | collective-permute-start | bytes 98312 | tf_op jit(solution)/shard_map/ppermute | solution.py:352
  91.8 30.8 %all-to-all-start.2 = ((bf16[512,4,128]{2,1,0:T(4,128)(2,1)}), bf16[512,4,128]{2,1,0:T(4,128)(2,1)S(1)}, u32[]{:S(2)}, u32[]{:S(2)}) async-start(bf16[512,4,128]{2,1,0:T(4,128)(2,1)} %bitcast.10), calls=%async_computation.2 | async-start | bytes 1048576 | tf_op jit(solution)/shard_map/all_to_all | solution.py:348
  100.6 15.8 %collective-permute-start.4 = (bf16[128,128]{1,0:T(8,128)(2,1)S(1)}, bf16[128,128]{1,0:T(8,128)(2,1)S(1)}, u32[]{:S(2)}, u32[]{:S(2)}) collective-permute-start(bf16[128,128]{1,0:T(8,128)(2,1)S(1)} %get-tuple-element.47), channel_id=1, source_target_pairs={{9,0},{10,1},{11,2},{12,3},{13,4},{14,5},{15,6},{16,7},{17,8},{18,... | collective-permute-start | bytes 98312 | tf_op jit(solution)/shard_map/ppermute | solution.py:352
